TPU v7x, 512 devices: a whole 4x8x8 slice. The times are simulated.
512 devices in a mesh: seq: 64 (over x, y_lo, z), aud: 8 (over y_hi, core).
Axes of the slice: x: 4, y: 8 (y_hi: 4, y_lo: 2; y = y_hi * 2 + y_lo), z: 8, core: 2. Of those that a mesh axis runs over, the one named last changes fastest.
Arguments:
- video_query: bfloat16 [8192, 2048], P('seq', 'aud'), may hold values from -9 to 9
- video_key: bfloat16 [8192, 2048], P('seq', 'aud'), may hold values from -9 to 9
- video_value: bfloat16 [8192, 2048], P('seq', 'aud'), may hold values from -6 to 6
- audio_query: bfloat16 [512, 2048], P('aud'), may hold values from -9 to 9
- audio_key: bfloat16 [512, 2048], P('aud'), may hold values from -9 to 9
- audio_value: bfloat16 [512, 2048], P('aud'), may hold values from -6 to 6
- video_grad: bfloat16 [8192, 2048], P('seq', 'aud'), may hold values from -6 to 6
- audio_grad: bfloat16 [512, 2048], P('aud'), may hold values from -6 to 6
- block_list: int32 [64, 3], P('seq'), may hold values from 0 to 3, as said below
- block_count: int32 [64], P('seq'), may hold values from 1 to 3, as said below
Outputs:
- video_out: bfloat16 [8192, 2048], P('seq', 'aud')
- audio_out: bfloat16 [512, 2048], P('aud')
- grad_audio_query: bfloat16 [512, 2048], P('aud')
- grad_audio_key: bfloat16 [512, 2048], P('aud')
- grad_audio_value: bfloat16 [512, 2048], P('aud')
Inputs may be any that keep to these rules, and one draw needn't show every extreme that they name: `block_list`: row b lists in rising order the audio blocks of 128 tokens that intersect video block b in time or lie next to that span; only the first block_count[b] entries count and the others repeat the first; every audio block is listed by some row. `block_count`: some row counts 3 entries.
All inputs are finite; a program needn't handle non-finite values.
Results may differ from a plain program's by a relative error of at most 0.01325.
The roundings to bfloat16 on the way count: a program that leaves them out, or rounds other values in their place, can miss the bound.
Values may be sent and summed in bfloat16 or wider, within the bound.
No kernel may reach another device: no remote copies, remote signals or barrier semaphores. Data moves between devices by JAX's collectives and lax.ppermute only.
A program may use at most 192 MiB of HBM per device.

v0:
```python
import math

import jax
import jax.numpy as jnp
from jax import lax
from jax.sharding import PartitionSpec as P

HEAD_DIM = 128
BLOCK = 128


def combined_all(value, axis, join):
    pieces = jax.tree.map(lambda part: lax.all_gather(part, axis), value)
    head = jax.tree.map(lambda part: part[0], pieces)
    tail = jax.tree.map(lambda part: part[1:], pieces)
    running, _ = lax.scan(lambda running, slab: (join(running, slab), None), head, tail)
    return running


def heads_first(matrix):
    return jnp.transpose(
        matrix.reshape(matrix.shape[0], matrix.shape[1] // HEAD_DIM, HEAD_DIM), (1, 0, 2)
    )


def join_heads(tensor):
    return jnp.transpose(tensor, (1, 0, 2)).reshape(
        tensor.shape[1], tensor.shape[0] * tensor.shape[2]
    )


def combine_partial(earlier, later):
    joint = jnp.maximum(earlier[0], later[0])
    factor_early = jnp.exp(earlier[0] - joint)
    factor_late = jnp.exp(later[0] - joint)
    row_total = earlier[1] * factor_early + later[1] * factor_late
    weighted = earlier[2] * factor_early[:, :, None] + later[2] * factor_late[:, :, None]
    return (joint, row_total, weighted)


def reorder_rows(matrix, audio_count, seq_count):
    return jnp.transpose(
        matrix.reshape(audio_count, seq_count, -1, matrix.shape[1]), (1, 0, 2, 3)
    ).reshape(matrix.shape)


def local(
    video_query,
    video_key,
    video_value,
    audio_query,
    audio_key,
    audio_value,
    video_grad,
    audio_grad,
    block_list,
    block_count,
):
    seq_count = lax.axis_size("seq")
    audio_count = lax.axis_size("aud")
    video_rows = video_query.shape[0]
    head_count = video_query.shape[1] // HEAD_DIM
    score_scale = 1.0 / math.sqrt(HEAD_DIM)
    video_heads = heads_first(video_query)
    key_local = heads_first(video_key)
    value_local = heads_first(video_value)
    audio_parts = (
        lax.all_to_all(audio_query, "aud", split_axis=1, concat_axis=0, tiled=True),
        lax.all_to_all(audio_key, "aud", split_axis=1, concat_axis=0, tiled=True),
        lax.all_to_all(audio_value, "aud", split_axis=1, concat_axis=0, tiled=True),
        lax.all_to_all(audio_grad, "aud", split_axis=1, concat_axis=0, tiled=True),
    )
    audio_tokens = audio_parts[0].shape[0]
    aud_queries = heads_first(audio_parts[0])
    aud_keys = heads_first(audio_parts[1])
    aud_values = heads_first(audio_parts[2])
    aud_upstream = heads_first(audio_parts[3])
    start_state = (
        jnp.full((head_count, video_rows), -jnp.inf, jnp.float32),
        jnp.zeros((head_count, video_rows), jnp.float32),
        jnp.zeros((head_count, video_rows, HEAD_DIM), jnp.float32),
    )
    scores = (
        jnp.einsum(
            "hqd,hkd->hqk",
            video_heads,
            lax.all_gather(key_local, "seq", axis=1, tiled=True),
            preferred_element_type=jnp.float32,
        )
        * score_scale
    )
    new_best = jnp.max(scores, axis=2)
    factor = jnp.exp(start_state[0] - new_best)
    weights = jnp.exp(scores - new_best[:, :, None])
    row_total = start_state[1] * factor + jnp.sum(weights, axis=2)
    weighted = start_state[2] * factor[:, :, None] + jnp.einsum(
        "hqk,hkd->hqd",
        weights.astype(jnp.bfloat16),
        lax.all_gather(value_local, "seq", axis=1, tiled=True),
        preferred_element_type=jnp.float32,
    )
    self_out = weighted / row_total[:, :, None]
    slot_ids = jnp.arange(block_list.shape[1])
    live_slots = slot_ids[None, :] < block_count[:, None]
    block_ids = jnp.arange(audio_tokens // BLOCK)
    block_pairs = jnp.any(
        live_slots[:, :, None] & (block_list[:, :, None] == block_ids[None, None, :]), axis=1
    )
    token_pairs = jnp.repeat(jnp.repeat(block_pairs, BLOCK, axis=0), BLOCK, axis=1)
    back_pairs = token_pairs.T
    cross_scores = (
        jnp.einsum("hqd,hkd->hqk", video_heads, aud_keys, preferred_element_type=jnp.float32)
        * score_scale
    )
    cross_best = jnp.max(jnp.where(token_pairs[None], cross_scores, -jnp.inf), axis=2)
    cross_weights = jnp.where(
        token_pairs[None], jnp.exp(cross_scores - cross_best[:, :, None]), 0.0
    )
    cross_total = jnp.sum(cross_weights, axis=2)
    cross_out = (
        jnp.einsum(
            "hqk,hkd->hqd",
            cross_weights.astype(jnp.bfloat16),
            aud_values,
            preferred_element_type=jnp.float32,
        )
        / cross_total[:, :, None]
    )
    video_out = join_heads(self_out + cross_out).astype(jnp.bfloat16)
    video_upstream = heads_first(video_grad)
    cross_probs = cross_weights / cross_total[:, :, None]
    cross_dprobs = jnp.einsum(
        "hqd,hkd->hqk", video_upstream, aud_values, preferred_element_type=jnp.float32
    )
    cross_delta = jnp.einsum("hqd,hqd->hq", video_upstream.astype(jnp.float32), cross_out)
    cross_dscores = cross_probs * (cross_dprobs - cross_delta[:, :, None])
    value_terms = jnp.einsum(
        "hqk,hqd->hkd",
        cross_probs.astype(jnp.bfloat16),
        video_upstream,
        preferred_element_type=jnp.float32,
    )
    key_terms = (
        jnp.einsum(
            "hqk,hqd->hkd",
            cross_dscores.astype(jnp.bfloat16),
            video_heads,
            preferred_element_type=jnp.float32,
        )
        * score_scale
    )
    back_scores = (
        jnp.einsum("hqd,hkd->hqk", aud_queries, key_local, preferred_element_type=jnp.float32)
        * score_scale
    )
    local_best = jnp.max(jnp.where(back_pairs[None], back_scores, -1e30), axis=2)
    local_weights = jnp.where(back_pairs[None], jnp.exp(back_scores - local_best[:, :, None]), 0.0)
    local_total = jnp.sum(local_weights, axis=2)
    local_weighted = jnp.einsum(
        "hqk,hkd->hqd",
        local_weights.astype(jnp.bfloat16),
        value_local,
        preferred_element_type=jnp.float32,
    )
    back_best, back_total, back_weighted = combined_all(
        (local_best, local_total, local_weighted), "seq", combine_partial
    )
    audio_attn = back_weighted / back_total[:, :, None]
    back_probs = (
        jnp.where(back_pairs[None], jnp.exp(back_scores - back_best[:, :, None]), 0.0)
        / back_total[:, :, None]
    )
    back_dprobs = jnp.einsum(
        "hqd,hkd->hqk", aud_upstream, value_local, preferred_element_type=jnp.float32
    )
    back_delta = jnp.einsum("hqd,hqd->hq", aud_upstream.astype(jnp.float32), audio_attn)
    back_dscores = back_probs * (back_dprobs - back_delta[:, :, None])
    query_terms = (
        jnp.einsum(
            "hqk,hkd->hqd",
            back_dscores.astype(jnp.bfloat16),
            key_local,
            preferred_element_type=jnp.float32,
        )
        * score_scale
    )
    flat_query = join_heads(query_terms)
    flat_key = join_heads(key_terms)
    flat_value = join_heads(value_terms)
    audio_flat = join_heads(audio_attn)
    summed = (
        lax.psum_scatter(
            reorder_rows(flat_query, audio_count, seq_count), "seq", scatter_dimension=0, tiled=True
        ),
        lax.psum_scatter(
            reorder_rows(flat_key, audio_count, seq_count), "seq", scatter_dimension=0, tiled=True
        ),
        lax.psum_scatter(
            reorder_rows(flat_value, audio_count, seq_count), "seq", scatter_dimension=0, tiled=True
        ),
    )
    share_rows = audio_tokens // seq_count
    out_share = lax.dynamic_slice_in_dim(
        reorder_rows(audio_flat, audio_count, seq_count),
        lax.axis_index("seq") * share_rows,
        share_rows,
        0,
    )
    moved = (
        lax.all_to_all(
            out_share.astype(jnp.bfloat16), "aud", split_axis=0, concat_axis=1, tiled=True
        ),
        lax.all_to_all(
            summed[0].astype(jnp.bfloat16), "aud", split_axis=0, concat_axis=1, tiled=True
        ),
        lax.all_to_all(
            summed[1].astype(jnp.bfloat16), "aud", split_axis=0, concat_axis=1, tiled=True
        ),
        lax.all_to_all(
            summed[2].astype(jnp.bfloat16), "aud", split_axis=0, concat_axis=1, tiled=True
        ),
    )
    finished = (
        lax.all_gather(moved[0], "seq", axis=0, tiled=True),
        lax.all_gather(moved[1], "seq", axis=0, tiled=True),
        lax.all_gather(moved[2], "seq", axis=0, tiled=True),
        lax.all_gather(moved[3], "seq", axis=0, tiled=True),
    )
    return (video_out, finished[0], finished[1], finished[2], finished[3])


def solution(mesh):
    placed = (
        P("seq", "aud"),
        P("seq", "aud"),
        P("seq", "aud"),
        P("aud", None),
        P("aud", None),
        P("aud", None),
        P("seq", "aud"),
        P("aud", None),
        P("seq", None),
        P("seq"),
    )
    return jax.shard_map(
        local,
        mesh=mesh,
        in_specs=placed,
        out_specs=(P("seq", "aud"), P("aud", None), P("aud", None), P("aud", None), P("aud", None)),
        check_vma=False,
    )
```

profile of v0, /device:TPU:48, one launch (start us, length us, event | category | flops | bytes accessed | tf_op | source)
XLA Modules:
  0.0 2251.3 jit_solution(230839172410568593)
XLA Ops:
  7.2 1.7 copy.296
  8.9 8.6 all-to-all-start
  17.5 1.7 copy.295
  19.2 5.2 all-to-all-done
  24.3 7.9 all-to-all-start.1
  33.7 6.4 all-to-all-done.1
  49.8 7.3 all-to-all-start.2
  57.3 8.8 all-to-all-done.2
  69.1 7.0 all-to-all-start.4
  76.8 162.6 %all-gather.4 = f32[64,2,512]{2,1,0:T(2,128)S(1)} all-gather(f32[1,2,512]{2,1,0:T(2,128)S(1)} %bitcast.239), channel_id=3, replica_groups=mesh['seq'=64,'aud'=8] {'seq'}, dimensions={0}, use_global_device_ids=true | all-gather | bytes 266240 | tf_op jit(solution)/shard_map/all_gather | solution.py:13
  239.4 151.2 %all-gather.3 = f32[64,2,512]{2,1,0:T(2,128)S(1)} all-gather(f32[1,2,512]{2,1,0:T(2,128)S(1)} %bitcast.234), channel_id=2, replica_groups=mesh['seq'=64,'aud'=8] {'seq'}, dimensions={0}, use_global_device_ids=true | all-gather | bytes 266240 | tf_op jit(solution)/shard_map/all_gather | solution.py:13
  393.2 7.3 all-to-all-start.6
  400.5 282.1 %reduce-scatter.8.cloned.1.call-done = f32[8,256]{1,0:T(8,128)} async-done(((f32[512,256]{1,0:T(8,128)}), f32[8,256]{1,0:T(8,128)}) %reduce-scatter.8.cloned.1.call-update) | async-done | bytes 8208 | tf_op jit(solution)/shard_map/reduce_scatter | solution.py:198
  684.6 6.3 all-to-all-start.7
  690.8 154.5 %all-gather.7 = bf16[64,1,2048]{2,1,0:T(2,128)(2,1)S(1)} all-gather(bf16[1,1,2048]{2,1,0:T(2,128)(2,1)S(1)} %bitcast.236), channel_id=1, replica_groups=mesh['seq'=64,'aud'=8] {'seq'}, dimensions={0}, use_global_device_ids=true | all-gather | bytes 266240 | tf_op jit(solution)/shard_map/all_gather | solution.py:226
  846.2 153.9 %all-gather.8 = bf16[64,1,2048]{2,1,0:T(2,128)(2,1)S(1)} all-gather(bf16[1,1,2048]{2,1,0:T(2,128)(2,1)S(1)} %bitcast.237), channel_id=1, replica_groups=mesh['seq'=64,'aud'=8] {'seq'}, dimensions={0}, use_global_device_ids=true | all-gather | bytes 266240 | tf_op jit(solution)/shard_map/all_gather | solution.py:227
  1000.9 3.5 fusion.96
  1004.5 3.2 copy-done.2
  1009.1 355.4 %all-gather.17.cloned.1.call-done = f32[128,512,128]{2,1,0:T(8,128)} async-done(((f32[2,512,128]{2,1,0:T(8,128)}), f32[128,512,128]{2,1,0:T(8,128)}) %all-gather.17.cloned.1.call-update) | async-done | bytes 33554448 | tf_op jit(solution)/shard_map/all_gather | solution.py:13
  1364.5 23.1 %slice.39 = f32[126,512,128]{2,1,0:T(8,128)} slice(f32[128,512,128]{2,1,0:T(8,128)} %all-gather.17.cloned.1.call-done), slice={[2:128], [0:512], [0:128]} | slice | bytes 66060288 | tf_op jit(solution)/shard_map/slice | solution.py:15
  1387.6 97.9 %while.14 = (s32[]{:T(128)}, f32[2,512]{1,0:T(2,128)S(1)}, f32[2,512]{1,0:T(2,128)S(1)}, f32[2,512,128]{2,1,0:T(8,128)S(1)}, f32[63,2,512]{2,1,0:T(2,128)S(1)}, ...) while((s32[]{:T(128)}, f32[2,512]{1,0:T(2,128)S(1)}, f32[2,512]{1,0:T(2,128)S(1)}, ...), condition=%wide.region_8.9_spmd, body=%wide.region_7.8_spmd.sunk | while | flops 399362 | bytes 1613917 | solution.py:16
  1395.4 1.5 fusion.114
  1406.3 1.5 fusion.114
  1417.2 1.5 fusion.114
  1428.1 1.5 fusion.114
  1490.4 7.5 all-to-all-start.3
  1497.9 111.0 %all-gather.15.cloned.1.call-done = bf16[2,8192,128]{1,2,0:T(8,128)(2,1)} async-done(((bf16[2,128,128]{1,2,0:T(8,128)(2,1)}), bf16[2,8192,128]{1,2,0:T(8,128)(2,1)}) %all-gather.15.cloned.1.call-update) | async-done | bytes 4194320 | tf_op jit(solution)/shard_map/all_gather | solution.py:99
  1609.0 6.1 fusion.30
  1615.9 310.4 %reduce-scatter.4.cloned.1.call-done = f32[8,256]{1,0:T(8,128)} async-done(((f32[512,256]{1,0:T(8,128)}), f32[8,256]{1,0:T(8,128)}) %reduce-scatter.4.cloned.1.call-update) | async-done | bytes 8208 | tf_op jit(solution)/shard_map/reduce_scatter | solution.py:192
  1928.3 7.2 all-to-all-start.5
  1935.5 153.9 %all-gather.5 = bf16[64,1,2048]{2,1,0:T(2,128)(2,1)S(1)} all-gather(bf16[1,1,2048]{2,1,0:T(2,128)(2,1)S(1)} %bitcast.235), channel_id=1, replica_groups=mesh['seq'=64,'aud'=8] {'seq'}, dimensions={0}, use_global_device_ids=true | all-gather | bytes 266240 | tf_op jit(solution)/shard_map/all_gather | solution.py:224
  2090.3 153.3 %all-gather.6 = bf16[64,1,2048]{2,1,0:T(2,128)(2,1)S(1)} all-gather(bf16[1,1,2048]{2,1,0:T(2,128)(2,1)S(1)} %bitcast.238), channel_id=1, replica_groups=mesh['seq'=64,'aud'=8] {'seq'}, dimensions={0}, use_global_device_ids=true | all-gather | bytes 266240 | tf_op jit(solution)/shard_map/all_gather | solution.py:225
  (240 shorter events, 121.8 us)
Async XLA Ops:
  7.2 33.3 %copy-start = (bf16[128,256]{1,0:T(8,128)(2,1)S(1)}, bf16[128,256]{1,0:T(8,128)(2,1)}, u32[]{:S(2)}) copy-start(bf16[128,256]{1,0:T(8,128)(2,1)} %param.12) | copy-start | bytes 196612
  7.2 38.3 %copy-start.10 = (bf16[128,256]{1,0:T(8,128)(2,1)S(1)}, bf16[128,256]{1,0:T(8,128)(2,1)}, u32[]{:S(2)}) copy-start(bf16[128,256]{1,0:T(8,128)(2,1)} %param.18) | copy-start | bytes 196612
  8.9 15.4 all-to-all-start
  24.3 15.8 all-to-all-start.1
  32.2 358.5 %reduce-scatter.6.cloned.1.call-start = ((), (), s32[]{:S(2)}) async-start(), calls=%async_computation.14 | async-start | bytes 532480 | tf_op jit(solution)/shard_map/reduce_scatter | solution.py:195
  40.2 8.0 copy-start.11
  40.2 8.9 copy-start.8
  40.7 16.5 copy-start.12
  42.3 26.0 %copy-start.9 = (bf16[64,2048]{1,0:T(8,128)(2,1)S(1)}, bf16[64,2048]{1,0:T(8,128)(2,1)}, u32[]{:S(2)}) copy-start(bf16[64,2048]{1,0:T(8,128)(2,1)} %param.19) | copy-start | bytes 786436
  45.4 637.1 %reduce-scatter.8.cloned.1.call-start = ((), (), s32[]{:S(2)}) async-start(), calls=%async_computation.15 | async-start | bytes 532480 | tf_op jit(solution)/shard_map/reduce_scatter | solution.py:198
  48.1 952.8 %all-gather.13.cloned.1.call-start = ((), (), s32[]{:S(2)}) async-start(), calls=%async_computation.11 | async-start | bytes 4259840 | tf_op jit(solution)/shard_map/all_gather | solution.py:87
  49.8 16.2 all-to-all-start.2
  57.1 1307.3 %all-gather.17.cloned.1.call-start = ((), (), s32[]{:S(2)}) async-start(), calls=%async_computation.16 | async-start | bytes 34078720 | tf_op jit(solution)/shard_map/all_gather | solution.py:13
  57.2 18.9 copy-start.5
  69.1 321.5 %all-to-all-start.4 = ((bf16[64,8,256]{2,0,1:T(8,128)(2,1)}), bf16[64,8,256]{2,0,1:T(8,128)(2,1)S(1)}, u32[]{:S(2)}, u32[]{:S(2)}) async-start(bf16[64,8,256]{2,0,1:T(8,128)(2,1)} %bitcast.194), calls=%async_computation.4 | async-start | bytes 524288 | tf_op jit(solution)/shard_map/all_to_all | solution.py:71
  76.1 1532.9 %all-gather.15.cloned.1.call-start = ((), (), s32[]{:S(2)}) async-start(), calls=%async_computation.12 | async-start | bytes 4259840 | tf_op jit(solution)/shard_map/all_gather | solution.py:99
  239.4 765.1 %copy-start.3 = (f32[64,2,512]{2,1,0:T(2,128)}, f32[64,2,512]{2,1,0:T(2,128)S(1)}, u32[]{:S(2)}) copy-start(f32[64,2,512]{2,1,0:T(2,128)S(1)} %all-gather.4) | copy-start | bytes 786436
  390.6 613.9 %copy-start.4 = (f32[64,2,512]{2,1,0:T(2,128)}, f32[64,2,512]{2,1,0:T(2,128)S(1)}, u32[]{:S(2)}) copy-start(f32[64,2,512]{2,1,0:T(2,128)S(1)} %all-gather.3) | copy-start | bytes 786436
  393.2 291.3 %all-to-all-start.6 = ((bf16[8,2,128]{2,1,0:T(2,128)(2,1)}), bf16[8,2,128]{2,1,0:T(2,128)(2,1)S(1)}, u32[]{:S(2)}, u32[]{:S(2)}) async-start(bf16[8,2,128]{2,1,0:T(2,128)(2,1)} %reshape.244), calls=%async_computation.8 | async-start | bytes 8192 | tf_op jit(solution)/shard_map/all_to_all | solution.py:216
  684.6 161.6 %all-to-all-start.7 = ((bf16[8,2,128]{2,1,0:T(2,128)(2,1)}), bf16[8,2,128]{2,1,0:T(2,128)(2,1)S(1)}, u32[]{:S(2)}, u32[]{:S(2)}) async-start(bf16[8,2,128]{2,1,0:T(2,128)(2,1)} %reshape.246), calls=%async_computation.10 | async-start | bytes 8192 | tf_op jit(solution)/shard_map/all_to_all | solution.py:219
  690.8 1235.5 %reduce-scatter.4.cloned.1.call-start = ((), (), s32[]{:S(2)}) async-start(), calls=%async_computation.13 | async-start | bytes 532480 | tf_op jit(solution)/shard_map/reduce_scatter | solution.py:192
  1004.4 3.2 copy-start.2
  1009.0 378.6 %slice-start.1 = ((f32[64,2,512]{2,1,0:T(2,128)}), f32[63,2,512]{2,1,0:T(2,128)S(1)}, s32[]{:S(2)}) async-start(f32[64,2,512]{2,1,0:T(2,128)} %copy-done.3), calls=%async_computation.18 | async-start | bytes 516096 | tf_op jit(solution)/shard_map/slice | solution.py:15
  1009.0 378.6 %slice-start.2 = ((f32[64,2,512]{2,1,0:T(2,128)}), f32[63,2,512]{2,1,0:T(2,128)S(1)}, s32[]{:S(2)}) async-start(f32[64,2,512]{2,1,0:T(2,128)} %copy-done.4), calls=%async_computation.19 | async-start | bytes 516096 | tf_op jit(solution)/shard_map/slice | solution.py:15
  1364.5 23.1 %slice-start = ((f32[128,512,128]{2,1,0:T(8,128)}), f32[2,512,128]{2,1,0:T(8,128)S(1)}, s32[]{:S(2)}) async-start(f32[128,512,128]{2,1,0:T(8,128)} %all-gather.17.cloned.1.call-done), calls=%async_computation.17 | async-start | bytes 1048576 | tf_op jit(solution)/shard_map/slice | solution.py:14
  1387.6 98.6 %copy-start.6 = (bf16[128,256]{0,1:T(8,128)(2,1)S(1)}, bf16[128,256]{0,1:T(8,128)(2,1)}, u32[]{:S(2)}) copy-start(bf16[128,256]{0,1:T(8,128)(2,1)} %copy-done.5) | copy-start | bytes 196612
  1387.6 98.6 %copy-start.7 = (bf16[128,2,128]{2,0,1:T(8,128)(2,1)S(1)}, bf16[128,2,128]{2,0,1:T(8,128)(2,1)}, u32[]{:S(2)}) copy-start(bf16[128,2,128]{2,0,1:T(8,128)(2,1)} %copy.172) | copy-start | bytes 196612
  1488.5 755.9 %copy-start.1 = (bf16[128,256]{1,0:T(8,128)(2,1)S(1)}, bf16[128,256]{1,0:T(8,128)(2,1)}, u32[]{:S(2)}) copy-start(bf16[128,256]{1,0:T(8,128)(2,1)} %param.12) | copy-start | bytes 196612
  1490.4 125.5 %all-to-all-start.3 = ((bf16[8,2,128]{2,1,0:T(2,128)(2,1)}), bf16[8,2,128]{2,1,0:T(2,128)(2,1)S(1)}, u32[]{:S(2)}, u32[]{:S(2)}) async-start(bf16[8,2,128]{2,1,0:T(2,128)(2,1)} %reshape.240), calls=%async_computation.3 | async-start | bytes 8192 | tf_op jit(solution)/shard_map/all_to_all | solution.py:210
  1928.3 161.9 %all-to-all-start.5 = ((bf16[8,2,128]{2,1,0:T(2,128)(2,1)}), bf16[8,2,128]{2,1,0:T(2,128)(2,1)S(1)}, u32[]{:S(2)}, u32[]{:S(2)}) async-start(bf16[8,2,128]{2,1,0:T(2,128)(2,1)} %reshape.242), calls=%async_computation.6 | async-start | bytes 8192 | tf_op jit(solution)/shard_map/all_to_all | solution.py:213
Sparse Core Ops, SparseCore 0:
  45.5 321.1 reduce-scatter.5
  369.7 312.7 reduce-scatter.7
  684.7 299.1 all-gather.12
  985.8 378.6 all-gather.16
  1366.9 242.0 all-gather.14
  1611.6 314.6 reduce-scatter.3
where the time goes:
time: 2260 us; the launch traced here: 2250 us
  waiting for transfers between devices  1080 us (48%)
  blocking collectives  929 us (41%)
  other arithmetic  105 us (5%)
  starting transfers between devices  59.1 us (3%)
  local copies, waits for them, and re-layouts  46.4 us (2%)
    all_gather x1, waiting for transfers between devices, combined_all(): pieces = jax.tree.map(lambda part: lax.all_gather(part, axis), value)  355 us
    all_gather x2, blocking collectives, combined_all(): pieces = jax.tree.map(lambda part: lax.all_gather(part, axis), value)  314 us
    reduce_scatter x1, waiting for transfers between devices, local(): lax.psum_scatter(reorder_rows(flat_query, audio_count, seq_count), 'seq',...  310 us
    reduce_scatter x1, waiting for transfers between devices, local(): lax.psum_scatter(reorder_rows(flat_value, audio_count, seq_count), 'seq',...  282 us
    all_gather x1, blocking collectives, local(): lax.all_gather(moved[2], 'seq', axis=0, tiled=True)  154 us
    all_gather x1, blocking collectives, local(): lax.all_gather(moved[0], 'seq', axis=0, tiled=True)  154 us
    all_gather x1, blocking collectives, local(): lax.all_gather(moved[3], 'seq', axis=0, tiled=True)  154 us
    all_gather x1, blocking collectives, local(): lax.all_gather(moved[1], 'seq', axis=0, tiled=True)  153 us
  transfers between devices with their start and end apart: 14, of which 7 were waited for; matrix products, arithmetic and copies ran while one was open for 7% of the time, Pallas kernels for 0%

commit v1 on v0

v1 whole, which is shorter than its diff:
```python
import functools
import math

import jax
import jax.numpy as jnp
from jax import lax
from jax.experimental import pallas as pl
from jax.experimental.pallas import tpu as pltpu
from jax.sharding import Mesh, PartitionSpec as P

HEAD_DIM = 128
ROWS = ("x", "yl")
COLS = ("z",)
AUD = ("yh", "core")
SEQ = ROWS + COLS
SCALE = 1.0 / math.sqrt(HEAD_DIM)
bf16 = jnp.bfloat16
f32 = jnp.float32
VMEM_LIMIT = 20 * 1024 * 1024
PACK = 528
CHUNK = 32
SENT = 160


VM = pl.BlockSpec(memory_space=pltpu.VMEM)
SM = pl.BlockSpec(memory_space=pltpu.SMEM)
HBM = pl.BlockSpec(memory_space=pl.ANY)


def call(
    kernel, outs, flops, scratch=(), smem=0, args=(), in_specs=None, out_specs=None, limit=VMEM_LIMIT
):
    return pl.pallas_call(
        kernel,
        out_shape=[jax.ShapeDtypeStruct(s, d) for s, d in outs],
        in_specs=in_specs or [SM] * smem + [VM] * (len(args) - smem),
        out_specs=out_specs or [VM] * len(outs),
        scratch_shapes=list(scratch),
        compiler_params=pltpu.CompilerParams(vmem_limit_bytes=limit),
        cost_estimate=pl.CostEstimate(flops=flops, bytes_accessed=4000000, transcendentals=0),
    )(*args)


def dot_t(left, right):
    return lax.dot_general(left, right, (((1,), (1,)), ((), ())), preferred_element_type=f32)


def dot_n(left, right):
    return lax.dot_general(left, right, (((1,), (0,)), ((), ())), preferred_element_type=f32)


def dot_tn(left, right):
    return lax.dot_general(left, right, (((0,), (0,)), ((), ())), preferred_element_type=f32)


def pack_video(list_ref, count_ref, *rest):
    ins, (out_ref, twice_ref), (held, marks, sems) = rest[:4], rest[4:6], rest[6:]
    loads = [
        pltpu.make_async_copy(ref, held.at[place], sems.at[place])
        for place, ref in enumerate(ins)
    ]
    for load in loads:
        load.start()
    lanes = lax.broadcasted_iota(jnp.int32, (16, 256), 1)
    block = (lanes % 64) // 16
    allow = jnp.zeros((16, 256), f32)
    for slot in range(3):
        entry = jnp.where(slot < count_ref[0], list_ref[0, slot], -2)
        allow = jnp.where(block == entry, 1.0, allow)
    marks[...] = allow.astype(bf16)
    stores = []
    for dest in range(8):
        stores.append(
            pltpu.make_async_copy(marks, out_ref.at[dest, 512:528], sems.at[4 + len(stores)])
        )
        stores[-1].start()
    for place, load in enumerate(loads):
        load.wait()
        targets = [out_ref.at[dest, place * 128 : place * 128 + 128] for dest in range(8)]
        if place == 0:
            targets += [twice_ref.at[0:128], twice_ref.at[128:256]]
        for target in targets:
            stores.append(
                pltpu.make_async_copy(held.at[place], target, sems.at[4 + len(stores)])
            )
            stores[-1].start()
    for store in stores:
        store.wait()


def pack_audio(where_ref, q_ref, g_ref, k_ref, v_ref, mine_ref, other_ref, wide):
    start = pl.multiple_of(where_ref[0] * 8, 8)
    core = lax.rem(where_ref[1], 2)
    for place, ref in enumerate((q_ref, g_ref, k_ref, v_ref)):
        wide[place, :, :] = ref[...].astype(f32)
    for shift in range(4):
        chip = lax.rem(where_ref[1] // 2 + shift, 4)
        for out, side in ((mine_ref, core), (other_ref, 1 - core)):
            cols = pl.ds(pl.multiple_of((chip * 2 + side) * 256, 256), 256)
            parts = [wide[place, pl.ds(start, 8), cols] for place in range(4)]
            out[shift, 0:16, :] = jnp.concatenate(parts[:2], 0).astype(bf16)
            out[shift, 16:32, :] = jnp.concatenate(parts[2:], 0).astype(bf16)


def pair_audio(mine_ref, other_ref, *outs):
    for shift in range(4):
        outs[shift][0] = mine_ref[shift]
        outs[shift][1] = other_ref[shift]


def gather_audio(where_ref, *rest):
    chunks, diag_ref, send_ref, wide_ref, flat_ref = rest[:4], *rest[4:]
    wide_ref[...] = jnp.zeros((4, 128, 256), f32)
    core = lax.rem(where_ref[1], 2)
    for piece in range(8):
        shift, side = piece // 2, piece % 2
        chip = lax.rem(where_ref[1] // 2 + (4 - shift), 4)
        source = chip * 2 + (core if side == 0 else 1 - core)
        part = chunks[shift][side].astype(f32)
        for place in range(4):
            piece_rows = part[place * 8 : place * 8 + 8, :]
            for h in range(2):
                rows = pl.ds(pl.multiple_of(source * 8 + h * 64, 8), 8)
                lanes = slice(h * 128, h * 128 + 128)
                wide_ref[place, rows, lanes] = piece_rows[:, lanes]
            if place >= 2:
                rows = pl.ds(pl.multiple_of(source * 8 + (place - 2) * 64, 8), 8)
                flat_ref[rows, :] = piece_rows
    diag_ref[...] = wide_ref[...].astype(bf16)
    flat = flat_ref[...].astype(bf16)
    for dest in range(8):
        send_ref[dest] = flat


def thirds(whole):
    high = whole.astype(bf16).astype(f32)
    middle = (whole - high).astype(bf16).astype(f32)
    return [high, middle, whole - high - middle]


def joined(rows):
    return rows[0:1, :] + rows[1:2, :] + rows[2:3, :]


def back_stats(packed_ref, diag_ref, stats_ref, score_ref, dprob_ref):
    queries, upstream = diag_ref[0], diag_ref[1]
    best = jnp.full((1, 128), -1e30, f32)
    for r in range(8):
        allowed = packed_ref[r, 512:528, 0:128].astype(f32)[0:1, :] > 0.5
        scores = dot_t(packed_ref[r, 128:256, :], queries) * SCALE
        score_ref[r] = scores
        dprob_ref[r] = dot_t(packed_ref[r, 256:384, :], upstream)
        peak = jnp.max(scores, axis=0, keepdims=True)
        best = jnp.maximum(best, jnp.where(allowed, peak, -1e30))
    total = jnp.zeros((1, 128), f32)
    delta = jnp.zeros((1, 128), f32)
    for r in range(8):
        allowed = packed_ref[r, 512:528, 0:128].astype(f32)[0:1, :] > 0.5
        weights = jnp.where(allowed, jnp.exp(score_ref[r] - best), 0.0)
        total += jnp.sum(weights, axis=0, keepdims=True)
        delta += jnp.sum(weights.astype(bf16).astype(f32) * dprob_ref[r], axis=0, keepdims=True)
    stats = thirds(best) + thirds(total) + thirds(delta) + [jnp.zeros((7, 128), f32)]
    stats = jnp.concatenate(stats, 0)
    stats_ref[...] = jnp.concatenate((stats, jnp.zeros((16, 128), f32)), 1).astype(bf16)


def self_part(cols_ref, packed_ref, stats_ref, out_ref):
    for block in range(8):
        logs = []
        for h in range(2):
            lanes = slice(h * 128, h * 128 + 128)
            queries = cols_ref[block, 0:128, lanes]
            keys = packed_ref[:, 128:256, lanes].reshape(1024, 128)
            values = packed_ref[:, 256:384, lanes].reshape(1024, 128)
            scores = dot_t(queries, keys)
            best = jnp.max(scores, axis=1, keepdims=True)
            weights = jnp.exp((scores - best) * SCALE)
            total = jnp.sum(weights, axis=1, keepdims=True)
            out = dot_n(weights.astype(bf16), values) / total
            out_ref[block, 0:128, lanes] = out.astype(bf16)
            logs.append(jnp.broadcast_to(best * SCALE + jnp.log(total), (128, 8)))
        whole = jnp.concatenate([jnp.transpose(part)[0:1, :] for part in logs], 1)
        rows = jnp.concatenate(thirds(whole) + [jnp.zeros((13, 256), f32)], 0)
        out_ref[block, 128:144, :] = rows.astype(bf16)
        out_ref[block, 144:160, :] = stats_ref[...]


def cross_part(where_ref, packed_ref, audio_ref, diag_ref, own_ref, gk_ref, gv_ref, out_ref):
    diag_key, diag_value = diag_ref[2], diag_ref[3]
    key_terms = jnp.zeros((128, 256), f32)
    value_terms = jnp.zeros((128, 256), f32)
    for r in range(8):
        allowed = packed_ref[r, 512:528, 0:128].astype(f32)[0:1, :] > 0.5
        queries2, upstream2 = packed_ref[r, 0:128, :], packed_ref[r, 384:512, :]
        stats = []
        for h in range(2):
            lanes = slice(h * 128, h * 128 + 128)
            keys = audio_ref[:, 0:64, lanes].reshape(512, 128)
            values = audio_ref[:, 64:128, lanes].reshape(512, 128)
            scores = dot_t(queries2[:, lanes], keys) * SCALE
            parts = [scores[:, b * 128 : b * 128 + 128] for b in range(4)]
            peak = jnp.where(allowed, functools.reduce(jnp.maximum, parts), -jnp.inf)
            best = jnp.max(peak, axis=1, keepdims=True)
            weights = [jnp.where(allowed, jnp.exp(p - best), 0.0) for p in parts]
            total = jnp.sum(sum(weights), axis=1, keepdims=True)
            weights = jnp.concatenate([w.astype(bf16) for w in weights], 1)
            out = dot_n(weights, values) / total
            out_ref[r, :, lanes] = out
            delta = jnp.sum(upstream2[:, lanes].astype(f32) * out, axis=1, keepdims=True)
            stats.append((best, total, delta))
        low_lanes = lax.broadcasted_iota(jnp.int32, (128, 128), 1) < 64
        best, total, delta = [jnp.where(low_lanes, s0, s1) for s0, s1 in zip(*stats)]
        scores = dot_t(queries2, diag_key) * SCALE
        probs = jnp.where(allowed, jnp.exp(scores - best), 0.0) / total
        dscores = probs * (dot_t(upstream2, diag_value) - delta)
        value_terms += dot_tn(probs.astype(bf16), upstream2)
        key_terms += dot_tn(dscores.astype(bf16), queries2)
    for h in range(2):
        rows, lanes = slice(h * 64, h * 64 + 64), slice(h * 128, h * 128 + 128)
        gk_ref[rows, :] = key_terms[rows, lanes] * SCALE
        gv_ref[rows, :] = value_terms[rows, lanes]
    own_ref[...] = out_ref[where_ref[0]]


def back_terms(sent_ref, packed_ref, diag_ref, gk_ref, gv_ref, out_ref):
    stats = [sent_ref[c, 144:160, 0:128].astype(f32) for c in range(8)]
    bests = [joined(part[0:3, :]) for part in stats]
    best = functools.reduce(jnp.maximum, bests)
    factors = [jnp.exp(part - best) for part in bests]
    total = sum(joined(part[3:6, :]) * factor for part, factor in zip(stats, factors))
    delta = sum(joined(part[6:9, :]) * factor for part, factor in zip(stats, factors)) / total
    queries, upstream = diag_ref[0], diag_ref[1]
    attn = jnp.zeros((128, 256), f32)
    grads = jnp.zeros((128, 256), f32)
    for r in range(8):
        allowed = packed_ref[r, 512:528, 0:128].astype(f32)[0:1, :] > 0.5
        keys, values = packed_ref[r, 128:256, :], packed_ref[r, 256:384, :]
        weights = jnp.where(allowed, jnp.exp(dot_t(keys, queries) * SCALE - best), 0.0)
        dscores = (weights / total) * (dot_t(values, upstream) - delta)
        attn += dot_tn(weights.astype(bf16), values)
        grads += dot_tn(dscores.astype(bf16), keys)
    totals = jnp.transpose(jnp.broadcast_to(total, (128, 128)))
    attn = jnp.concatenate((attn[:, 0:128] / totals, attn[:, 128:256] / totals), 1)
    grads = grads * SCALE
    for h in range(2):
        lanes = slice(h * 128, h * 128 + 128)
        for a in range(8):
            rows = slice(h * 64 + a * 8, h * 64 + a * 8 + 8)
            out_ref[a * 8 + h] = attn[rows, lanes]
            out_ref[a * 8 + 2 + h] = grads[rows, lanes]
            out_ref[a * 8 + 4 + h] = gk_ref[rows, :]
            out_ref[a * 8 + 6 + h] = gv_ref[rows, :]


def add_terms(terms_ref, out_ref):
    sums = [sum(terms_ref[a * 8 + c] for c in range(8)) for a in range(8)]
    sums = jnp.concatenate(sums, 0).astype(bf16)
    for dest in range(64):
        out_ref[dest] = sums


def lay_out(final_ref, *outs):
    for i in range(4):
        for h in range(2):
            for pair in range(4):
                first = final_ref[pair * 16 + i * 2 + h].astype(f32)
                second = final_ref[pair * 16 + 8 + i * 2 + h].astype(f32)
                for a in range(8):
                    both = jnp.concatenate(
                        (first[a * 8 : a * 8 + 8, :], second[a * 8 : a * 8 + 8, :]), 0
                    )
                    outs[i][
                        pair * 16 : pair * 16 + 16, a * 256 + h * 128 : a * 256 + h * 128 + 128
                    ] = both.astype(bf16)


def join_video(own_ref, sent_ref, out_ref):
    logs = [joined(sent_ref[c, 128:144, :].astype(f32)) for c in range(8)]
    best = functools.reduce(jnp.maximum, logs)
    shares = [jnp.exp(log - best) for log in logs]
    total = sum(shares)
    for h in range(2):
        lanes = slice(h * 128, h * 128 + 128)
        result = own_ref[:, lanes]
        for c in range(8):
            column = jnp.transpose(jnp.broadcast_to((shares[c] / total)[:, lanes], (128, 128)))
            result += sent_ref[c, 0:128, lanes].astype(f32) * column
        out_ref[:, lanes] = result.astype(bf16)


def rotate(value, axis, shift):
    count = lax.axis_size(axis)
    return lax.ppermute(value, axis, [(i, (i + shift) % count) for i in range(count)])


def local(
    video_query,
    video_key,
    video_value,
    audio_query,
    audio_key,
    audio_value,
    video_grad,
    audio_grad,
    block_list,
    block_count,
):
    where = jnp.stack(
        (lax.axis_index(ROWS), lax.axis_index(AUD), lax.axis_index(COLS))
    ).astype(jnp.int32)

    mine, other = call(
        pack_audio,
        [((4, CHUNK, 256), bf16)] * 2,
        10**6,
        scratch=[pltpu.VMEM((4, 64, 2048), f32)],
        smem=1,
        args=(where, audio_query, audio_grad, audio_key, audio_value),
    )
    other = rotate(other, "core", 1)
    packed, twice = call(
        pack_video,
        [((8, PACK, 256), bf16), ((256, 256), bf16)],
        10**6,
        scratch=[
            pltpu.VMEM((4, 128, 256), bf16),
            pltpu.VMEM((16, 256), bf16),
            pltpu.SemaphoreType.DMA((46,)),
        ],
        in_specs=[SM, SM] + [HBM] * 4,
        limit=60 * 1024 * 1024,
        out_specs=[HBM, HBM],
        args=(block_list, block_count, video_query, video_key, video_value, video_grad),
    )
    cols_query = lax.all_gather(twice, COLS)
    packed = lax.all_to_all(packed, ROWS, 0, 0, tiled=True)
    chunks = call(pair_audio, [((2, CHUNK, 256), bf16)] * 4, 10**6, args=(mine, other))
    chunks = [chunks[0]] + [rotate(chunks[shift], "yh", shift) for shift in range(1, 4)]

    diag, shared = call(
        gather_audio,
        [((4, 128, 256), bf16), ((8, 128, 256), bf16)],
        10**6,
        scratch=[pltpu.VMEM((4, 128, 256), f32), pltpu.VMEM((128, 256), f32)],
        smem=1,
        args=(where, *chunks),
    )
    packed, shared = lax.optimization_barrier((packed, shared))
    shared = lax.all_to_all(shared, ROWS, 0, 0, tiled=True)
    (stats,) = call(
        back_stats,
        [((16, 256), bf16)],
        10**9,
        scratch=[pltpu.VMEM((8, 128, 128), f32)] * 2,
        args=(packed, diag),
    )
    (sent,) = call(
        self_part, [((8, SENT, 256), bf16)], 4 * 10**9, args=(cols_query, packed, stats)
    )
    sent, shared = lax.optimization_barrier((sent, shared))
    sent = lax.all_to_all(sent, COLS, 0, 0, tiled=True)
    cross_own, key_terms, value_terms = call(
        cross_part,
        [((128, 256), f32), ((128, 128), f32), ((128, 128), f32)],
        4 * 10**9,
        scratch=[pltpu.VMEM((8, 128, 256), f32)],
        smem=1,
        args=(where, packed, shared, diag),
    )
    (terms,) = call(
        back_terms,
        [((64, 8, 128), f32)],
        10**9,
        args=(sent, packed, diag, key_terms, value_terms),
    )
    terms = lax.all_to_all(terms, AUD + COLS, 0, 0, tiled=True)
    (video_out,) = call(join_video, [((128, 256), bf16)], 10**7, args=(cross_own, sent))
    (summed,) = call(add_terms, [((64, 64, 128), bf16)], 10**6, args=(terms,))
    final = lax.all_to_all(summed, SEQ, 0, 0, tiled=True)
    finished = call(lay_out, [((64, 2048), bf16)] * 4, 10**6, args=(final,))
    return (video_out, *finished)


def solution(mesh):
    fine = Mesh(mesh.devices.reshape(4, 2, 8, 4, 2), ("x", "yl", "z", "yh", "core"))
    video, audio = P(SEQ, AUD), P(AUD, None)
    return jax.shard_map(
        local,
        mesh=fine,
        in_specs=(
            video,
            video,
            video,
            audio,
            audio,
            audio,
            video,
            audio,
            P(SEQ, None),
            P(SEQ),
        ),
        out_specs=(video, audio, audio, audio, audio),
        check_vma=False,
    )
```

time: 2260 us -> 166 us (0.07)
  the two profiles are of different devices: /device:TPU:48 before, /device:TPU:1 now
where the time goes in v1:
time: 166 us; the launch traced here: 164 us
  waiting for transfers between devices  55.1 us (33%)
  starting transfers between devices  38.7 us (23%)
  blocking collectives  26.1 us (16%)
  Pallas kernels  25 us (15%)
  between operations  14.8 us (9%)
  local copies, waits for them, and re-layouts  4.47 us (3%)
    all_to_all x1, blocking collectives, local(): terms = lax.all_to_all(terms, AUD + COLS, 0, 0, tiled=True)  26.1 us
    all_to_all x1, waiting for transfers between devices, local(): final = lax.all_to_all(summed, SEQ, 0, 0, tiled=True)  26 us
    pallas_call x11, Pallas kernels, call(): pl.pallas_call(kernel, out_shape=[jax.ShapeDtypeStruct(s, d) for s, d in...  25 us
    ppermute x4, starting transfers between devices, rotate(): lax.ppermute(value, axis, [(i, (i + shift) % count) for i in range(count)])  16.8 us
    ppermute x4, waiting for transfers between devices, rotate(): lax.ppermute(value, axis, [(i, (i + shift) % count) for i in range(count)])  11.8 us
    all_gather x1, waiting for transfers between devices, local(): cols_query = lax.all_gather(twice, COLS)  8.83 us
    all_to_all x1, waiting for transfers between devices, local(): sent = lax.all_to_all(sent, COLS, 0, 0, tiled=True)  7.68 us
    all_to_all x1, starting transfers between devices, local(): final = lax.all_to_all(summed, SEQ, 0, 0, tiled=True)  6.85 us
  transfers between devices with their start and end apart: 9, of which 6 were waited for; matrix products, arithmetic and copies ran while one was open for 0% of the time, Pallas kernels for 11%

profile of v1, /device:TPU:1, one launch (start us, length us, event | category | flops | bytes accessed | tf_op | source)
XLA Modules:
  0.0 164.2 jit_solution(4631045129575907823)
XLA Ops:
  7.8 3.2 %shard_map.137 = (bf16[8,528,256]{2,1,0:T(8,128)(2,1)}, bf16[256,256]{1,0:T(8,128)(2,1)}) custom-call(s32[1,3]{1,0:T(1,128)} %list_ref.1, s32[1]{0:T(128)S(6)} %copy.15.count_ref, bf16[128,256]{1,0:T(8,128)(2,1)} %rest_0_.1, bf16[128,256]{1,0:T(8,128)(2,1)} %rest_1_.1, bf16[128,256]{1,0:T(8,128)(2,1)} %rest_2_.1, bf16[128,256]{1,0:T(8,128)(2,1)} %rest_3_.1), custom_call_target="tpu_custom_call" | custom-call | flops 1000000 | bytes 4000000 | tf_op jit(solution)/shard_map/pallas_call | solution.py:33
  11.1 0.0 copy-start.5
  11.1 6.0 %all-to-all-start = ((bf16[8,528,256]{2,1,0:T(8,128)(2,1)}), bf16[8,528,256]{2,1,0:T(8,128)(2,1)S(1)}, u32[]{:S(2)}, u32[]{:S(2)}) async-start(bf16[8,528,256]{2,1,0:T(8,128)(2,1)} %get-tuple-element.26), calls=%async_computation | async-start | bytes 4325376 | tf_op jit(solution)/shard_map/all_to_all | solution.py:336
  17.1 0.0 all-gather.3.cloned.1.call-start
  17.2 0.7 all-gather.3.cloned.1.call-update
  17.9 0.1 pad_add_fusion.where_ref
  18.0 0.7 shard_map.138
  18.7 6.5 %collective-permute-start = (bf16[4,32,256]{2,1,0:T(8,128)(2,1)S(1)}, bf16[4,32,256]{2,1,0:T(8,128)(2,1)S(1)}, u32[]{:S(2)}, u32[]{:S(2)}) collective-permute-start(bf16[4,32,256]{2,1,0:T(8,128)(2,1)S(1)} %get-tuple-element.28), channel_id=1, source_target_pairs={{0,1},{1,0},{2,3},{3,2},{4,5},{5,4},{6,7},{7,6},{8,9},{9,8},{10,11... | collective-permute-start | bytes 196616 | tf_op jit(solution)/shard_map/ppermute | solution.py:293
  25.2 0.9 collective-permute-done.other_ref
  26.1 1.9 %collective-permute-start.1 = (bf16[2,32,256]{2,1,0:T(8,128)(2,1)S(1)}, bf16[2,32,256]{2,1,0:T(8,128)(2,1)S(1)}, u32[]{:S(2)}, u32[]{:S(2)}) collective-permute-start(bf16[2,32,256]{2,1,0:T(8,128)(2,1)S(1)} %get-tuple-element.30), channel_id=1, source_target_pairs={{0,2},{2,4},{4,6},{6,0},{1,3},{3,5},{5,7},{7,1},{8,10},{10,12},{12... | collective-permute-start | bytes 98312 | tf_op jit(solution)/shard_map/ppermute | solution.py:293
  28.0 3.4 %collective-permute-start.2 = (bf16[2,32,256]{2,1,0:T(8,128)(2,1)S(1)}, bf16[2,32,256]{2,1,0:T(8,128)(2,1)S(1)}, u32[]{:S(2)}, u32[]{:S(2)}) collective-permute-start(bf16[2,32,256]{2,1,0:T(8,128)(2,1)S(1)} %get-tuple-element.31), channel_id=1, source_target_pairs={{0,4},{2,6},{4,0},{6,2},{1,5},{3,7},{5,1},{7,3},{8,12},{10,14},{12... | collective-permute-start | bytes 98312 | tf_op jit(solution)/shard_map/ppermute | solution.py:293
  31.4 5.0 %collective-permute-start.3 = (bf16[2,32,256]{2,1,0:T(8,128)(2,1)S(1)}, bf16[2,32,256]{2,1,0:T(8,128)(2,1)S(1)}, u32[]{:S(2)}, u32[]{:S(2)}) collective-permute-start(bf16[2,32,256]{2,1,0:T(8,128)(2,1)S(1)} %get-tuple-element.32), channel_id=1, source_target_pairs={{0,6},{2,0},{4,2},{6,4},{1,7},{3,1},{5,3},{7,5},{8,14},{10,8},{12,... | collective-permute-start | bytes 98312 | tf_op jit(solution)/shard_map/ppermute | solution.py:293
  36.4 9.0 %collective-permute-done.1.rest_1_ = bf16[2,32,256]{2,1,0:T(8,128)(2,1)S(1)} collective-permute-done((bf16[2,32,256]{2,1,0:T(8,128)(2,1)S(1)}, bf16[2,32,256]{2,1,0:T(8,128)(2,1)S(1)}, u32[]{:S(2)}, u32[]{:S(2)}) %collective-permute-start.1) | collective-permute-done | bytes 32800 | tf_op jit(solution)/shard_map/ppermute | solution.py:293
  45.4 2.0 %collective-permute-done.2.rest_2_ = bf16[2,32,256]{2,1,0:T(8,128)(2,1)S(1)} collective-permute-done((bf16[2,32,256]{2,1,0:T(8,128)(2,1)S(1)}, bf16[2,32,256]{2,1,0:T(8,128)(2,1)S(1)}, u32[]{:S(2)}, u32[]{:S(2)}) %collective-permute-start.2) | collective-permute-done | bytes 32800 | tf_op jit(solution)/shard_map/ppermute | solution.py:293
  47.3 1.5 shard_map.140
  48.8 4.6 %all-to-all-start.1 = ((bf16[8,128,256]{2,1,0:T(8,128)(2,1)}), bf16[8,128,256]{2,1,0:T(8,128)(2,1)S(1)}, u32[]{:S(2)}, u32[]{:S(2)}) async-start(bf16[8,128,256]{2,1,0:T(8,128)(2,1)} %get-tuple-element.37), calls=%async_computation.1 | async-start | bytes 1048576 | tf_op jit(solution)/shard_map/all_to_all | solution.py:349
  53.4 0.6 shard_map.141.stats_ref
  54.1 8.8 %all-gather.3.cloned.1.call-done = bf16[2048,256]{1,0:T(8,128)(2,1)} async-done(((bf16[256,256]{1,0:T(8,128)(2,1)}), bf16[2048,256]{1,0:T(8,128)(2,1)}) %all-gather.3.cloned.1.call-update) | async-done | bytes 1048592 | tf_op jit(solution)/shard_map/all_gather | solution.py:335
  62.9 1.2 copy-done.7
  64.1 6.8 %shard_map.142 = bf16[8,160,256]{2,1,0:T(8,128)(2,1)} custom-call(bf16[8,256,256]{2,1,0:T(8,128)(2,1)S(1)} %bitcast.4, bf16[8,528,256]{2,1,0:T(8,128)(2,1)S(1)} %all-to-all-done.packed_ref, bf16[16,256]{1,0:T(8,128)(2,1)S(1)} %shard_map.141.stats_ref), custom_call_target="tpu_custom_call" | custom-call | flops 4000000000 | bytes 4000000 | tf_op jit(solution)/shard_map/pallas_call | solution.py:33
  70.9 4.4 %all-to-all-start.2 = ((bf16[8,160,256]{2,1,0:T(8,128)(2,1)}), bf16[8,160,256]{2,1,0:T(8,128)(2,1)S(1)}, u32[]{:S(2)}, u32[]{:S(2)}) async-start(bf16[8,160,256]{2,1,0:T(8,128)(2,1)} %shard_map.142), calls=%async_computation.2 | async-start | bytes 1310720 | tf_op jit(solution)/shard_map/all_to_all | solution.py:361
  75.3 1.6 copy-done.1
  76.9 6.9 %shard_map.143 = (f32[128,256]{1,0:T(8,128)S(1)}, f32[128,128]{1,0:T(8,128)S(1)}, f32[128,128]{1,0:T(8,128)S(1)}) custom-call(s32[3]{0:T(128)S(1)} %pad_add_fusion.where_ref, bf16[8,528,256]{2,1,0:T(8,128)(2,1)S(1)} %copy-done.1, bf16[8,128,256]{2,1,0:T(8,128)(2,1)S(1)} %all-to-all-done.1.audio_ref, bf16[4,128,256]{2,1,0:T(8,128)(2,1)S(1)} %get-tuple-element.36.diag_ref), custom_call_target="tpu_custom_call" | custom-call | flops 4000000000 | bytes 4000000 | tf_op jit(solution)/shard_map/pallas_call | solution.py:33
  83.8 7.7 %all-to-all-done.2.sent_ref = bf16[8,160,256]{2,1,0:T(8,128)(2,1)S(1)} async-done(((bf16[8,160,256]{2,1,0:T(8,128)(2,1)}), bf16[8,160,256]{2,1,0:T(8,128)(2,1)S(1)}, u32[]{:S(2)}, u32[]{:S(2)}) %all-to-all-start.2) | async-done | bytes 655392 | tf_op jit(solution)/shard_map/all_to_all | solution.py:361
  91.5 1.6 copy-done.2
  93.1 2.0 %shard_map.145 = f32[64,8,128]{2,1,0:T(8,128)S(1)} custom-call(bf16[8,160,256]{2,1,0:T(8,128)(2,1)S(1)} %all-to-all-done.2.sent_ref, bf16[8,528,256]{2,1,0:T(8,128)(2,1)S(1)} %copy-done.2, bf16[4,128,256]{2,1,0:T(8,128)(2,1)S(1)} %get-tuple-element.36.diag_ref, f32[128,128]{1,0:T(8,128)S(1)} %get-tuple-element.41.gk_ref, f32[128,128]{1,0:T(8,128)S(1)} %get-tuple-element.42.gv_ref), custom_call_target="tpu_custom_call" | custom-call | flops 1000000000 | bytes 4000000 | tf_op jit(solution)/shard_map/pallas_call | solution.py:33
  95.1 26.1 %all_to_all.25.terms_ref = f32[64,8,128]{2,1,0:T(8,128)S(1)} all-to-all(f32[64,8,128]{2,1,0:T(8,128)S(1)} %shard_map.145), channel_id=1, replica_groups=mesh['x'=4,'yl'=2,'z'=8,'yh'=4,'core'=2] {'yh','core','z'}, dimensions={0} | all-to-all | bytes 524288 | tf_op jit(solution)/shard_map/all_to_all | solution.py:376
  121.2 1.1 shard_map.146
  122.3 6.9 %all-to-all-start.4 = ((bf16[64,64,128]{2,1,0:T(8,128)(2,1)}), bf16[64,64,128]{2,1,0:T(8,128)(2,1)S(1)}, u32[]{:S(2)}, u32[]{:S(2)}) async-start(bf16[64,64,128]{2,1,0:T(8,128)(2,1)} %shard_map.146), calls=%async_computation.4 | async-start | bytes 2097152 | tf_op jit(solution)/shard_map/all_to_all | solution.py:379
  129.2 1.0 shard_map.144
  130.2 26.0 %all-to-all-done.4.final_ref = bf16[64,64,128]{2,1,0:T(8,128)(2,1)S(1)} async-done(((bf16[64,64,128]{2,1,0:T(8,128)(2,1)}), bf16[64,64,128]{2,1,0:T(8,128)(2,1)S(1)}, u32[]{:S(2)}, u32[]{:S(2)}) %all-to-all-start.4) | async-done | bytes 1048608 | tf_op jit(solution)/shard_map/all_to_all | solution.py:379
  156.2 1.1 shard_map.147
  (16 shorter events, 0.0 us)
Async XLA Ops:
  11.1 6.9 %copy-start.3 = (bf16[64,2048]{1,0:T(8,128)(2,1)S(1)}, bf16[64,2048]{1,0:T(8,128)(2,1)}, u32[]{:S(2)}) copy-start(bf16[64,2048]{1,0:T(8,128)(2,1)} %q_ref.1) | copy-start | bytes 786436
  11.1 6.9 %copy-start.4 = (bf16[64,2048]{1,0:T(8,128)(2,1)S(1)}, bf16[64,2048]{1,0:T(8,128)(2,1)}, u32[]{:S(2)}) copy-start(bf16[64,2048]{1,0:T(8,128)(2,1)} %g_ref.1) | copy-start | bytes 786436
  11.1 6.9 %copy-start.5 = (bf16[64,2048]{1,0:T(8,128)(2,1)S(1)}, bf16[64,2048]{1,0:T(8,128)(2,1)}, u32[]{:S(2)}) copy-start(bf16[64,2048]{1,0:T(8,128)(2,1)} %k_ref.1) | copy-start | bytes 786436
  11.1 6.9 %copy-start.6 = (bf16[64,2048]{1,0:T(8,128)(2,1)S(1)}, bf16[64,2048]{1,0:T(8,128)(2,1)}, u32[]{:S(2)}) copy-start(bf16[64,2048]{1,0:T(8,128)(2,1)} %v_ref.1) | copy-start | bytes 786436
  11.1 37.7 %all-to-all-start = ((bf16[8,528,256]{2,1,0:T(8,128)(2,1)}), bf16[8,528,256]{2,1,0:T(8,128)(2,1)S(1)}, u32[]{:S(2)}, u32[]{:S(2)}) async-start(bf16[8,528,256]{2,1,0:T(8,128)(2,1)} %get-tuple-element.26), calls=%async_computation | async-start | bytes 4325376 | tf_op jit(solution)/shard_map/all_to_all | solution.py:336
  17.1 45.8 %all-gather.3.cloned.1.call-start = ((), (), s32[]{:S(2)}) async-start(), calls=%async_computation.5 | async-start | bytes 1179648 | tf_op jit(solution)/shard_map/all_gather | solution.py:335
  18.7 7.4 %collective-permute-start = (bf16[4,32,256]{2,1,0:T(8,128)(2,1)S(1)}, bf16[4,32,256]{2,1,0:T(8,128)(2,1)S(1)}, u32[]{:S(2)}, u32[]{:S(2)}) collective-permute-start(bf16[4,32,256]{2,1,0:T(8,128)(2,1)S(1)} %get-tuple-element.28), channel_id=1, source_target_pairs={{0,1},{1,0},{2,3},{3,2},{4,5},{5,4},{6,7},{7,6},{8,9},{9,8},{10,11... | collective-permute-start | bytes 196616 | tf_op jit(solution)/shard_map/ppermute | solution.py:293
  26.1 19.3 %collective-permute-start.1 = (bf16[2,32,256]{2,1,0:T(8,128)(2,1)S(1)}, bf16[2,32,256]{2,1,0:T(8,128)(2,1)S(1)}, u32[]{:S(2)}, u32[]{:S(2)}) collective-permute-start(bf16[2,32,256]{2,1,0:T(8,128)(2,1)S(1)} %get-tuple-element.30), channel_id=1, source_target_pairs={{0,2},{2,4},{4,6},{6,0},{1,3},{3,5},{5,7},{7,1},{8,10},{10,12},{12... | collective-permute-start | bytes 98312 | tf_op jit(solution)/shard_map/ppermute | solution.py:293
  28.0 19.3 %collective-permute-start.2 = (bf16[2,32,256]{2,1,0:T(8,128)(2,1)S(1)}, bf16[2,32,256]{2,1,0:T(8,128)(2,1)S(1)}, u32[]{:S(2)}, u32[]{:S(2)}) collective-permute-start(bf16[2,32,256]{2,1,0:T(8,128)(2,1)S(1)} %get-tuple-element.31), channel_id=1, source_target_pairs={{0,4},{2,6},{4,0},{6,2},{1,5},{3,7},{5,1},{7,3},{8,12},{10,14},{12... | collective-permute-start | bytes 98312 | tf_op jit(solution)/shard_map/ppermute | solution.py:293
  31.4 15.9 %collective-permute-start.3 = (bf16[2,32,256]{2,1,0:T(8,128)(2,1)S(1)}, bf16[2,32,256]{2,1,0:T(8,128)(2,1)S(1)}, u32[]{:S(2)}, u32[]{:S(2)}) collective-permute-start(bf16[2,32,256]{2,1,0:T(8,128)(2,1)S(1)} %get-tuple-element.32), channel_id=1, source_target_pairs={{0,6},{2,0},{4,2},{6,4},{1,7},{3,1},{5,3},{7,5},{8,14},{10,8},{12,... | collective-permute-start | bytes 98312 | tf_op jit(solution)/shard_map/ppermute | solution.py:293
  48.8 14.1 %copy-start = (bf16[8,528,256]{2,1,0:T(8,128)(2,1)}, bf16[8,528,256]{2,1,0:T(8,128)(2,1)S(1)}, u32[]{:S(2)}) copy-start(bf16[8,528,256]{2,1,0:T(8,128)(2,1)S(1)} %all-to-all-done.packed_ref) | copy-start | bytes 6488068
  48.8 22.1 %all-to-all-start.1 = ((bf16[8,128,256]{2,1,0:T(8,128)(2,1)}), bf16[8,128,256]{2,1,0:T(8,128)(2,1)S(1)}, u32[]{:S(2)}, u32[]{:S(2)}) async-start(bf16[8,128,256]{2,1,0:T(8,128)(2,1)} %get-tuple-element.37), calls=%async_computation.1 | async-start | bytes 1048576 | tf_op jit(solution)/shard_map/all_to_all | solution.py:349
  62.9 1.2 copy-start.7
  70.9 20.6 %all-to-all-start.2 = ((bf16[8,160,256]{2,1,0:T(8,128)(2,1)}), bf16[8,160,256]{2,1,0:T(8,128)(2,1)S(1)}, u32[]{:S(2)}, u32[]{:S(2)}) async-start(bf16[8,160,256]{2,1,0:T(8,128)(2,1)} %shard_map.142), calls=%async_computation.2 | async-start | bytes 1310720 | tf_op jit(solution)/shard_map/all_to_all | solution.py:361
  75.3 1.6 copy-start.1
  91.5 1.6 copy-start.2
  122.3 33.9 %all-to-all-start.4 = ((bf16[64,64,128]{2,1,0:T(8,128)(2,1)}), bf16[64,64,128]{2,1,0:T(8,128)(2,1)S(1)}, u32[]{:S(2)}, u32[]{:S(2)}) async-start(bf16[64,64,128]{2,1,0:T(8,128)(2,1)} %shard_map.146), calls=%async_computation.4 | async-start | bytes 2097152 | tf_op jit(solution)/shard_map/all_to_all | solution.py:379
Sparse Core Ops, SparseCore 0:
  20.6 42.2 all-gather.2

commit v2 on v1

v2 whole, which is shorter than its diff:
```python
import functools
import math

import jax
import jax.numpy as jnp
from jax import lax
from jax.experimental import pallas as pl
from jax.experimental.pallas import tpu as pltpu
from jax.sharding import Mesh, PartitionSpec as P

HEAD_DIM = 128
ROWS = ("x", "yl")
COLS = ("z",)
AUD = ("yh", "core")
SEQ = ROWS + COLS
SCALE = 1.0 / math.sqrt(HEAD_DIM)
bf16 = jnp.bfloat16
f32 = jnp.float32
VMEM_LIMIT = 20 * 1024 * 1024
PACK = 656
CHUNK = 32
SENT = 144


VM = pl.BlockSpec(memory_space=pltpu.VMEM)
SM = pl.BlockSpec(memory_space=pltpu.SMEM)
HBM = pl.BlockSpec(memory_space=pl.ANY)


def call(
    kernel,
    outs,
    flops,
    scratch=(),
    smem=0,
    args=(),
    in_specs=None,
    out_specs=None,
    limit=VMEM_LIMIT,
    aliases=None,
):
    return pl.pallas_call(
        kernel,
        out_shape=[jax.ShapeDtypeStruct(s, d) for s, d in outs],
        in_specs=in_specs or [SM] * smem + [VM] * (len(args) - smem),
        out_specs=out_specs or [VM] * len(outs),
        scratch_shapes=list(scratch),
        input_output_aliases=aliases or {},
        compiler_params=pltpu.CompilerParams(vmem_limit_bytes=limit),
        cost_estimate=pl.CostEstimate(flops=flops, bytes_accessed=4000000, transcendentals=0),
    )(*args)


def dot_t(left, right):
    return lax.dot_general(left, right, (((1,), (1,)), ((), ())), preferred_element_type=f32)


def dot_n(left, right):
    return lax.dot_general(left, right, (((1,), (0,)), ((), ())), preferred_element_type=f32)


def dot_tn(left, right):
    return lax.dot_general(left, right, (((0,), (0,)), ((), ())), preferred_element_type=f32)


def side_by_side(first_ref, second_ref, out_ref):
    count = first_ref.shape[0]
    out_ref[0:count] = first_ref[...]
    out_ref[count : 2 * count] = second_ref[...]


def pack_video(list_ref, count_ref, *rest):
    ins, out_ref, held, marks, sems = rest[:4], *rest[4:]
    loads = [
        pltpu.make_async_copy(ref, held.at[place], sems.at[place])
        for place, ref in enumerate(ins)
    ]
    for load in loads:
        load.start()
    lanes = lax.broadcasted_iota(jnp.int32, (16, 256), 1)
    block = (lanes % 64) // 16
    allow = jnp.zeros((16, 256), f32)
    for slot in range(3):
        entry = jnp.where(slot < count_ref[0], list_ref[0, slot], -2)
        allow = jnp.where(block == entry, 1.0, allow)
    marks[...] = allow.astype(bf16)
    stores = []
    for dest in range(8):
        stores.append(
            pltpu.make_async_copy(marks, out_ref.at[dest, 512:528], sems.at[4 + len(stores)])
        )
        stores[-1].start()
    for place, load in enumerate(loads):
        load.wait()
        for dest in range(8):
            target = out_ref.at[dest, place * 128 : place * 128 + 128]
            stores.append(
                pltpu.make_async_copy(held.at[place], target, sems.at[4 + len(stores)])
            )
            stores[-1].start()
    for store in stores:
        store.wait()


def pack_audio(*rest):
    ins, out_ref, held, sems = rest[:4], *rest[4:]
    row = lax.axis_index(ROWS)
    pair = pl.ds(pl.multiple_of(row // 2 * 16, 16), 16)
    loads = [
        pltpu.make_async_copy(ref.at[pair], held.at[place], sems.at[place])
        for place, ref in enumerate(ins)
    ]
    for load in loads:
        load.start()
    parts = []
    for place, load in enumerate(loads):
        load.wait()
        both = held[place].astype(f32)
        parts.append(jnp.where(lax.rem(row, 2) == 0, both[0:8, :], both[8:16, :]))
    parts = jnp.concatenate(parts, 0).astype(bf16)
    for dest in range(8):
        out_ref[dest] = parts[:, dest * 256 : dest * 256 + 256]


def add_audio(audio_ref, given_ref, diag_ref, out_ref, wide_ref, flat_ref, flat16_ref, sems):
    for source in range(8):
        part = audio_ref[source].astype(f32)
        for place in (2, 3):
            row = source * 8 + (place - 2) * 64
            flat_ref[row : row + 8, :] = part[place * 8 : place * 8 + 8, :]
    flat16_ref[...] = flat_ref[...].astype(bf16)
    stores = [
        pltpu.make_async_copy(flat16_ref, out_ref.at[dest, 528:656], sems.at[dest])
        for dest in range(8)
    ]
    for store in stores:
        store.start()
    wide_ref[...] = jnp.zeros((4, 128, 256), f32)
    for source in range(8):
        part = audio_ref[source].astype(f32)
        for place in range(4):
            for h in range(2):
                row, lanes = source * 8 + h * 64, slice(h * 128, h * 128 + 128)
                wide_ref[place, row : row + 8, lanes] = part[place * 8 : place * 8 + 8, lanes]
    diag_ref[...] = wide_ref[...].astype(bf16)
    for store in stores:
        store.wait()


def thirds(whole):
    high = whole.astype(bf16).astype(f32)
    middle = (whole - high).astype(bf16).astype(f32)
    return [high, middle, whole - high - middle]


def joined(rows):
    return rows[0:1, :] + rows[1:2, :] + rows[2:3, :]


def back_stats(packed_ref, diag_ref, stats_ref, score_ref, dprob_ref):
    queries, upstream = diag_ref[0], diag_ref[1]
    best = jnp.full((1, 128), -1e30, f32)
    for r in range(8):
        allowed = packed_ref[r, 512:528, 0:128].astype(f32)[0:1, :] > 0.5
        scores = dot_t(packed_ref[r, 128:256, :], queries) * SCALE
        score_ref[r] = scores
        dprob_ref[r] = dot_t(packed_ref[r, 256:384, :], upstream)
        peak = jnp.max(scores, axis=0, keepdims=True)
        best = jnp.maximum(best, jnp.where(allowed, peak, -1e30))
    total = jnp.zeros((1, 128), f32)
    delta = jnp.zeros((1, 128), f32)
    for r in range(8):
        allowed = packed_ref[r, 512:528, 0:128].astype(f32)[0:1, :] > 0.5
        weights = jnp.where(allowed, jnp.exp(score_ref[r] - best), 0.0)
        total += jnp.sum(weights, axis=0, keepdims=True)
        delta += jnp.sum(weights.astype(bf16).astype(f32) * dprob_ref[r], axis=0, keepdims=True)
    stats = thirds(best) + thirds(total) + thirds(delta) + [jnp.zeros((4, 128), f32)]
    stats = jnp.concatenate(stats, 0)
    stats_ref[...] = jnp.concatenate((stats, jnp.zeros((13, 128), f32)), 1)


def self_part(near_ref, far_ref, packed_ref, stats_ref, out_ref):
    column = lax.axis_index("z")
    for part_ref, distances in ((near_ref, (0, 4, 2, 6)), (far_ref, (1, 5, 3, 7))):
        logs = []
        for h in range(2):
            lanes = slice(h * 128, h * 128 + 128)
            queries = part_ref[:, :, lanes].reshape(512, 128)
            keys = packed_ref[:, 128:256, lanes].reshape(1024, 128)
            values = packed_ref[:, 256:384, lanes].reshape(1024, 128)
            scores = dot_t(queries, keys)
            best = jnp.max(scores, axis=1, keepdims=True)
            weights = jnp.exp2((scores - best) * (SCALE * math.log2(math.e)))
            total = jnp.sum(weights, axis=1, keepdims=True)
            out = dot_n(weights.astype(bf16), values) / total
            out = out.astype(bf16).reshape(4, 128, 128)
            for place, distance in enumerate(distances):
                out_ref[7 - (column ^ distance), 0:128, lanes] = out[place]
            logs.append(jnp.broadcast_to(best * SCALE + jnp.log(total), (512, 128)))
        logs = [jnp.transpose(part)[0:1, :] for part in logs]
        for place, distance in enumerate(distances):
            whole = jnp.concatenate([part[:, place * 128 : place * 128 + 128] for part in logs], 1)
            rows = jnp.concatenate(thirds(whole) + [stats_ref[...]], 0)
            out_ref[7 - (column ^ distance), 128:144, :] = rows.astype(bf16)


def cross_part(
    packed_ref, diag_ref, own_ref, sums_ref, out_ref
):
    diag_key, diag_value = diag_ref[2], diag_ref[3]
    key_terms = jnp.zeros((128, 256), f32)
    value_terms = jnp.zeros((128, 256), f32)
    for r in range(8):
        allowed = packed_ref[r, 512:528, 0:128].astype(f32)[0:1, :] > 0.5
        queries2, upstream2 = packed_ref[r, 0:128, :], packed_ref[r, 384:512, :]
        stats = []
        for h in range(2):
            lanes = slice(h * 128, h * 128 + 128)
            keys = packed_ref[:, 528:592, lanes].reshape(512, 128)
            values = packed_ref[:, 592:656, lanes].reshape(512, 128)
            scores = dot_t(queries2[:, lanes], keys) * SCALE
            parts = [scores[:, b * 128 : b * 128 + 128] for b in range(4)]
            peak = jnp.where(allowed, functools.reduce(jnp.maximum, parts), -jnp.inf)
            best = jnp.max(peak, axis=1, keepdims=True)
            weights = [jnp.where(allowed, jnp.exp(p - best), 0.0) for p in parts]
            total = jnp.sum(sum(weights), axis=1, keepdims=True)
            weights = jnp.concatenate([w.astype(bf16) for w in weights], 1)
            out = dot_n(weights, values) / total
            out_ref[r, :, lanes] = out
            delta = jnp.sum(upstream2[:, lanes].astype(f32) * out, axis=1, keepdims=True)
            stats.append((best, total, delta))
        low_lanes = lax.broadcasted_iota(jnp.int32, (128, 128), 1) < 64
        best, total, delta = [jnp.where(low_lanes, s0, s1) for s0, s1 in zip(*stats)]
        scores = dot_t(queries2, diag_key) * SCALE
        probs = jnp.where(allowed, jnp.exp(scores - best), 0.0) / total
        dscores = probs * (dot_t(upstream2, diag_value) - delta)
        value_terms += dot_tn(probs.astype(bf16), upstream2)
        key_terms += dot_tn(dscores.astype(bf16), queries2)
    for h in range(2):
        rows, lanes = slice(h * 64, h * 64 + 64), slice(h * 128, h * 128 + 128)
        sums_ref[0, rows, :] = key_terms[rows, lanes] * SCALE
        sums_ref[1, rows, :] = value_terms[rows, lanes]
    own_ref[...] = out_ref[lax.axis_index(ROWS)]


def back_terms(
    sent_ref, packed_ref, diag_far_ref, sums_far_ref, out_ref, diag_ref, sums_ref, sems
):
    loads = [
        pltpu.make_async_copy(diag_far_ref.at[0:2], diag_ref, sems.at[0]),
        pltpu.make_async_copy(sums_far_ref, sums_ref, sems.at[1]),
    ]
    for load in loads:
        load.start()
    stats = [sent_ref[c, 128:144, 0:128].astype(f32) for c in range(8)]
    bests = [joined(part[3:6, :]) for part in stats]
    best = functools.reduce(jnp.maximum, bests)
    factors = [jnp.exp(part - best) for part in bests]
    total = sum(joined(part[6:9, :]) * factor for part, factor in zip(stats, factors))
    delta = sum(joined(part[9:12, :]) * factor for part, factor in zip(stats, factors)) / total
    for load in loads:
        load.wait()
    queries, upstream = diag_ref[0], diag_ref[1]
    attn = jnp.zeros((128, 256), f32)
    grads = jnp.zeros((128, 256), f32)
    for r in range(8):
        allowed = packed_ref[r, 512:528, 0:128].astype(f32)[0:1, :] > 0.5
        keys, values = packed_ref[r, 128:256, :], packed_ref[r, 256:384, :]
        weights = jnp.where(allowed, jnp.exp(dot_t(keys, queries) * SCALE - best), 0.0)
        dscores = (weights / total) * (dot_t(values, upstream) - delta)
        attn += dot_tn(weights.astype(bf16), values)
        grads += dot_tn(dscores.astype(bf16), keys)
    totals = jnp.transpose(jnp.broadcast_to(total, (128, 128)))
    attn = jnp.concatenate((attn[:, 0:128] / totals, attn[:, 128:256] / totals), 1)
    grads = grads * SCALE
    for h in range(2):
        lanes = slice(h * 128, h * 128 + 128)
        for a in range(8):
            rows = slice(h * 64 + a * 8, h * 64 + a * 8 + 8)
            out_ref[a * 8 + h] = attn[rows, lanes]
            out_ref[a * 8 + 2 + h] = grads[rows, lanes]
            out_ref[a * 8 + 4 + h] = sums_ref[0, rows, :]
            out_ref[a * 8 + 6 + h] = sums_ref[1, rows, :]


def add_terms(terms_ref, out_ref):
    sums = [sum(terms_ref[a * 8 + c] for c in range(8)) for a in range(8)]
    sums = jnp.concatenate(sums, 0).astype(bf16)
    for dest in range(8):
        out_ref[dest] = sums


def again(ref, out_ref):
    for dest in range(8):
        out_ref[dest] = ref[...]


def lay_out(final_ref, *outs):
    for i in range(4):
        for h in range(2):
            for pair in range(4):
                first = final_ref[pair * 2, 7 - i * 2 - h].astype(f32)
                second = final_ref[pair * 2 + 1, 7 - i * 2 - h].astype(f32)
                for a in range(8):
                    both = jnp.concatenate(
                        (first[a * 8 : a * 8 + 8, :], second[a * 8 : a * 8 + 8, :]), 0
                    )
                    outs[i][
                        pair * 16 : pair * 16 + 16, a * 256 + h * 128 : a * 256 + h * 128 + 128
                    ] = both.astype(bf16)


def join_video(own_ref, sent_ref, out_ref):
    logs = [joined(sent_ref[c, 128:144, :].astype(f32)) for c in range(8)]
    best = functools.reduce(jnp.maximum, logs)
    shares = [jnp.exp(log - best) for log in logs]
    total = sum(shares)
    for h in range(2):
        lanes = slice(h * 128, h * 128 + 128)
        result = own_ref[:, lanes]
        for c in range(8):
            column = jnp.transpose(jnp.broadcast_to((shares[c] / total)[:, lanes], (128, 128)))
            result += sent_ref[c, 0:128, lanes].astype(f32) * column
        out_ref[:, lanes] = result.astype(bf16)


def swap(value, axis, distance):
    count = lax.axis_size(axis)
    return lax.ppermute(value, axis, [(i, i ^ distance) for i in range(count)])


def backwards(value):
    return lax.all_to_all(
        value, "z", 0, 0, axis_index_groups=[[7, 6, 5, 4, 3, 2, 1, 0]], tiled=True
    )


def local(
    video_query,
    video_key,
    video_value,
    audio_query,
    audio_key,
    audio_value,
    video_grad,
    audio_grad,
    block_list,
    block_count,
):
    (audio,) = call(
        pack_audio,
        [((8, CHUNK, 256), bf16)],
        10**6,
        scratch=[
            pltpu.VMEM((4, 16, 2048), bf16),
            pltpu.SemaphoreType.DMA((4,)),
        ],
        in_specs=[HBM] * 4,
        limit=60 * 1024 * 1024,
        args=(audio_query, audio_grad, audio_key, audio_value),
    )
    audio = lax.all_to_all(audio, AUD, 0, 0, tiled=True)
    (packed,) = call(
        pack_video,
        [((8, PACK, 256), bf16)],
        10**6,
        scratch=[
            pltpu.VMEM((4, 128, 256), bf16),
            pltpu.VMEM((16, 256), bf16),
            pltpu.SemaphoreType.DMA((44,)),
        ],
        in_specs=[SM, SM] + [HBM] * 4,
        out_specs=[HBM],
        limit=60 * 1024 * 1024,
        args=(block_list, block_count, video_query, video_key, video_value, video_grad),
    )
    diag, packed = call(
        add_audio,
        [((4, 128, 256), bf16), ((8, PACK, 256), bf16)],
        10**6,
        scratch=[
            pltpu.VMEM((4, 128, 256), f32),
            pltpu.VMEM((128, 256), f32),
            pltpu.VMEM((128, 256), bf16),
            pltpu.SemaphoreType.DMA((8,)),
        ],
        in_specs=[VM, HBM],
        out_specs=[VM, HBM],
        aliases={1: 1},
        limit=60 * 1024 * 1024,
        args=(audio, packed),
    )
    near = video_query.reshape(1, 128, 256)
    packed, near = lax.optimization_barrier((packed, near))
    packed = lax.all_to_all(packed, ROWS, 0, 0, tiled=True)
    for distance in (4, 2):
        far = swap(near, "z", distance)
        (near,) = call(
            side_by_side, [((2 * near.shape[0], 128, 256), bf16)], 10**6, args=(near, far)
        )
    far = swap(near, "z", 1)
    (stats,) = call(
        back_stats,
        [((13, 256), f32)],
        10**9,
        scratch=[pltpu.VMEM((8, 128, 128), f32)] * 2,
        args=(packed, diag),
    )
    (sent,) = call(
        self_part,
        [((8, SENT, 256), bf16)],
        4 * 10**9,
        args=(near, far, packed, stats),
    )
    sent = backwards(sent)
    cross_own, sums = call(
        cross_part,
        [((128, 256), f32), ((2, 128, 128), f32)],
        4 * 10**9,
        scratch=[pltpu.VMEM((8, 128, 256), f32)],
        args=(packed, diag),
    )
    (terms,) = call(
        back_terms,
        [((64, 8, 128), f32)],
        10**9,
        scratch=[
            pltpu.VMEM((2, 128, 256), bf16),
            pltpu.VMEM((2, 128, 128), f32),
            pltpu.SemaphoreType.DMA((2,)),
        ],
        in_specs=[VM, VM, HBM, HBM],
        limit=48 * 1024 * 1024,
        args=(sent, packed, diag, sums),
    )
    terms = lax.all_to_all(terms, AUD + COLS, 0, 0, tiled=True)
    (video_out,) = call(join_video, [((128, 256), bf16)], 10**7, args=(cross_own, sent))
    (summed,) = call(add_terms, [((8, 64, 128), bf16)], 10**6, args=(terms,))
    final = backwards(summed)
    (final,) = call(again, [((8, 8, 64, 128), bf16)], 10**6, args=(final,))
    final = lax.all_to_all(final, ROWS, 0, 0, tiled=True)
    finished = call(lay_out, [((64, 2048), bf16)] * 4, 10**6, args=(final,))
    return (video_out, *finished)


def solution(mesh):
    fine = Mesh(mesh.devices.reshape(4, 2, 8, 4, 2), ("x", "yl", "z", "yh", "core"))
    video, audio = P(SEQ, AUD), P(AUD, None)
    return jax.shard_map(
        local,
        mesh=fine,
        in_specs=(
            video,
            video,
            video,
            audio,
            audio,
            audio,
            video,
            audio,
            P(SEQ, None),
            P(SEQ),
        ),
        out_specs=(video, audio, audio, audio, audio),
        check_vma=False,
    )
```

time: 166 us -> 147 us (0.89)
  waiting for transfers between devices: 55.1 us -> 35.1 us
  between operations: 14.8 us -> 1.44 us
  blocking collectives: 26.1 us -> 37.9 us
  starting transfers between devices: 38.7 us -> 43.5 us
    all_to_all x3, waiting for transfers between devices: 33.7 us -> 18.7 us  [the longest x1 12 us: local(): final = lax.all_to_all(final, ROWS, 0, 0, tiled=True)]
    all_to_all x1, waiting for transfers between devices: 0.01 us -> 10.6 us  [local(): packed = lax.all_to_all(packed, ROWS, 0, 0, tiled=True)]
    all_to_all x0 -> x1, blocking collectives: none -> 9.89 us  [backwards(): lax.all_to_all(value, 'z', 0, 0, axis_index_groups=[[7, 6, 5, 4, 3, 2, 1,...]
    all_gather x1 -> x0, waiting for transfers between devices: 8.83 us -> none  [local(): cols_query = lax.all_gather(twice, COLS)]
    all_to_all x3, starting transfers between devices: 15.8 us -> 23.8 us  [the longest x1 10.2 us: local(): audio = lax.all_to_all(audio, AUD, 0, 0, tiled=True)]
    ppermute x4 -> x3, waiting for transfers between devices: 11.8 us -> 5.75 us  [swap(): return lax.ppermute(value, axis, [(i, i ^ distance) for i in range(count)])]
    all_to_all x1, starting transfers between devices: 6.01 us -> 3.77 us  [local(): packed = lax.all_to_all(packed, ROWS, 0, 0, tiled=True)]
    all_to_all x1, blocking collectives: 26.1 us -> 28 us  [local(): terms = lax.all_to_all(terms, AUD + COLS, 0, 0, tiled=True)]
  transfers between devices with their start and end apart: 9 -> 7, of which waited for: 6 -> 6; matrix products, arithmetic and copies ran while one was open for 0% -> 0% of each run, Pallas kernels for 11% -> 8%
where the time goes in v2:
time: 147 us; the launch traced here: 145 us
  starting transfers between devices  43.5 us (30%)
  blocking collectives  37.9 us (26%)
  waiting for transfers between devices  35.1 us (24%)
  Pallas kernels  23.5 us (16%)
  local copies, waits for them, and re-layouts  3.71 us (3%)
    all_to_all x1, blocking collectives, local(): terms = lax.all_to_all(terms, AUD + COLS, 0, 0, tiled=True)  28 us
    pallas_call x13, Pallas kernels, call(): pl.pallas_call(kernel, out_shape=[jax.ShapeDtypeStruct(s, d) for s, d in...  23.5 us
    ppermute x3, starting transfers between devices, swap(): return lax.ppermute(value, axis, [(i, i ^ distance) for i in range(count)])  15.9 us
    all_to_all x1, waiting for transfers between devices, local(): final = lax.all_to_all(final, ROWS, 0, 0, tiled=True)  12 us
    all_to_all x1, waiting for transfers between devices, local(): packed = lax.all_to_all(packed, ROWS, 0, 0, tiled=True)  10.6 us
    all_to_all x1, starting transfers between devices, local(): audio = lax.all_to_all(audio, AUD, 0, 0, tiled=True)  10.2 us
    all_to_all x1, blocking collectives, backwards(): lax.all_to_all(value, 'z', 0, 0, axis_index_groups=[[7, 6, 5, 4, 3, 2, 1,...  9.89 us
    all_to_all x1, starting transfers between devices, backwards(): lax.all_to_all(value, 'z', 0, 0, axis_index_groups=[[7, 6, 5, 4, 3, 2, 1,...  9.76 us
  transfers between devices with their start and end apart: 7, of which 6 were waited for; matrix products, arithmetic and copies ran while one was open for 0% of the time, Pallas kernels for 8%

profile of v2, /device:TPU:1, one launch (start us, length us, event | category | flops | bytes accessed | tf_op | source)
XLA Modules:
  0.0 145.2 jit_solution(6446852716840005886)
XLA Ops:
  0.6 1.7 %shard_map.137 = bf16[8,32,256]{2,1,0:T(8,128)(2,1)} custom-call(bf16[64,2048]{1,0:T(8,128)(2,1)} %rest_0_.2, bf16[64,2048]{1,0:T(8,128)(2,1)} %rest_1_.2, bf16[64,2048]{1,0:T(8,128)(2,1)} %rest_2_.2, bf16[64,2048]{1,0:T(8,128)(2,1)} %rest_3_.2), custom_call_target="tpu_custom_call" | custom-call | flops 1000000 | bytes 4000000 | tf_op jit(solution)/shard_map/pallas_call | solution.py:42
  2.3 10.2 %all-to-all-start = ((bf16[8,32,256]{2,1,0:T(8,128)(2,1)}), bf16[8,32,256]{2,1,0:T(8,128)(2,1)S(1)}, u32[]{:S(2)}, u32[]{:S(2)}) async-start(bf16[8,32,256]{2,1,0:T(8,128)(2,1)} %shard_map.137), calls=%async_computation | async-start | bytes 262144 | tf_op jit(solution)/shard_map/all_to_all | solution.py:362
  13.1 3.2 %shard_map.138.given_ref = bf16[8,656,256]{2,1,0:T(8,128)(2,1)} custom-call(s32[1,3]{1,0:T(1,128)} %list_ref.1, s32[1]{0:T(128)S(6)} %copy.17.count_ref, bf16[128,256]{1,0:T(8,128)(2,1)} %rest_0_.3, bf16[128,256]{1,0:T(8,128)(2,1)} %rest_1_.3, bf16[128,256]{1,0:T(8,128)(2,1)} %rest_2_.3, bf16[128,256]{1,0:T(8,128)(2,1)} %rest_3_.3), custom_call_target="tpu_custom_call" | custom-call | flops 1000000 | bytes 4000000 | tf_op jit(solution)/shard_map/pallas_call | solution.py:42
  16.4 4.5 %all-to-all-done.audio_ref = bf16[8,32,256]{2,1,0:T(8,128)(2,1)S(1)} async-done(((bf16[8,32,256]{2,1,0:T(8,128)(2,1)}), bf16[8,32,256]{2,1,0:T(8,128)(2,1)S(1)}, u32[]{:S(2)}, u32[]{:S(2)}) %all-to-all-start) | async-done | bytes 131104 | tf_op jit(solution)/shard_map/all_to_all | solution.py:362
  20.8 0.7 copy-done.7
  21.5 2.5 %shard_map.139 = (bf16[4,128,256]{2,1,0:T(8,128)(2,1)}, bf16[8,656,256]{2,1,0:T(8,128)(2,1)}) custom-call(bf16[8,32,256]{2,1,0:T(8,128)(2,1)} %copy-done.7, bf16[8,656,256]{2,1,0:T(8,128)(2,1)} %shard_map.138.given_ref), custom_call_target="tpu_custom_call", output_to_operand_aliasing={{1}: (1, {})} | custom-call | flops 1000000 | bytes 4000000 | tf_op jit(solution)/shard_map/pallas_call | solution.py:42
  24.0 0.0 copy-start.2
  24.0 3.8 %all-to-all-start.1 = ((bf16[8,656,256]{2,1,0:T(8,128)(2,1)}), bf16[8,656,256]{2,1,0:T(8,128)(2,1)S(1)}, u32[]{:S(2)}, u32[]{:S(2)}) async-start(bf16[8,656,256]{2,1,0:T(8,128)(2,1)} %get-tuple-element.16), calls=%async_computation.1 | async-start | bytes 5373952 | tf_op jit(solution)/shard_map/all_to_all | solution.py:395
  27.8 9.3 %collective-permute-start = (bf16[1,128,256]{2,1,0:T(8,128)(2,1)S(1)}, bf16[1,128,256]{2,1,0:T(8,128)(2,1)S(1)}, u32[]{:S(2)}, u32[]{:S(2)}) collective-permute-start(bf16[1,128,256]{2,1,0:T(8,128)(2,1)S(1)} %bitcast.1), channel_id=1, source_target_pairs={{0,32},{8,40},{16,48},{24,56},{32,0},{40,8},{48,16},{56,24},{1,33}... | collective-permute-start | bytes 196616 | tf_op jit(solution)/shard_map/ppermute | solution.py:329
  37.1 1.7 %collective-permute-done.second_ref = bf16[1,128,256]{2,1,0:T(8,128)(2,1)S(1)} collective-permute-done((bf16[1,128,256]{2,1,0:T(8,128)(2,1)S(1)}, bf16[1,128,256]{2,1,0:T(8,128)(2,1)S(1)}, u32[]{:S(2)}, u32[]{:S(2)}) %collective-permute-start) | collective-permute-done | bytes 65568 | tf_op jit(solution)/shard_map/ppermute | solution.py:329
  38.8 4.7 %collective-permute-start.1 = (bf16[2,128,256]{2,1,0:T(8,128)(2,1)S(1)}, bf16[2,128,256]{2,1,0:T(8,128)(2,1)S(1)}, u32[]{:S(2)}, u32[]{:S(2)}) collective-permute-start(bf16[2,128,256]{2,1,0:T(8,128)(2,1)S(1)} %shard_map.141.first_ref), channel_id=1, source_target_pairs={{0,16},{8,24},{16,0},{24,8},{32,48},{40,56},{48,32},{56,40},{1,17}... | collective-permute-start | bytes 393224 | tf_op jit(solution)/shard_map/ppermute | solution.py:329
  43.6 4.0 %collective-permute-done.1.second_ref = bf16[2,128,256]{2,1,0:T(8,128)(2,1)S(1)} collective-permute-done((bf16[2,128,256]{2,1,0:T(8,128)(2,1)S(1)}, bf16[2,128,256]{2,1,0:T(8,128)(2,1)S(1)}, u32[]{:S(2)}, u32[]{:S(2)}) %collective-permute-start.1) | collective-permute-done | bytes 131104 | tf_op jit(solution)/shard_map/ppermute | solution.py:329
  47.6 1.9 %collective-permute-start.2 = (bf16[4,128,256]{2,1,0:T(8,128)(2,1)S(1)}, bf16[4,128,256]{2,1,0:T(8,128)(2,1)S(1)}, u32[]{:S(2)}, u32[]{:S(2)}) collective-permute-start(bf16[4,128,256]{2,1,0:T(8,128)(2,1)S(1)} %shard_map.142.near_ref), channel_id=1, source_target_pairs={{0,8},{8,0},{16,24},{24,16},{32,40},{40,32},{48,56},{56,48},{1,9},... | collective-permute-start | bytes 786440 | tf_op jit(solution)/shard_map/ppermute | solution.py:329
  49.5 10.6 %all-to-all-done.1.packed_ref = bf16[8,656,256]{2,1,0:T(8,128)(2,1)S(1)} async-done(((bf16[8,656,256]{2,1,0:T(8,128)(2,1)}), bf16[8,656,256]{2,1,0:T(8,128)(2,1)S(1)}, u32[]{:S(2)}, u32[]{:S(2)}) %all-to-all-start.1) | async-done | bytes 2687008 | tf_op jit(solution)/shard_map/all_to_all | solution.py:395
  60.2 0.6 shard_map.143.stats_ref
  60.8 3.4 %shard_map.144 = bf16[8,144,256]{2,1,0:T(8,128)(2,1)S(1)} custom-call(bf16[4,128,256]{2,1,0:T(8,128)(2,1)S(1)} %shard_map.142.near_ref, bf16[4,128,256]{2,1,0:T(8,128)(2,1)S(1)} %collective-permute-done.2.far_ref, bf16[8,656,256]{2,1,0:T(8,128)(2,1)S(1)} %all-to-all-done.1.packed_ref, f32[13,256]{1,0:T(8,128)S(1)} %shard_map.143.stats_ref), custom_call_target="tpu_custom_call" | custom-call | flops 4000000000 | bytes 4000000 | tf_op jit(solution)/shard_map/pallas_call | solution.py:42
  64.3 0.8 copy-done
  65.1 9.8 %all-to-all-start.2 = ((bf16[8,144,256]{2,1,0:T(8,128)(2,1)}), bf16[8,144,256]{2,1,0:T(8,128)(2,1)S(1)}, u32[]{:S(2)}, u32[]{:S(2)}) async-start(bf16[8,144,256]{2,1,0:T(8,128)(2,1)} %copy-done), calls=%async_computation.2 | async-start | bytes 1179648 | tf_op jit(solution)/shard_map/all_to_all | solution.py:333
  74.9 6.4 %shard_map.140 = (f32[128,256]{1,0:T(8,128)S(1)}, f32[2,128,128]{2,1,0:T(8,128)S(1)}) custom-call(bf16[8,656,256]{2,1,0:T(8,128)(2,1)S(1)} %all-to-all-done.1.packed_ref, bf16[4,128,256]{2,1,0:T(8,128)(2,1)S(1)} %copy-done.2), custom_call_target="tpu_custom_call" | custom-call | flops 4000000000 | bytes 4000000 | tf_op jit(solution)/shard_map/pallas_call | solution.py:42
  81.3 0.6 copy-done.3
  81.9 0.7 copy-done.5
  82.6 2.3 %all-to-all-done.2.sent_ref = bf16[8,144,256]{2,1,0:T(8,128)(2,1)S(1)} async-done(((bf16[8,144,256]{2,1,0:T(8,128)(2,1)}), bf16[8,144,256]{2,1,0:T(8,128)(2,1)S(1)}, u32[]{:S(2)}, u32[]{:S(2)}) %all-to-all-start.2) | async-done | bytes 589856 | tf_op jit(solution)/shard_map/all_to_all | solution.py:333
  84.9 0.9 copy-done.4
  85.8 2.3 %shard_map.146 = f32[64,8,128]{2,1,0:T(8,128)S(1)} custom-call(bf16[8,144,256]{2,1,0:T(8,128)(2,1)S(1)} %all-to-all-done.2.sent_ref, bf16[8,656,256]{2,1,0:T(8,128)(2,1)S(1)} %all-to-all-done.1.packed_ref, bf16[4,128,256]{2,1,0:T(8,128)(2,1)S(1)} %copy-done.2, f32[2,128,128]{2,1,0:T(8,128)S(1)} %copy-done.4), custom_call_target="tpu_custom_call" | custom-call | flops 1000000000 | bytes 4000000 | tf_op jit(solution)/shard_map/pallas_call | solution.py:42
  88.1 0.0 copy-start.6
  88.1 28.0 %all_to_all.30.terms_ref = f32[64,8,128]{2,1,0:T(8,128)S(1)} all-to-all(f32[64,8,128]{2,1,0:T(8,128)S(1)} %shard_map.146), channel_id=1, replica_groups=mesh['x'=4,'yl'=2,'z'=8,'yh'=4,'core'=2] {'yh','core','z'}, dimensions={0} | all-to-all | bytes 524288 | tf_op jit(solution)/shard_map/all_to_all | solution.py:436
  116.2 9.9 %all_to_all.31.ref = bf16[8,64,128]{2,1,0:T(8,128)(2,1)S(1)} all-to-all(bf16[8,64,128]{2,1,0:T(8,128)(2,1)S(1)} %shard_map.147), channel_id=1, replica_groups={{56,48,40,32,24,16,8,0},{57,49,41,33,25,17,9,1},{58,50,42,34,26,18,10,2..., dimensions={0} | all-to-all | bytes 262144 | tf_op jit(solution)/shard_map/all_to_all | solution.py:333
  126.1 1.1 shard_map.148
  127.2 3.9 %all-to-all-start.5 = ((bf16[8,8,64,128]{3,2,1,0:T(8,128)(2,1)}), bf16[8,8,64,128]{3,2,1,0:T(8,128)(2,1)S(1)}, u32[]{:S(2)}, u32[]{:S(2)}) async-start(bf16[8,8,64,128]{3,2,1,0:T(8,128)(2,1)} %shard_map.148), calls=%async_computation.5 | async-start | bytes 2097152 | tf_op jit(solution)/shard_map/all_to_all | solution.py:441
  131.1 1.0 shard_map.145
  132.1 12.0 %all-to-all-done.5.final_ref = bf16[8,8,64,128]{3,2,1,0:T(8,128)(2,1)S(1)} async-done(((bf16[8,8,64,128]{3,2,1,0:T(8,128)(2,1)}), bf16[8,8,64,128]{3,2,1,0:T(8,128)(2,1)S(1)}, u32[]{:S(2)}, u32[]{:S(2)}) %all-to-all-start.5) | async-done | bytes 1048608 | tf_op jit(solution)/shard_map/all_to_all | solution.py:441
  144.1 1.1 shard_map.149
  (13 shorter events, 0.1 us)
Async XLA Ops:
  2.3 18.5 %all-to-all-start = ((bf16[8,32,256]{2,1,0:T(8,128)(2,1)}), bf16[8,32,256]{2,1,0:T(8,128)(2,1)S(1)}, u32[]{:S(2)}, u32[]{:S(2)}) async-start(bf16[8,32,256]{2,1,0:T(8,128)(2,1)} %shard_map.137), calls=%async_computation | async-start | bytes 262144 | tf_op jit(solution)/shard_map/all_to_all | solution.py:362
  20.8 0.7 copy-start.7
  24.0 3.8 %copy-start.1 = (bf16[128,256]{1,0:T(8,128)(2,1)S(1)}, bf16[128,256]{1,0:T(8,128)(2,1)}, u32[]{:S(2)}) copy-start(bf16[128,256]{1,0:T(8,128)(2,1)} %rest_0_.3) | copy-start | bytes 196612
  24.0 36.2 %copy-start.2 = (bf16[4,128,256]{2,1,0:T(8,128)(2,1)S(1)}, bf16[4,128,256]{2,1,0:T(8,128)(2,1)}, u32[]{:S(2)}) copy-start(bf16[4,128,256]{2,1,0:T(8,128)(2,1)} %get-tuple-element.17.diag_ref.diag_far_ref) | copy-start | bytes 786436
  24.0 36.2 %all-to-all-start.1 = ((bf16[8,656,256]{2,1,0:T(8,128)(2,1)}), bf16[8,656,256]{2,1,0:T(8,128)(2,1)S(1)}, u32[]{:S(2)}, u32[]{:S(2)}) async-start(bf16[8,656,256]{2,1,0:T(8,128)(2,1)} %get-tuple-element.16), calls=%async_computation.1 | async-start | bytes 5373952 | tf_op jit(solution)/shard_map/all_to_all | solution.py:395
  27.8 11.0 %collective-permute-start = (bf16[1,128,256]{2,1,0:T(8,128)(2,1)S(1)}, bf16[1,128,256]{2,1,0:T(8,128)(2,1)S(1)}, u32[]{:S(2)}, u32[]{:S(2)}) collective-permute-start(bf16[1,128,256]{2,1,0:T(8,128)(2,1)S(1)} %bitcast.1), channel_id=1, source_target_pairs={{0,32},{8,40},{16,48},{24,56},{32,0},{40,8},{48,16},{56,24},{1,33}... | collective-permute-start | bytes 196616 | tf_op jit(solution)/shard_map/ppermute | solution.py:329
  38.8 8.8 %collective-permute-start.1 = (bf16[2,128,256]{2,1,0:T(8,128)(2,1)S(1)}, bf16[2,128,256]{2,1,0:T(8,128)(2,1)S(1)}, u32[]{:S(2)}, u32[]{:S(2)}) collective-permute-start(bf16[2,128,256]{2,1,0:T(8,128)(2,1)S(1)} %shard_map.141.first_ref), channel_id=1, source_target_pairs={{0,16},{8,24},{16,0},{24,8},{32,48},{40,56},{48,32},{56,40},{1,17}... | collective-permute-start | bytes 393224 | tf_op jit(solution)/shard_map/ppermute | solution.py:329
  47.6 13.2 %collective-permute-start.2 = (bf16[4,128,256]{2,1,0:T(8,128)(2,1)S(1)}, bf16[4,128,256]{2,1,0:T(8,128)(2,1)S(1)}, u32[]{:S(2)}, u32[]{:S(2)}) collective-permute-start(bf16[4,128,256]{2,1,0:T(8,128)(2,1)S(1)} %shard_map.142.near_ref), channel_id=1, source_target_pairs={{0,8},{8,0},{16,24},{24,16},{32,40},{40,32},{48,56},{56,48},{1,9},... | collective-permute-start | bytes 786440 | tf_op jit(solution)/shard_map/ppermute | solution.py:329
  64.3 0.8 copy-start
  65.1 19.8 %all-to-all-start.2 = ((bf16[8,144,256]{2,1,0:T(8,128)(2,1)}), bf16[8,144,256]{2,1,0:T(8,128)(2,1)S(1)}, u32[]{:S(2)}, u32[]{:S(2)}) async-start(bf16[8,144,256]{2,1,0:T(8,128)(2,1)} %copy-done), calls=%async_computation.2 | async-start | bytes 1179648 | tf_op jit(solution)/shard_map/all_to_all | solution.py:333
  81.2 0.7 copy-start.3
  81.9 0.7 copy-start.5
  84.9 0.9 copy-start.4
  88.1 43.0 %copy-start.6 = (f32[128,256]{1,0:T(8,128)S(1)}, f32[128,256]{1,0:T(8,128)}, u32[]{:S(2)}) copy-start(f32[128,256]{1,0:T(8,128)} %copy-done.5) | copy-start | bytes 393220
  127.2 16.9 %all-to-all-start.5 = ((bf16[8,8,64,128]{3,2,1,0:T(8,128)(2,1)}), bf16[8,8,64,128]{3,2,1,0:T(8,128)(2,1)S(1)}, u32[]{:S(2)}, u32[]{:S(2)}) async-start(bf16[8,8,64,128]{3,2,1,0:T(8,128)(2,1)} %shard_map.148), calls=%async_computation.5 | async-start | bytes 2097152 | tf_op jit(solution)/shard_map/all_to_all | solution.py:441

commit v3 on v2

--- a/solution.py
+++ b/solution.py
@@ -87,13 +87,13 @@
     stores = []
     for dest in range(8):
         stores.append(
-            pltpu.make_async_copy(marks, out_ref.at[dest, 512:528], sems.at[4 + len(stores)])
+            pltpu.make_async_copy(marks, out_ref.at[dest, 32], sems.at[4 + len(stores)])
         )
         stores[-1].start()
     for place, load in enumerate(loads):
         load.wait()
         for dest in range(8):
-            target = out_ref.at[dest, place * 128 : place * 128 + 128]
+            target = out_ref.at[dest, place * 8 : place * 8 + 8]
             stores.append(
                 pltpu.make_async_copy(held.at[place], target, sems.at[4 + len(stores)])
             )
@@ -122,15 +122,9 @@
         out_ref[dest] = parts[:, dest * 256 : dest * 256 + 256]
 
 
-def add_audio(audio_ref, given_ref, diag_ref, out_ref, wide_ref, flat_ref, flat16_ref, sems):
-    for source in range(8):
-        part = audio_ref[source].astype(f32)
-        for place in (2, 3):
-            row = source * 8 + (place - 2) * 64
-            flat_ref[row : row + 8, :] = part[place * 8 : place * 8 + 8, :]
-    flat16_ref[...] = flat_ref[...].astype(bf16)
+def add_audio(audio_ref, given_ref, diag_ref, out_ref, wide_ref, sems):
     stores = [
-        pltpu.make_async_copy(flat16_ref, out_ref.at[dest, 528:656], sems.at[dest])
+        pltpu.make_async_copy(audio_ref.at[:, 16:32], out_ref.at[dest, 33:41], sems.at[dest])
         for dest in range(8)
     ]
     for store in stores:
@@ -208,6 +202,9 @@
     packed_ref, diag_ref, own_ref, sums_ref, out_ref
 ):
     diag_key, diag_value = diag_ref[2], diag_ref[3]
+    audio = packed_ref[:, 528:656, :].astype(f32).reshape(8, 8, 16, 256)
+    all_keys = audio[:, :, 0:8, :].reshape(512, 256).astype(bf16)
+    all_values = audio[:, :, 8:16, :].reshape(512, 256).astype(bf16)
     key_terms = jnp.zeros((128, 256), f32)
     value_terms = jnp.zeros((128, 256), f32)
     for r in range(8):
@@ -216,16 +213,14 @@
         stats = []
         for h in range(2):
             lanes = slice(h * 128, h * 128 + 128)
-            keys = packed_ref[:, 528:592, lanes].reshape(512, 128)
-            values = packed_ref[:, 592:656, lanes].reshape(512, 128)
-            scores = dot_t(queries2[:, lanes], keys) * SCALE
+            scores = dot_t(queries2[:, lanes], all_keys[:, lanes]) * SCALE
             parts = [scores[:, b * 128 : b * 128 + 128] for b in range(4)]
             peak = jnp.where(allowed, functools.reduce(jnp.maximum, parts), -jnp.inf)
             best = jnp.max(peak, axis=1, keepdims=True)
             weights = [jnp.where(allowed, jnp.exp(p - best), 0.0) for p in parts]
             total = jnp.sum(sum(weights), axis=1, keepdims=True)
             weights = jnp.concatenate([w.astype(bf16) for w in weights], 1)
-            out = dot_n(weights, values) / total
+            out = dot_n(weights, all_values[:, lanes]) / total
             out_ref[r, :, lanes] = out
             delta = jnp.sum(upstream2[:, lanes].astype(f32) * out, axis=1, keepdims=True)
             stats.append((best, total, delta))
@@ -277,14 +272,14 @@
         lanes = slice(h * 128, h * 128 + 128)
         for a in range(8):
             rows = slice(h * 64 + a * 8, h * 64 + a * 8 + 8)
-            out_ref[a * 8 + h] = attn[rows, lanes]
-            out_ref[a * 8 + 2 + h] = grads[rows, lanes]
-            out_ref[a * 8 + 4 + h] = sums_ref[0, rows, :]
-            out_ref[a * 8 + 6 + h] = sums_ref[1, rows, :]
+            out_ref[63 - (a * 8 + h)] = attn[rows, lanes]
+            out_ref[63 - (a * 8 + 2 + h)] = grads[rows, lanes]
+            out_ref[63 - (a * 8 + 4 + h)] = sums_ref[0, rows, :]
+            out_ref[63 - (a * 8 + 6 + h)] = sums_ref[1, rows, :]
 
 
 def add_terms(terms_ref, out_ref):
-    sums = [sum(terms_ref[a * 8 + c] for c in range(8)) for a in range(8)]
+    sums = [sum(terms_ref[(7 - a) * 8 + c] for c in range(8)) for a in range(8)]
     sums = jnp.concatenate(sums, 0).astype(bf16)
     for dest in range(8):
         out_ref[dest] = sums
@@ -329,10 +324,9 @@
     return lax.ppermute(value, axis, [(i, i ^ distance) for i in range(count)])
 
 
-def backwards(value):
-    return lax.all_to_all(
-        value, "z", 0, 0, axis_index_groups=[[7, 6, 5, 4, 3, 2, 1, 0]], tiled=True
-    )
+def backwards(value, axes):
+    order = list(range(value.shape[0]))[::-1]
+    return lax.all_to_all(value, axes, 0, 0, axis_index_groups=[order], tiled=True)
 
 
 def local(
@@ -362,28 +356,30 @@
     audio = lax.all_to_all(audio, AUD, 0, 0, tiled=True)
     (packed,) = call(
         pack_video,
-        [((8, PACK, 256), bf16)],
+        [((8, PACK // 16, 16, 256), bf16)],
         10**6,
         scratch=[
-            pltpu.VMEM((4, 128, 256), bf16),
+            pltpu.VMEM((4, 8, 16, 256), bf16),
             pltpu.VMEM((16, 256), bf16),
             pltpu.SemaphoreType.DMA((44,)),
         ],
         in_specs=[SM, SM] + [HBM] * 4,
         out_specs=[HBM],
         limit=60 * 1024 * 1024,
-        args=(block_list, block_count, video_query, video_key, video_value, video_grad),
+        args=(
+            block_list,
+            block_count,
+            *(
+                matrix.reshape(8, 16, 256)
+                for matrix in (video_query, video_key, video_value, video_grad)
+            ),
+        ),
     )
     diag, packed = call(
         add_audio,
-        [((4, 128, 256), bf16), ((8, PACK, 256), bf16)],
+        [((4, 128, 256), bf16), ((8, PACK // 16, 16, 256), bf16)],
         10**6,
-        scratch=[
-            pltpu.VMEM((4, 128, 256), f32),
-            pltpu.VMEM((128, 256), f32),
-            pltpu.VMEM((128, 256), bf16),
-            pltpu.SemaphoreType.DMA((8,)),
-        ],
+        scratch=[pltpu.VMEM((4, 128, 256), f32), pltpu.SemaphoreType.DMA((8,))],
         in_specs=[VM, HBM],
         out_specs=[VM, HBM],
         aliases={1: 1},
@@ -392,7 +388,7 @@
     )
     near = video_query.reshape(1, 128, 256)
     packed, near = lax.optimization_barrier((packed, near))
-    packed = lax.all_to_all(packed, ROWS, 0, 0, tiled=True)
+    packed = lax.all_to_all(packed, ROWS, 0, 0, tiled=True).reshape(8, PACK, 256)
     for distance in (4, 2):
         far = swap(near, "z", distance)
         (near,) = call(
@@ -412,7 +408,7 @@
         4 * 10**9,
         args=(near, far, packed, stats),
     )
-    sent = backwards(sent)
+    sent = backwards(sent, COLS)
     cross_own, sums = call(
         cross_part,
         [((128, 256), f32), ((2, 128, 128), f32)],
@@ -433,10 +429,10 @@
         limit=48 * 1024 * 1024,
         args=(sent, packed, diag, sums),
     )
-    terms = lax.all_to_all(terms, AUD + COLS, 0, 0, tiled=True)
+    terms = backwards(terms, AUD + COLS)
     (video_out,) = call(join_video, [((128, 256), bf16)], 10**7, args=(cross_own, sent))
     (summed,) = call(add_terms, [((8, 64, 128), bf16)], 10**6, args=(terms,))
-    final = backwards(summed)
+    final = backwards(summed, COLS)
     (final,) = call(again, [((8, 8, 64, 128), bf16)], 10**6, args=(final,))
     final = lax.all_to_all(final, ROWS, 0, 0, tiled=True)
     finished = call(lay_out, [((64, 2048), bf16)] * 4, 10**6, args=(final,))

time: 147 us -> 146 us (level)
  no operation moved by 1% of the time
where the time goes in v3:
time: 146 us; the launch traced here: 145 us
  starting transfers between devices  43.2 us (30%)
  blocking collectives  36.6 us (25%)
  waiting for transfers between devices  36.1 us (25%)
  Pallas kernels  23.5 us (16%)
  local copies, waits for them, and re-layouts  3.71 us (3%)
    all_to_all x2, blocking collectives, backwards(): lax.all_to_all(value, axes, 0, 0, axis_index_groups=[order], tiled=True)  36.6 us
    pallas_call x13, Pallas kernels, call(): pl.pallas_call(kernel, out_shape=[jax.ShapeDtypeStruct(s, d) for s, d in...  23.5 us
    ppermute x3, starting transfers between devices, swap(): return lax.ppermute(value, axis, [(i, i ^ distance) for i in range(count)])  15.9 us
    all_to_all x1, waiting for transfers between devices, local(): final = lax.all_to_all(final, ROWS, 0, 0, tiled=True)  12.9 us
    all_to_all x1, waiting for transfers between devices, local(): lax.all_to_all(packed, ROWS, 0, 0, tiled=True).reshape(8, PACK, 256)  10.6 us
    all_to_all x1, starting transfers between devices, local(): audio = lax.all_to_all(audio, AUD, 0, 0, tiled=True)  10.2 us
    all_to_all x1, starting transfers between devices, backwards(): lax.all_to_all(value, axes, 0, 0, axis_index_groups=[order], tiled=True)  9.75 us
    ppermute x3, waiting for transfers between devices, swap(): return lax.ppermute(value, axis, [(i, i ^ distance) for i in range(count)])  5.75 us
  transfers between devices with their start and end apart: 7, of which 6 were waited for; matrix products, arithmetic and copies ran while one was open for 0% of the time, Pallas kernels for 8%

profile of v3, /device:TPU:1, one launch (start us, length us, event | category | flops | bytes accessed | tf_op | source)
XLA Modules:
  0.0 144.5 jit_solution(1718220456837642549)
XLA Ops:
  0.6 1.7 %shard_map.137 = bf16[8,32,256]{2,1,0:T(8,128)(2,1)} custom-call(bf16[64,2048]{1,0:T(8,128)(2,1)} %rest_0_.1, bf16[64,2048]{1,0:T(8,128)(2,1)} %rest_1_.1, bf16[64,2048]{1,0:T(8,128)(2,1)} %rest_2_.1, bf16[64,2048]{1,0:T(8,128)(2,1)} %rest_3_.1), custom_call_target="tpu_custom_call" | custom-call | flops 1000000 | bytes 4000000 | tf_op jit(solution)/shard_map/pallas_call | solution.py:42
  2.3 10.2 %all-to-all-start = ((bf16[8,32,256]{2,1,0:T(8,128)(2,1)}), bf16[8,32,256]{2,1,0:T(8,128)(2,1)S(1)}, u32[]{:S(2)}, u32[]{:S(2)}) async-start(bf16[8,32,256]{2,1,0:T(8,128)(2,1)} %shard_map.137), calls=%async_computation | async-start | bytes 262144 | tf_op jit(solution)/shard_map/all_to_all | solution.py:356
  13.1 3.2 %shard_map.138.given_ref = bf16[8,41,16,256]{3,2,1,0:T(8,128)(2,1)} custom-call(s32[1,3]{1,0:T(1,128)} %list_ref.1, s32[1]{0:T(128)S(6)} %copy.17.count_ref, bf16[8,16,256]{2,1,0:T(8,128)(2,1)} %bitcast.10, bf16[8,16,256]{2,1,0:T(8,128)(2,1)} %bitcast.13, bf16[8,16,256]{2,1,0:T(8,128)(2,1)} %bitcast.14, bf16[8,16,256]{2,1,0:T(8,128)(2,1)} %bitcast.15), custom_call_target="tpu_custom_call" | custom-call | flops 1000000 | bytes 4000000 | tf_op jit(solution)/shard_map/pallas_call | solution.py:42
  16.4 4.5 %all-to-all-done.audio_ref = bf16[8,32,256]{2,1,0:T(8,128)(2,1)S(1)} async-done(((bf16[8,32,256]{2,1,0:T(8,128)(2,1)}), bf16[8,32,256]{2,1,0:T(8,128)(2,1)S(1)}, u32[]{:S(2)}, u32[]{:S(2)}) %all-to-all-start) | async-done | bytes 131104 | tf_op jit(solution)/shard_map/all_to_all | solution.py:356
  20.8 0.7 copy-done.7
  21.5 2.5 %shard_map.139 = (bf16[4,128,256]{2,1,0:T(8,128)(2,1)}, bf16[8,41,16,256]{3,2,1,0:T(8,128)(2,1)}) custom-call(bf16[8,32,256]{2,1,0:T(8,128)(2,1)} %copy-done.7, bf16[8,41,16,256]{3,2,1,0:T(8,128)(2,1)} %shard_map.138.given_ref), custom_call_target="tpu_custom_call", output_to_operand_aliasing={{1}: (1, {})} | custom-call | flops 1000000 | bytes 4000000 | tf_op jit(solution)/shard_map/pallas_call | solution.py:42
  24.0 0.0 copy-start.2
  24.0 3.8 %all-to-all-start.1 = ((bf16[8,41,16,256]{3,2,1,0:T(8,128)(2,1)}), bf16[8,41,16,256]{3,2,1,0:T(8,128)(2,1)S(1)}, u32[]{:S(2)}, u32[]{:S(2)}) async-start(bf16[8,41,16,256]{3,2,1,0:T(8,128)(2,1)} %get-tuple-element.16), calls=%async_computation.1 | async-start | bytes 5373952 | tf_op jit(solution)/shard_map/all_to_all | solution.py:391
  27.8 9.3 %collective-permute-start = (bf16[1,128,256]{2,1,0:T(8,128)(2,1)S(1)}, bf16[1,128,256]{2,1,0:T(8,128)(2,1)S(1)}, u32[]{:S(2)}, u32[]{:S(2)}) collective-permute-start(bf16[1,128,256]{2,1,0:T(8,128)(2,1)S(1)} %bitcast.11), channel_id=1, source_target_pairs={{0,32},{8,40},{16,48},{24,56},{32,0},{40,8},{48,16},{56,24},{1,33}... | collective-permute-start | bytes 196616 | tf_op jit(solution)/shard_map/ppermute | solution.py:324
  37.1 1.7 %collective-permute-done.second_ref = bf16[1,128,256]{2,1,0:T(8,128)(2,1)S(1)} collective-permute-done((bf16[1,128,256]{2,1,0:T(8,128)(2,1)S(1)}, bf16[1,128,256]{2,1,0:T(8,128)(2,1)S(1)}, u32[]{:S(2)}, u32[]{:S(2)}) %collective-permute-start) | collective-permute-done | bytes 65568 | tf_op jit(solution)/shard_map/ppermute | solution.py:324
  38.8 4.7 %collective-permute-start.1 = (bf16[2,128,256]{2,1,0:T(8,128)(2,1)S(1)}, bf16[2,128,256]{2,1,0:T(8,128)(2,1)S(1)}, u32[]{:S(2)}, u32[]{:S(2)}) collective-permute-start(bf16[2,128,256]{2,1,0:T(8,128)(2,1)S(1)} %shard_map.141.first_ref), channel_id=1, source_target_pairs={{0,16},{8,24},{16,0},{24,8},{32,48},{40,56},{48,32},{56,40},{1,17}... | collective-permute-start | bytes 393224 | tf_op jit(solution)/shard_map/ppermute | solution.py:324
  43.5 4.0 %collective-permute-done.1.second_ref = bf16[2,128,256]{2,1,0:T(8,128)(2,1)S(1)} collective-permute-done((bf16[2,128,256]{2,1,0:T(8,128)(2,1)S(1)}, bf16[2,128,256]{2,1,0:T(8,128)(2,1)S(1)}, u32[]{:S(2)}, u32[]{:S(2)}) %collective-permute-start.1) | collective-permute-done | bytes 131104 | tf_op jit(solution)/shard_map/ppermute | solution.py:324
  47.6 1.9 %collective-permute-start.2 = (bf16[4,128,256]{2,1,0:T(8,128)(2,1)S(1)}, bf16[4,128,256]{2,1,0:T(8,128)(2,1)S(1)}, u32[]{:S(2)}, u32[]{:S(2)}) collective-permute-start(bf16[4,128,256]{2,1,0:T(8,128)(2,1)S(1)} %shard_map.142.near_ref), channel_id=1, source_target_pairs={{0,8},{8,0},{16,24},{24,16},{32,40},{40,32},{48,56},{56,48},{1,9},... | collective-permute-start | bytes 786440 | tf_op jit(solution)/shard_map/ppermute | solution.py:324
  49.5 10.6 %all-to-all-done.1 = bf16[8,41,16,256]{3,2,1,0:T(8,128)(2,1)S(1)} async-done(((bf16[8,41,16,256]{3,2,1,0:T(8,128)(2,1)}), bf16[8,41,16,256]{3,2,1,0:T(8,128)(2,1)S(1)}, u32[]{:S(2)}, u32[]{:S(2)}) %all-to-all-start.1) | async-done | bytes 2687008 | tf_op jit(solution)/shard_map/all_to_all | solution.py:391
  60.2 0.6 shard_map.143.stats_ref
  60.8 3.4 %shard_map.144 = bf16[8,144,256]{2,1,0:T(8,128)(2,1)S(1)} custom-call(bf16[4,128,256]{2,1,0:T(8,128)(2,1)S(1)} %shard_map.142.near_ref, bf16[4,128,256]{2,1,0:T(8,128)(2,1)S(1)} %collective-permute-done.2.far_ref, bf16[8,656,256]{2,1,0:T(8,128)(2,1)S(1)} %bitcast.7, f32[13,256]{1,0:T(8,128)S(1)} %shard_map.143.stats_ref), custom_call_target="tpu_custom_call" | custom-call | flops 4000000000 | bytes 4000000 | tf_op jit(solution)/shard_map/pallas_call | solution.py:42
  64.3 0.8 copy-done
  65.1 9.8 %all-to-all-start.2 = ((bf16[8,144,256]{2,1,0:T(8,128)(2,1)}), bf16[8,144,256]{2,1,0:T(8,128)(2,1)S(1)}, u32[]{:S(2)}, u32[]{:S(2)}) async-start(bf16[8,144,256]{2,1,0:T(8,128)(2,1)} %copy-done), calls=%async_computation.2 | async-start | bytes 1179648 | tf_op jit(solution)/shard_map/all_to_all | solution.py:329
  74.8 6.4 %shard_map.140 = (f32[128,256]{1,0:T(8,128)S(1)}, f32[2,128,128]{2,1,0:T(8,128)S(1)}) custom-call(bf16[8,656,256]{2,1,0:T(8,128)(2,1)S(1)} %bitcast.8, bf16[4,128,256]{2,1,0:T(8,128)(2,1)S(1)} %copy-done.2), custom_call_target="tpu_custom_call" | custom-call | flops 4000000000 | bytes 4000000 | tf_op jit(solution)/shard_map/pallas_call | solution.py:42
  81.2 0.0 copy-start.3
  81.2 0.6 copy-done.3
  81.9 0.7 copy-done.5
  82.5 2.3 %all-to-all-done.2.sent_ref = bf16[8,144,256]{2,1,0:T(8,128)(2,1)S(1)} async-done(((bf16[8,144,256]{2,1,0:T(8,128)(2,1)}), bf16[8,144,256]{2,1,0:T(8,128)(2,1)S(1)}, u32[]{:S(2)}, u32[]{:S(2)}) %all-to-all-start.2) | async-done | bytes 589856 | tf_op jit(solution)/shard_map/all_to_all | solution.py:329
  84.9 0.9 copy-done.4
  85.8 2.3 %shard_map.146 = f32[64,8,128]{2,1,0:T(8,128)S(1)} custom-call(bf16[8,144,256]{2,1,0:T(8,128)(2,1)S(1)} %all-to-all-done.2.sent_ref, bf16[8,656,256]{2,1,0:T(8,128)(2,1)S(1)} %bitcast.9, bf16[4,128,256]{2,1,0:T(8,128)(2,1)S(1)} %copy-done.2, f32[2,128,128]{2,1,0:T(8,128)S(1)} %copy-done.4), custom_call_target="tpu_custom_call" | custom-call | flops 1000000000 | bytes 4000000 | tf_op jit(solution)/shard_map/pallas_call | solution.py:42
  88.1 26.4 %all_to_all.30.terms_ref = f32[64,8,128]{2,1,0:T(8,128)S(1)} all-to-all(f32[64,8,128]{2,1,0:T(8,128)S(1)} %shard_map.146), channel_id=1, replica_groups={{63,55,47,39,31,23,15,7,62,54,46,38,30,22,14,6,61,53,45,37,29,21,13,5,6..., dimensions={0} | all-to-all | bytes 524288 | tf_op jit(solution)/shard_map/all_to_all | solution.py:329
  114.5 10.2 %all_to_all.31.ref = bf16[8,64,128]{2,1,0:T(8,128)(2,1)S(1)} all-to-all(bf16[8,64,128]{2,1,0:T(8,128)(2,1)S(1)} %shard_map.147), channel_id=1, replica_groups={{56,48,40,32,24,16,8,0},{57,49,41,33,25,17,9,1},{58,50,42,34,26,18,10,2..., dimensions={0} | all-to-all | bytes 262144 | tf_op jit(solution)/shard_map/all_to_all | solution.py:329
  124.7 1.1 shard_map.148
  125.8 3.6 %all-to-all-start.5 = ((bf16[8,8,64,128]{3,2,1,0:T(8,128)(2,1)}), bf16[8,8,64,128]{3,2,1,0:T(8,128)(2,1)S(1)}, u32[]{:S(2)}, u32[]{:S(2)}) async-start(bf16[8,8,64,128]{3,2,1,0:T(8,128)(2,1)} %shard_map.148), calls=%async_computation.5 | async-start | bytes 2097152 | tf_op jit(solution)/shard_map/all_to_all | solution.py:437
  129.4 1.0 shard_map.145
  130.5 12.9 %all-to-all-done.5.final_ref = bf16[8,8,64,128]{3,2,1,0:T(8,128)(2,1)S(1)} async-done(((bf16[8,8,64,128]{3,2,1,0:T(8,128)(2,1)}), bf16[8,8,64,128]{3,2,1,0:T(8,128)(2,1)S(1)}, u32[]{:S(2)}, u32[]{:S(2)}) %all-to-all-start.5) | async-done | bytes 1048608 | tf_op jit(solution)/shard_map/all_to_all | solution.py:437
  143.4 1.1 shard_map.149
  (13 shorter events, 0.1 us)
Async XLA Ops:
  2.3 18.5 %all-to-all-start = ((bf16[8,32,256]{2,1,0:T(8,128)(2,1)}), bf16[8,32,256]{2,1,0:T(8,128)(2,1)S(1)}, u32[]{:S(2)}, u32[]{:S(2)}) async-start(bf16[8,32,256]{2,1,0:T(8,128)(2,1)} %shard_map.137), calls=%async_computation | async-start | bytes 262144 | tf_op jit(solution)/shard_map/all_to_all | solution.py:356
  20.8 0.7 copy-start.7
  24.0 3.8 %copy-start.1 = (bf16[128,256]{1,0:T(8,128)(2,1)S(1)}, bf16[128,256]{1,0:T(8,128)(2,1)}, u32[]{:S(2)}) copy-start(bf16[128,256]{1,0:T(8,128)(2,1)} %param.10) | copy-start | bytes 196612
  24.0 36.2 %copy-start.2 = (bf16[4,128,256]{2,1,0:T(8,128)(2,1)S(1)}, bf16[4,128,256]{2,1,0:T(8,128)(2,1)}, u32[]{:S(2)}) copy-start(bf16[4,128,256]{2,1,0:T(8,128)(2,1)} %get-tuple-element.17.diag_ref.diag_far_ref) | copy-start | bytes 786436
  24.0 36.2 %all-to-all-start.1 = ((bf16[8,41,16,256]{3,2,1,0:T(8,128)(2,1)}), bf16[8,41,16,256]{3,2,1,0:T(8,128)(2,1)S(1)}, u32[]{:S(2)}, u32[]{:S(2)}) async-start(bf16[8,41,16,256]{3,2,1,0:T(8,128)(2,1)} %get-tuple-element.16), calls=%async_computation.1 | async-start | bytes 5373952 | tf_op jit(solution)/shard_map/all_to_all | solution.py:391
  27.8 11.0 %collective-permute-start = (bf16[1,128,256]{2,1,0:T(8,128)(2,1)S(1)}, bf16[1,128,256]{2,1,0:T(8,128)(2,1)S(1)}, u32[]{:S(2)}, u32[]{:S(2)}) collective-permute-start(bf16[1,128,256]{2,1,0:T(8,128)(2,1)S(1)} %bitcast.11), channel_id=1, source_target_pairs={{0,32},{8,40},{16,48},{24,56},{32,0},{40,8},{48,16},{56,24},{1,33}... | collective-permute-start | bytes 196616 | tf_op jit(solution)/shard_map/ppermute | solution.py:324
  38.8 8.8 %collective-permute-start.1 = (bf16[2,128,256]{2,1,0:T(8,128)(2,1)S(1)}, bf16[2,128,256]{2,1,0:T(8,128)(2,1)S(1)}, u32[]{:S(2)}, u32[]{:S(2)}) collective-permute-start(bf16[2,128,256]{2,1,0:T(8,128)(2,1)S(1)} %shard_map.141.first_ref), channel_id=1, source_target_pairs={{0,16},{8,24},{16,0},{24,8},{32,48},{40,56},{48,32},{56,40},{1,17}... | collective-permute-start | bytes 393224 | tf_op jit(solution)/shard_map/ppermute | solution.py:324
  47.6 13.2 %collective-permute-start.2 = (bf16[4,128,256]{2,1,0:T(8,128)(2,1)S(1)}, bf16[4,128,256]{2,1,0:T(8,128)(2,1)S(1)}, u32[]{:S(2)}, u32[]{:S(2)}) collective-permute-start(bf16[4,128,256]{2,1,0:T(8,128)(2,1)S(1)} %shard_map.142.near_ref), channel_id=1, source_target_pairs={{0,8},{8,0},{16,24},{24,16},{32,40},{40,32},{48,56},{56,48},{1,9},... | collective-permute-start | bytes 786440 | tf_op jit(solution)/shard_map/ppermute | solution.py:324
  64.3 0.8 copy-start
  65.1 19.8 %all-to-all-start.2 = ((bf16[8,144,256]{2,1,0:T(8,128)(2,1)}), bf16[8,144,256]{2,1,0:T(8,128)(2,1)S(1)}, u32[]{:S(2)}, u32[]{:S(2)}) async-start(bf16[8,144,256]{2,1,0:T(8,128)(2,1)} %copy-done), calls=%async_computation.2 | async-start | bytes 1179648 | tf_op jit(solution)/shard_map/all_to_all | solution.py:329
  81.2 0.7 copy-start.3
  81.9 0.7 copy-start.5
  84.9 0.9 copy-start.4
  88.1 41.3 %copy-start.6 = (f32[128,256]{1,0:T(8,128)S(1)}, f32[128,256]{1,0:T(8,128)}, u32[]{:S(2)}) copy-start(f32[128,256]{1,0:T(8,128)} %copy-done.5) | copy-start | bytes 393220
  125.8 17.5 %all-to-all-start.5 = ((bf16[8,8,64,128]{3,2,1,0:T(8,128)(2,1)}), bf16[8,8,64,128]{3,2,1,0:T(8,128)(2,1)S(1)}, u32[]{:S(2)}, u32[]{:S(2)}) async-start(bf16[8,8,64,128]{3,2,1,0:T(8,128)(2,1)} %shard_map.148), calls=%async_computation.5 | async-start | bytes 2097152 | tf_op jit(solution)/shard_map/all_to_all | solution.py:437

commit v4 on v3

--- a/solution.py
+++ b/solution.py
@@ -119,7 +119,7 @@
         parts.append(jnp.where(lax.rem(row, 2) == 0, both[0:8, :], both[8:16, :]))
     parts = jnp.concatenate(parts, 0).astype(bf16)
     for dest in range(8):
-        out_ref[dest] = parts[:, dest * 256 : dest * 256 + 256]
+        out_ref[7 - dest] = parts[:, dest * 256 : dest * 256 + 256]
 
 
 def add_audio(audio_ref, given_ref, diag_ref, out_ref, wide_ref, sems):
@@ -131,7 +131,7 @@
         store.start()
     wide_ref[...] = jnp.zeros((4, 128, 256), f32)
     for source in range(8):
-        part = audio_ref[source].astype(f32)
+        part = audio_ref[7 - source].astype(f32)
         for place in range(4):
             for h in range(2):
                 row, lanes = source * 8 + h * 64, slice(h * 128, h * 128 + 128)
@@ -203,6 +203,7 @@
 ):
     diag_key, diag_value = diag_ref[2], diag_ref[3]
     audio = packed_ref[:, 528:656, :].astype(f32).reshape(8, 8, 16, 256)
+    audio = jnp.stack([audio[:, 7 - a] for a in range(8)], 1)
     all_keys = audio[:, :, 0:8, :].reshape(512, 256).astype(bf16)
     all_values = audio[:, :, 8:16, :].reshape(512, 256).astype(bf16)
     key_terms = jnp.zeros((128, 256), f32)
@@ -294,8 +295,8 @@
     for i in range(4):
         for h in range(2):
             for pair in range(4):
-                first = final_ref[pair * 2, 7 - i * 2 - h].astype(f32)
-                second = final_ref[pair * 2 + 1, 7 - i * 2 - h].astype(f32)
+                first = final_ref[7 - pair * 2, 7 - i * 2 - h].astype(f32)
+                second = final_ref[6 - pair * 2, 7 - i * 2 - h].astype(f32)
                 for a in range(8):
                     both = jnp.concatenate(
                         (first[a * 8 : a * 8 + 8, :], second[a * 8 : a * 8 + 8, :]), 0
@@ -353,7 +354,7 @@
         limit=60 * 1024 * 1024,
         args=(audio_query, audio_grad, audio_key, audio_value),
     )
-    audio = lax.all_to_all(audio, AUD, 0, 0, tiled=True)
+    audio = backwards(audio, AUD)
     (packed,) = call(
         pack_video,
         [((8, PACK // 16, 16, 256), bf16)],
@@ -434,7 +435,7 @@
     (summed,) = call(add_terms, [((8, 64, 128), bf16)], 10**6, args=(terms,))
     final = backwards(summed, COLS)
     (final,) = call(again, [((8, 8, 64, 128), bf16)], 10**6, args=(final,))
-    final = lax.all_to_all(final, ROWS, 0, 0, tiled=True)
+    final = backwards(final, ROWS)
     finished = call(lay_out, [((64, 2048), bf16)] * 4, 10**6, args=(final,))
     return (video_out, *finished)
 

time: 146 us -> 145 us (level)
  starting transfers between devices: 43.2 us -> 48.7 us
  waiting for transfers between devices: 36.1 us -> 30.8 us
    all_to_all x1 -> x3, starting transfers between devices: 9.75 us -> 27.8 us  [backwards(): lax.all_to_all(value, axes, 0, 0, axis_index_groups=[order], tiled=True)]
    all_to_all x2 -> x0, waiting for transfers between devices: 17.4 us -> none  [the longest x1 12.9 us: local(): final = lax.all_to_all(final, ROWS, 0, 0, tiled=True)]
    all_to_all x2 -> x0, starting transfers between devices: 13.8 us -> none  [the longest x1 10.2 us: local(): audio = lax.all_to_all(audio, AUD, 0, 0, tiled=True)]
    all_to_all x1 -> x3, waiting for transfers between devices: 2.31 us -> 15.7 us  [backwards(): lax.all_to_all(value, axes, 0, 0, axis_index_groups=[order], tiled=True)]
    all_to_all x1, waiting for transfers between devices: 10.6 us -> 7.86 us  [local(): lax.all_to_all(packed, ROWS, 0, 0, tiled=True).reshape(8, PACK, 256)]
    ppermute x3, waiting for transfers between devices: 5.75 us -> 7.26 us  [swap(): return lax.ppermute(value, axis, [(i, i ^ distance) for i in range(count)])]
where the time goes in v4:
time: 145 us; the launch traced here: 144 us
  starting transfers between devices  48.7 us (34%)
  blocking collectives  35.7 us (25%)
  waiting for transfers between devices  30.8 us (21%)
  Pallas kernels  23.5 us (16%)
  local copies, waits for them, and re-layouts  3.71 us (3%)
    all_to_all x2, blocking collectives, backwards(): lax.all_to_all(value, axes, 0, 0, axis_index_groups=[order], tiled=True)  35.7 us
    all_to_all x3, starting transfers between devices, backwards(): lax.all_to_all(value, axes, 0, 0, axis_index_groups=[order], tiled=True)  27.8 us
    pallas_call x13, Pallas kernels, call(): pl.pallas_call(kernel, out_shape=[jax.ShapeDtypeStruct(s, d) for s, d in...  23.5 us
    ppermute x3, starting transfers between devices, swap(): return lax.ppermute(value, axis, [(i, i ^ distance) for i in range(count)])  17.1 us
    all_to_all x3, waiting for transfers between devices, backwards(): lax.all_to_all(value, axes, 0, 0, axis_index_groups=[order], tiled=True)  15.7 us
    all_to_all x1, waiting for transfers between devices, local(): lax.all_to_all(packed, ROWS, 0, 0, tiled=True).reshape(8, PACK, 256)  7.86 us
    ppermute x3, waiting for transfers between devices, swap(): return lax.ppermute(value, axis, [(i, i ^ distance) for i in range(count)])  7.26 us
    all_to_all x1, starting transfers between devices, local(): lax.all_to_all(packed, ROWS, 0, 0, tiled=True).reshape(8, PACK, 256)  3.77 us
  transfers between devices with their start and end apart: 7, of which 6 were waited for; matrix products, arithmetic and copies ran while one was open for 0% of the time, Pallas kernels for 8%

profile of v4, /device:TPU:1, one launch (start us, length us, event | category | flops | bytes accessed | tf_op | source)
XLA Modules:
  0.0 143.8 jit_solution(1108735731483949121)
XLA Ops:
  0.6 1.7 %shard_map.137 = bf16[8,32,256]{2,1,0:T(8,128)(2,1)} custom-call(bf16[64,2048]{1,0:T(8,128)(2,1)} %rest_0_.1, bf16[64,2048]{1,0:T(8,128)(2,1)} %rest_1_.1, bf16[64,2048]{1,0:T(8,128)(2,1)} %rest_2_.1, bf16[64,2048]{1,0:T(8,128)(2,1)} %rest_3_.1), custom_call_target="tpu_custom_call" | custom-call | flops 1000000 | bytes 4000000 | tf_op jit(solution)/shard_map/pallas_call | solution.py:42
  2.3 11.6 %all-to-all-start = ((bf16[8,32,256]{2,1,0:T(8,128)(2,1)}), bf16[8,32,256]{2,1,0:T(8,128)(2,1)S(1)}, u32[]{:S(2)}, u32[]{:S(2)}) async-start(bf16[8,32,256]{2,1,0:T(8,128)(2,1)} %shard_map.137), calls=%async_computation | async-start | bytes 262144 | tf_op jit(solution)/shard_map/all_to_all | solution.py:330
  14.6 3.2 %shard_map.138.given_ref = bf16[8,41,16,256]{3,2,1,0:T(8,128)(2,1)} custom-call(s32[1,3]{1,0:T(1,128)} %list_ref.1, s32[1]{0:T(128)S(6)} %copy.17.count_ref, bf16[8,16,256]{2,1,0:T(8,128)(2,1)} %bitcast.10, bf16[8,16,256]{2,1,0:T(8,128)(2,1)} %bitcast.13, bf16[8,16,256]{2,1,0:T(8,128)(2,1)} %bitcast.14, bf16[8,16,256]{2,1,0:T(8,128)(2,1)} %bitcast.15), custom_call_target="tpu_custom_call" | custom-call | flops 1000000 | bytes 4000000 | tf_op jit(solution)/shard_map/pallas_call | solution.py:42
  17.8 1.0 all-to-all-done.audio_ref
  18.8 0.7 copy-done.7
  19.4 2.5 %shard_map.139 = (bf16[4,128,256]{2,1,0:T(8,128)(2,1)}, bf16[8,41,16,256]{3,2,1,0:T(8,128)(2,1)}) custom-call(bf16[8,32,256]{2,1,0:T(8,128)(2,1)} %copy-done.7, bf16[8,41,16,256]{3,2,1,0:T(8,128)(2,1)} %shard_map.138.given_ref), custom_call_target="tpu_custom_call", output_to_operand_aliasing={{1}: (1, {})} | custom-call | flops 1000000 | bytes 4000000 | tf_op jit(solution)/shard_map/pallas_call | solution.py:42
  22.0 0.0 copy-start.1
  22.0 3.8 %all-to-all-start.1 = ((bf16[8,41,16,256]{3,2,1,0:T(8,128)(2,1)}), bf16[8,41,16,256]{3,2,1,0:T(8,128)(2,1)S(1)}, u32[]{:S(2)}, u32[]{:S(2)}) async-start(bf16[8,41,16,256]{3,2,1,0:T(8,128)(2,1)} %get-tuple-element.16), calls=%async_computation.1 | async-start | bytes 5373952 | tf_op jit(solution)/shard_map/all_to_all | solution.py:392
  25.8 9.3 %collective-permute-start = (bf16[1,128,256]{2,1,0:T(8,128)(2,1)S(1)}, bf16[1,128,256]{2,1,0:T(8,128)(2,1)S(1)}, u32[]{:S(2)}, u32[]{:S(2)}) collective-permute-start(bf16[1,128,256]{2,1,0:T(8,128)(2,1)S(1)} %bitcast.11), channel_id=1, source_target_pairs={{0,32},{8,40},{16,48},{24,56},{32,0},{40,8},{48,16},{56,24},{1,33}... | collective-permute-start | bytes 196616 | tf_op jit(solution)/shard_map/ppermute | solution.py:325
  35.1 1.7 %collective-permute-done.second_ref = bf16[1,128,256]{2,1,0:T(8,128)(2,1)S(1)} collective-permute-done((bf16[1,128,256]{2,1,0:T(8,128)(2,1)S(1)}, bf16[1,128,256]{2,1,0:T(8,128)(2,1)S(1)}, u32[]{:S(2)}, u32[]{:S(2)}) %collective-permute-start) | collective-permute-done | bytes 65568 | tf_op jit(solution)/shard_map/ppermute | solution.py:325
  36.8 5.9 %collective-permute-start.1 = (bf16[2,128,256]{2,1,0:T(8,128)(2,1)S(1)}, bf16[2,128,256]{2,1,0:T(8,128)(2,1)S(1)}, u32[]{:S(2)}, u32[]{:S(2)}) collective-permute-start(bf16[2,128,256]{2,1,0:T(8,128)(2,1)S(1)} %shard_map.141.first_ref), channel_id=1, source_target_pairs={{0,16},{8,24},{16,0},{24,8},{32,48},{40,56},{48,32},{56,40},{1,17}... | collective-permute-start | bytes 393224 | tf_op jit(solution)/shard_map/ppermute | solution.py:325
  42.7 5.5 %collective-permute-done.1.second_ref = bf16[2,128,256]{2,1,0:T(8,128)(2,1)S(1)} collective-permute-done((bf16[2,128,256]{2,1,0:T(8,128)(2,1)S(1)}, bf16[2,128,256]{2,1,0:T(8,128)(2,1)S(1)}, u32[]{:S(2)}, u32[]{:S(2)}) %collective-permute-start.1) | collective-permute-done | bytes 131104 | tf_op jit(solution)/shard_map/ppermute | solution.py:325
  48.3 1.9 %collective-permute-start.2 = (bf16[4,128,256]{2,1,0:T(8,128)(2,1)S(1)}, bf16[4,128,256]{2,1,0:T(8,128)(2,1)S(1)}, u32[]{:S(2)}, u32[]{:S(2)}) collective-permute-start(bf16[4,128,256]{2,1,0:T(8,128)(2,1)S(1)} %shard_map.142.near_ref), channel_id=1, source_target_pairs={{0,8},{8,0},{16,24},{24,16},{32,40},{40,32},{48,56},{56,48},{1,9},... | collective-permute-start | bytes 786440 | tf_op jit(solution)/shard_map/ppermute | solution.py:325
  50.2 7.9 %all-to-all-done.1 = bf16[8,41,16,256]{3,2,1,0:T(8,128)(2,1)S(1)} async-done(((bf16[8,41,16,256]{3,2,1,0:T(8,128)(2,1)}), bf16[8,41,16,256]{3,2,1,0:T(8,128)(2,1)S(1)}, u32[]{:S(2)}, u32[]{:S(2)}) %all-to-all-start.1) | async-done | bytes 2687008 | tf_op jit(solution)/shard_map/all_to_all | solution.py:392
  58.1 0.6 shard_map.143.stats_ref
  58.7 3.4 %shard_map.144 = bf16[8,144,256]{2,1,0:T(8,128)(2,1)S(1)} custom-call(bf16[4,128,256]{2,1,0:T(8,128)(2,1)S(1)} %shard_map.142.near_ref, bf16[4,128,256]{2,1,0:T(8,128)(2,1)S(1)} %collective-permute-done.2.far_ref, bf16[8,656,256]{2,1,0:T(8,128)(2,1)S(1)} %bitcast.7, f32[13,256]{1,0:T(8,128)S(1)} %shard_map.143.stats_ref), custom_call_target="tpu_custom_call" | custom-call | flops 4000000000 | bytes 4000000 | tf_op jit(solution)/shard_map/pallas_call | solution.py:42
  62.2 0.8 copy-done
  63.0 11.0 %all-to-all-start.2 = ((bf16[8,144,256]{2,1,0:T(8,128)(2,1)}), bf16[8,144,256]{2,1,0:T(8,128)(2,1)S(1)}, u32[]{:S(2)}, u32[]{:S(2)}) async-start(bf16[8,144,256]{2,1,0:T(8,128)(2,1)} %copy-done), calls=%async_computation.2 | async-start | bytes 1179648 | tf_op jit(solution)/shard_map/all_to_all | solution.py:330
  74.0 6.4 %shard_map.140 = (f32[128,256]{1,0:T(8,128)S(1)}, f32[2,128,128]{2,1,0:T(8,128)S(1)}) custom-call(bf16[8,656,256]{2,1,0:T(8,128)(2,1)S(1)} %bitcast.8, bf16[4,128,256]{2,1,0:T(8,128)(2,1)S(1)} %copy-done.2), custom_call_target="tpu_custom_call" | custom-call | flops 4000000000 | bytes 4000000 | tf_op jit(solution)/shard_map/pallas_call | solution.py:42
  80.4 0.0 copy-start.3
  80.4 0.6 copy-done.3
  81.1 0.7 copy-done.5
  81.7 2.9 %all-to-all-done.2.sent_ref = bf16[8,144,256]{2,1,0:T(8,128)(2,1)S(1)} async-done(((bf16[8,144,256]{2,1,0:T(8,128)(2,1)}), bf16[8,144,256]{2,1,0:T(8,128)(2,1)S(1)}, u32[]{:S(2)}, u32[]{:S(2)}) %all-to-all-start.2) | async-done | bytes 589856 | tf_op jit(solution)/shard_map/all_to_all | solution.py:330
  84.6 0.9 copy-done.4
  85.5 2.3 %shard_map.146 = f32[64,8,128]{2,1,0:T(8,128)S(1)} custom-call(bf16[8,144,256]{2,1,0:T(8,128)(2,1)S(1)} %all-to-all-done.2.sent_ref, bf16[8,656,256]{2,1,0:T(8,128)(2,1)S(1)} %bitcast.9, bf16[4,128,256]{2,1,0:T(8,128)(2,1)S(1)} %copy-done.2, f32[2,128,128]{2,1,0:T(8,128)S(1)} %copy-done.4), custom_call_target="tpu_custom_call" | custom-call | flops 1000000000 | bytes 4000000 | tf_op jit(solution)/shard_map/pallas_call | solution.py:42
  87.9 25.6 %all_to_all.30.terms_ref = f32[64,8,128]{2,1,0:T(8,128)S(1)} all-to-all(f32[64,8,128]{2,1,0:T(8,128)S(1)} %shard_map.146), channel_id=1, replica_groups={{63,55,47,39,31,23,15,7,62,54,46,38,30,22,14,6,61,53,45,37,29,21,13,5,6..., dimensions={0} | all-to-all | bytes 524288 | tf_op jit(solution)/shard_map/all_to_all | solution.py:330
  113.4 10.2 %all_to_all.31.ref = bf16[8,64,128]{2,1,0:T(8,128)(2,1)S(1)} all-to-all(bf16[8,64,128]{2,1,0:T(8,128)(2,1)S(1)} %shard_map.147), channel_id=1, replica_groups={{56,48,40,32,24,16,8,0},{57,49,41,33,25,17,9,1},{58,50,42,34,26,18,10,2..., dimensions={0} | all-to-all | bytes 262144 | tf_op jit(solution)/shard_map/all_to_all | solution.py:330
  123.6 1.1 shard_map.148
  124.7 5.2 %all-to-all-start.5 = ((bf16[8,8,64,128]{3,2,1,0:T(8,128)(2,1)}), bf16[8,8,64,128]{3,2,1,0:T(8,128)(2,1)S(1)}, u32[]{:S(2)}, u32[]{:S(2)}) async-start(bf16[8,8,64,128]{3,2,1,0:T(8,128)(2,1)} %shard_map.148), calls=%async_computation.5 | async-start | bytes 2097152 | tf_op jit(solution)/shard_map/all_to_all | solution.py:330
  129.9 1.0 shard_map.145
  130.9 11.8 %all-to-all-done.5.final_ref = bf16[8,8,64,128]{3,2,1,0:T(8,128)(2,1)S(1)} async-done(((bf16[8,8,64,128]{3,2,1,0:T(8,128)(2,1)}), bf16[8,8,64,128]{3,2,1,0:T(8,128)(2,1)S(1)}, u32[]{:S(2)}, u32[]{:S(2)}) %all-to-all-start.5) | async-done | bytes 1048608 | tf_op jit(solution)/shard_map/all_to_all | solution.py:330
  142.7 1.1 shard_map.149
  (13 shorter events, 0.1 us)
Async XLA Ops:
  2.3 16.5 %all-to-all-start = ((bf16[8,32,256]{2,1,0:T(8,128)(2,1)}), bf16[8,32,256]{2,1,0:T(8,128)(2,1)S(1)}, u32[]{:S(2)}, u32[]{:S(2)}) async-start(bf16[8,32,256]{2,1,0:T(8,128)(2,1)} %shard_map.137), calls=%async_computation | async-start | bytes 262144 | tf_op jit(solution)/shard_map/all_to_all | solution.py:330
  18.8 0.7 copy-start.7
  22.0 3.8 %copy-start.1 = (bf16[128,256]{1,0:T(8,128)(2,1)S(1)}, bf16[128,256]{1,0:T(8,128)(2,1)}, u32[]{:S(2)}) copy-start(bf16[128,256]{1,0:T(8,128)(2,1)} %param.10) | copy-start | bytes 196612
  22.0 36.1 %copy-start.2 = (bf16[4,128,256]{2,1,0:T(8,128)(2,1)S(1)}, bf16[4,128,256]{2,1,0:T(8,128)(2,1)}, u32[]{:S(2)}) copy-start(bf16[4,128,256]{2,1,0:T(8,128)(2,1)} %get-tuple-element.17.diag_ref.diag_far_ref) | copy-start | bytes 786436
  22.0 36.1 %all-to-all-start.1 = ((bf16[8,41,16,256]{3,2,1,0:T(8,128)(2,1)}), bf16[8,41,16,256]{3,2,1,0:T(8,128)(2,1)S(1)}, u32[]{:S(2)}, u32[]{:S(2)}) async-start(bf16[8,41,16,256]{3,2,1,0:T(8,128)(2,1)} %get-tuple-element.16), calls=%async_computation.1 | async-start | bytes 5373952 | tf_op jit(solution)/shard_map/all_to_all | solution.py:392
  25.8 11.1 %collective-permute-start = (bf16[1,128,256]{2,1,0:T(8,128)(2,1)S(1)}, bf16[1,128,256]{2,1,0:T(8,128)(2,1)S(1)}, u32[]{:S(2)}, u32[]{:S(2)}) collective-permute-start(bf16[1,128,256]{2,1,0:T(8,128)(2,1)S(1)} %bitcast.11), channel_id=1, source_target_pairs={{0,32},{8,40},{16,48},{24,56},{32,0},{40,8},{48,16},{56,24},{1,33}... | collective-permute-start | bytes 196616 | tf_op jit(solution)/shard_map/ppermute | solution.py:325
  36.8 11.4 %collective-permute-start.1 = (bf16[2,128,256]{2,1,0:T(8,128)(2,1)S(1)}, bf16[2,128,256]{2,1,0:T(8,128)(2,1)S(1)}, u32[]{:S(2)}, u32[]{:S(2)}) collective-permute-start(bf16[2,128,256]{2,1,0:T(8,128)(2,1)S(1)} %shard_map.141.first_ref), channel_id=1, source_target_pairs={{0,16},{8,24},{16,0},{24,8},{32,48},{40,56},{48,32},{56,40},{1,17}... | collective-permute-start | bytes 393224 | tf_op jit(solution)/shard_map/ppermute | solution.py:325
  48.3 10.4 %collective-permute-start.2 = (bf16[4,128,256]{2,1,0:T(8,128)(2,1)S(1)}, bf16[4,128,256]{2,1,0:T(8,128)(2,1)S(1)}, u32[]{:S(2)}, u32[]{:S(2)}) collective-permute-start(bf16[4,128,256]{2,1,0:T(8,128)(2,1)S(1)} %shard_map.142.near_ref), channel_id=1, source_target_pairs={{0,8},{8,0},{16,24},{24,16},{32,40},{40,32},{48,56},{56,48},{1,9},... | collective-permute-start | bytes 786440 | tf_op jit(solution)/shard_map/ppermute | solution.py:325
  62.2 0.8 copy-start
  63.0 21.6 %all-to-all-start.2 = ((bf16[8,144,256]{2,1,0:T(8,128)(2,1)}), bf16[8,144,256]{2,1,0:T(8,128)(2,1)S(1)}, u32[]{:S(2)}, u32[]{:S(2)}) async-start(bf16[8,144,256]{2,1,0:T(8,128)(2,1)} %copy-done), calls=%async_computation.2 | async-start | bytes 1179648 | tf_op jit(solution)/shard_map/all_to_all | solution.py:330
  80.4 0.7 copy-start.3
  81.0 0.7 copy-start.5
  84.6 0.9 copy-start.4
  87.8 42.1 %copy-start.6 = (f32[128,256]{1,0:T(8,128)S(1)}, f32[128,256]{1,0:T(8,128)}, u32[]{:S(2)}) copy-start(f32[128,256]{1,0:T(8,128)} %copy-done.5) | copy-start | bytes 393220
  124.7 18.0 %all-to-all-start.5 = ((bf16[8,8,64,128]{3,2,1,0:T(8,128)(2,1)}), bf16[8,8,64,128]{3,2,1,0:T(8,128)(2,1)S(1)}, u32[]{:S(2)}, u32[]{:S(2)}) async-start(bf16[8,8,64,128]{3,2,1,0:T(8,128)(2,1)} %shard_map.148), calls=%async_computation.5 | async-start | bytes 2097152 | tf_op jit(solution)/shard_map/all_to_all | solution.py:330

commit v5 on v4

--- a/solution.py
+++ b/solution.py
@@ -70,9 +70,9 @@
 
 
 def pack_video(list_ref, count_ref, *rest):
-    ins, out_ref, held, marks, sems = rest[:4], *rest[4:]
+    ins, out_ref, held, sems = rest[:4], *rest[4:]
     loads = [
-        pltpu.make_async_copy(ref, held.at[place], sems.at[place])
+        pltpu.make_async_copy(ref, held.at[place * 8 : place * 8 + 8], sems.at[place])
         for place, ref in enumerate(ins)
     ]
     for load in loads:
@@ -83,21 +83,14 @@
     for slot in range(3):
         entry = jnp.where(slot < count_ref[0], list_ref[0, slot], -2)
         allow = jnp.where(block == entry, 1.0, allow)
-    marks[...] = allow.astype(bf16)
-    stores = []
-    for dest in range(8):
-        stores.append(
-            pltpu.make_async_copy(marks, out_ref.at[dest, 32], sems.at[4 + len(stores)])
-        )
-        stores[-1].start()
-    for place, load in enumerate(loads):
+    held[32] = allow.astype(bf16)
+    for load in loads:
         load.wait()
-        for dest in range(8):
-            target = out_ref.at[dest, place * 8 : place * 8 + 8]
-            stores.append(
-                pltpu.make_async_copy(held.at[place], target, sems.at[4 + len(stores)])
-            )
-            stores[-1].start()
+    stores = [
+        pltpu.make_async_copy(held, out_ref.at[dest, 0:33], sems.at[4 + dest]) for dest in range(8)
+    ]
+    for store in stores:
+        store.start()
     for store in stores:
         store.wait()
 
@@ -236,7 +229,7 @@
         rows, lanes = slice(h * 64, h * 64 + 64), slice(h * 128, h * 128 + 128)
         sums_ref[0, rows, :] = key_terms[rows, lanes] * SCALE
         sums_ref[1, rows, :] = value_terms[rows, lanes]
-    own_ref[...] = out_ref[lax.axis_index(ROWS)]
+    own_ref[...] = out_ref[7 - lax.axis_index(ROWS)]
 
 
 def back_terms(
@@ -360,9 +353,8 @@
         [((8, PACK // 16, 16, 256), bf16)],
         10**6,
         scratch=[
-            pltpu.VMEM((4, 8, 16, 256), bf16),
-            pltpu.VMEM((16, 256), bf16),
-            pltpu.SemaphoreType.DMA((44,)),
+            pltpu.VMEM((33, 16, 256), bf16),
+            pltpu.SemaphoreType.DMA((12,)),
         ],
         in_specs=[SM, SM] + [HBM] * 4,
         out_specs=[HBM],
@@ -389,7 +381,7 @@
     )
     near = video_query.reshape(1, 128, 256)
     packed, near = lax.optimization_barrier((packed, near))
-    packed = lax.all_to_all(packed, ROWS, 0, 0, tiled=True).reshape(8, PACK, 256)
+    packed = backwards(packed, ROWS).reshape(8, PACK, 256)
     for distance in (4, 2):
         far = swap(near, "z", distance)
         (near,) = call(

time: 145 us -> 146 us (level)
  starting transfers between devices: 48.7 us -> 51.2 us
    all_to_all x1 -> x0, waiting for transfers between devices: 7.86 us -> none  [local(): lax.all_to_all(packed, ROWS, 0, 0, tiled=True).reshape(8, PACK, 256)]
    all_to_all x3 -> x4, waiting for transfers between devices: 15.7 us -> 22.9 us  [backwards(): lax.all_to_all(value, axes, 0, 0, axis_index_groups=[order], tiled=True)]
    all_to_all x3 -> x4, starting transfers between devices: 27.8 us -> 33.6 us  [backwards(): lax.all_to_all(value, axes, 0, 0, axis_index_groups=[order], tiled=True)]
    all_to_all x1 -> x0, starting transfers between devices: 3.77 us -> none  [local(): lax.all_to_all(packed, ROWS, 0, 0, tiled=True).reshape(8, PACK, 256)]
where the time goes in v5:
time: 146 us; the launch traced here: 145 us
  starting transfers between devices  51.2 us (35%)
  blocking collectives  34.8 us (24%)
  waiting for transfers between devices  30.4 us (21%)
  Pallas kernels  23.3 us (16%)
  local copies, waits for them, and re-layouts  3.71 us (3%)
    all_to_all x2, blocking collectives, backwards(): lax.all_to_all(value, axes, 0, 0, axis_index_groups=[order], tiled=True)  34.8 us
    all_to_all x4, starting transfers between devices, backwards(): lax.all_to_all(value, axes, 0, 0, axis_index_groups=[order], tiled=True)  33.6 us
    pallas_call x13, Pallas kernels, call(): pl.pallas_call(kernel, out_shape=[jax.ShapeDtypeStruct(s, d) for s, d in...  23.3 us
    all_to_all x4, waiting for transfers between devices, backwards(): lax.all_to_all(value, axes, 0, 0, axis_index_groups=[order], tiled=True)  22.9 us
    ppermute x3, starting transfers between devices, swap(): return lax.ppermute(value, axis, [(i, i ^ distance) for i in range(count)])  17.6 us
    ppermute x3, waiting for transfers between devices, swap(): return lax.ppermute(value, axis, [(i, i ^ distance) for i in range(count)])  7.44 us
    unnamed x16, local copies, waits for them, and re-layouts  3.71 us
  transfers between devices with their start and end apart: 7, of which 6 were waited for; matrix products, arithmetic and copies ran while one was open for 0% of the time, Pallas kernels for 8%

profile of v5, /device:TPU:1, one launch (start us, length us, event | category | flops | bytes accessed | tf_op | source)
XLA Modules:
  0.0 144.8 jit_solution(14424266341196366405)
XLA Ops:
  0.6 1.7 %shard_map.137 = bf16[8,32,256]{2,1,0:T(8,128)(2,1)} custom-call(bf16[64,2048]{1,0:T(8,128)(2,1)} %rest_0_.1, bf16[64,2048]{1,0:T(8,128)(2,1)} %rest_1_.1, bf16[64,2048]{1,0:T(8,128)(2,1)} %rest_2_.1, bf16[64,2048]{1,0:T(8,128)(2,1)} %rest_3_.1), custom_call_target="tpu_custom_call" | custom-call | flops 1000000 | bytes 4000000 | tf_op jit(solution)/shard_map/pallas_call | solution.py:42
  2.3 11.6 %all-to-all-start = ((bf16[8,32,256]{2,1,0:T(8,128)(2,1)}), bf16[8,32,256]{2,1,0:T(8,128)(2,1)S(1)}, u32[]{:S(2)}, u32[]{:S(2)}) async-start(bf16[8,32,256]{2,1,0:T(8,128)(2,1)} %shard_map.137), calls=%async_computation | async-start | bytes 262144 | tf_op jit(solution)/shard_map/all_to_all | solution.py:323
  14.6 3.1 %shard_map.138.given_ref = bf16[8,41,16,256]{3,2,1,0:T(8,128)(2,1)} custom-call(s32[1,3]{1,0:T(1,128)} %list_ref.1, s32[1]{0:T(128)S(6)} %copy.17.count_ref, bf16[8,16,256]{2,1,0:T(8,128)(2,1)} %bitcast.10, bf16[8,16,256]{2,1,0:T(8,128)(2,1)} %bitcast.13, bf16[8,16,256]{2,1,0:T(8,128)(2,1)} %bitcast.14, bf16[8,16,256]{2,1,0:T(8,128)(2,1)} %bitcast.15), custom_call_target="tpu_custom_call" | custom-call | flops 1000000 | bytes 4000000 | tf_op jit(solution)/shard_map/pallas_call | solution.py:42
  17.6 1.1 all-to-all-done.audio_ref
  18.8 0.7 copy-done.7
  19.4 2.5 %shard_map.139 = (bf16[4,128,256]{2,1,0:T(8,128)(2,1)}, bf16[8,41,16,256]{3,2,1,0:T(8,128)(2,1)}) custom-call(bf16[8,32,256]{2,1,0:T(8,128)(2,1)} %copy-done.7, bf16[8,41,16,256]{3,2,1,0:T(8,128)(2,1)} %shard_map.138.given_ref), custom_call_target="tpu_custom_call", output_to_operand_aliasing={{1}: (1, {})} | custom-call | flops 1000000 | bytes 4000000 | tf_op jit(solution)/shard_map/pallas_call | solution.py:42
  22.0 0.0 copy-start.1
  22.0 5.0 %all-to-all-start.1 = ((bf16[8,41,16,256]{3,2,1,0:T(8,128)(2,1)}), bf16[8,41,16,256]{3,2,1,0:T(8,128)(2,1)S(1)}, u32[]{:S(2)}, u32[]{:S(2)}) async-start(bf16[8,41,16,256]{3,2,1,0:T(8,128)(2,1)} %get-tuple-element.16), calls=%async_computation.1 | async-start | bytes 5373952 | tf_op jit(solution)/shard_map/all_to_all | solution.py:323
  27.0 10.0 %collective-permute-start = (bf16[1,128,256]{2,1,0:T(8,128)(2,1)S(1)}, bf16[1,128,256]{2,1,0:T(8,128)(2,1)S(1)}, u32[]{:S(2)}, u32[]{:S(2)}) collective-permute-start(bf16[1,128,256]{2,1,0:T(8,128)(2,1)S(1)} %bitcast.11), channel_id=1, source_target_pairs={{0,32},{8,40},{16,48},{24,56},{32,0},{40,8},{48,16},{56,24},{1,33}... | collective-permute-start | bytes 196616 | tf_op jit(solution)/shard_map/ppermute | solution.py:318
  37.0 1.7 %collective-permute-done.second_ref = bf16[1,128,256]{2,1,0:T(8,128)(2,1)S(1)} collective-permute-done((bf16[1,128,256]{2,1,0:T(8,128)(2,1)S(1)}, bf16[1,128,256]{2,1,0:T(8,128)(2,1)S(1)}, u32[]{:S(2)}, u32[]{:S(2)}) %collective-permute-start) | collective-permute-done | bytes 65568 | tf_op jit(solution)/shard_map/ppermute | solution.py:318
  38.7 5.7 %collective-permute-start.1 = (bf16[2,128,256]{2,1,0:T(8,128)(2,1)S(1)}, bf16[2,128,256]{2,1,0:T(8,128)(2,1)S(1)}, u32[]{:S(2)}, u32[]{:S(2)}) collective-permute-start(bf16[2,128,256]{2,1,0:T(8,128)(2,1)S(1)} %shard_map.141.first_ref), channel_id=1, source_target_pairs={{0,16},{8,24},{16,0},{24,8},{32,48},{40,56},{48,32},{56,40},{1,17}... | collective-permute-start | bytes 393224 | tf_op jit(solution)/shard_map/ppermute | solution.py:318
  44.4 5.7 %collective-permute-done.1.second_ref = bf16[2,128,256]{2,1,0:T(8,128)(2,1)S(1)} collective-permute-done((bf16[2,128,256]{2,1,0:T(8,128)(2,1)S(1)}, bf16[2,128,256]{2,1,0:T(8,128)(2,1)S(1)}, u32[]{:S(2)}, u32[]{:S(2)}) %collective-permute-start.1) | collective-permute-done | bytes 131104 | tf_op jit(solution)/shard_map/ppermute | solution.py:318
  50.2 1.9 %collective-permute-start.2 = (bf16[4,128,256]{2,1,0:T(8,128)(2,1)S(1)}, bf16[4,128,256]{2,1,0:T(8,128)(2,1)S(1)}, u32[]{:S(2)}, u32[]{:S(2)}) collective-permute-start(bf16[4,128,256]{2,1,0:T(8,128)(2,1)S(1)} %shard_map.142.near_ref), channel_id=1, source_target_pairs={{0,8},{8,0},{16,24},{24,16},{32,40},{40,32},{48,56},{56,48},{1,9},... | collective-permute-start | bytes 786440 | tf_op jit(solution)/shard_map/ppermute | solution.py:318
  52.1 6.2 %all-to-all-done.1 = bf16[8,41,16,256]{3,2,1,0:T(8,128)(2,1)S(1)} async-done(((bf16[8,41,16,256]{3,2,1,0:T(8,128)(2,1)}), bf16[8,41,16,256]{3,2,1,0:T(8,128)(2,1)S(1)}, u32[]{:S(2)}, u32[]{:S(2)}) %all-to-all-start.1) | async-done | bytes 2687008 | tf_op jit(solution)/shard_map/all_to_all | solution.py:323
  58.3 0.6 shard_map.143.stats_ref
  59.0 3.4 %shard_map.144 = bf16[8,144,256]{2,1,0:T(8,128)(2,1)S(1)} custom-call(bf16[4,128,256]{2,1,0:T(8,128)(2,1)S(1)} %shard_map.142.near_ref, bf16[4,128,256]{2,1,0:T(8,128)(2,1)S(1)} %collective-permute-done.2.far_ref, bf16[8,656,256]{2,1,0:T(8,128)(2,1)S(1)} %bitcast.7, f32[13,256]{1,0:T(8,128)S(1)} %shard_map.143.stats_ref), custom_call_target="tpu_custom_call" | custom-call | flops 4000000000 | bytes 4000000 | tf_op jit(solution)/shard_map/pallas_call | solution.py:42
  62.4 0.8 copy-done
  63.2 11.6 %all-to-all-start.2 = ((bf16[8,144,256]{2,1,0:T(8,128)(2,1)}), bf16[8,144,256]{2,1,0:T(8,128)(2,1)S(1)}, u32[]{:S(2)}, u32[]{:S(2)}) async-start(bf16[8,144,256]{2,1,0:T(8,128)(2,1)} %copy-done), calls=%async_computation.2 | async-start | bytes 1179648 | tf_op jit(solution)/shard_map/all_to_all | solution.py:323
  74.8 6.4 %shard_map.140 = (f32[128,256]{1,0:T(8,128)S(1)}, f32[2,128,128]{2,1,0:T(8,128)S(1)}) custom-call(bf16[8,656,256]{2,1,0:T(8,128)(2,1)S(1)} %bitcast.8, bf16[4,128,256]{2,1,0:T(8,128)(2,1)S(1)} %copy-done.2), custom_call_target="tpu_custom_call" | custom-call | flops 4000000000 | bytes 4000000 | tf_op jit(solution)/shard_map/pallas_call | solution.py:42
  81.2 0.0 copy-start.3
  81.2 0.6 copy-done.3
  81.8 0.7 copy-done.5
  82.5 3.5 %all-to-all-done.2.sent_ref = bf16[8,144,256]{2,1,0:T(8,128)(2,1)S(1)} async-done(((bf16[8,144,256]{2,1,0:T(8,128)(2,1)}), bf16[8,144,256]{2,1,0:T(8,128)(2,1)S(1)}, u32[]{:S(2)}, u32[]{:S(2)}) %all-to-all-start.2) | async-done | bytes 589856 | tf_op jit(solution)/shard_map/all_to_all | solution.py:323
  86.0 0.9 copy-done.4
  86.9 2.3 %shard_map.146 = f32[64,8,128]{2,1,0:T(8,128)S(1)} custom-call(bf16[8,144,256]{2,1,0:T(8,128)(2,1)S(1)} %all-to-all-done.2.sent_ref, bf16[8,656,256]{2,1,0:T(8,128)(2,1)S(1)} %bitcast.9, bf16[4,128,256]{2,1,0:T(8,128)(2,1)S(1)} %copy-done.2, f32[2,128,128]{2,1,0:T(8,128)S(1)} %copy-done.4), custom_call_target="tpu_custom_call" | custom-call | flops 1000000000 | bytes 4000000 | tf_op jit(solution)/shard_map/pallas_call | solution.py:42
  89.2 23.8 %all_to_all.30.terms_ref = f32[64,8,128]{2,1,0:T(8,128)S(1)} all-to-all(f32[64,8,128]{2,1,0:T(8,128)S(1)} %shard_map.146), channel_id=1, replica_groups={{63,55,47,39,31,23,15,7,62,54,46,38,30,22,14,6,61,53,45,37,29,21,13,5,6..., dimensions={0} | all-to-all | bytes 524288 | tf_op jit(solution)/shard_map/all_to_all | solution.py:323
  113.0 11.0 %all_to_all.31.ref = bf16[8,64,128]{2,1,0:T(8,128)(2,1)S(1)} all-to-all(bf16[8,64,128]{2,1,0:T(8,128)(2,1)S(1)} %shard_map.147), channel_id=1, replica_groups={{56,48,40,32,24,16,8,0},{57,49,41,33,25,17,9,1},{58,50,42,34,26,18,10,2..., dimensions={0} | all-to-all | bytes 262144 | tf_op jit(solution)/shard_map/all_to_all | solution.py:323
  124.0 1.1 shard_map.148
  125.1 5.4 %all-to-all-start.5 = ((bf16[8,8,64,128]{3,2,1,0:T(8,128)(2,1)}), bf16[8,8,64,128]{3,2,1,0:T(8,128)(2,1)S(1)}, u32[]{:S(2)}, u32[]{:S(2)}) async-start(bf16[8,8,64,128]{3,2,1,0:T(8,128)(2,1)} %shard_map.148), calls=%async_computation.5 | async-start | bytes 2097152 | tf_op jit(solution)/shard_map/all_to_all | solution.py:323
  130.6 1.0 shard_map.145
  131.6 12.1 %all-to-all-done.5.final_ref = bf16[8,8,64,128]{3,2,1,0:T(8,128)(2,1)S(1)} async-done(((bf16[8,8,64,128]{3,2,1,0:T(8,128)(2,1)}), bf16[8,8,64,128]{3,2,1,0:T(8,128)(2,1)S(1)}, u32[]{:S(2)}, u32[]{:S(2)}) %all-to-all-start.5) | async-done | bytes 1048608 | tf_op jit(solution)/shard_map/all_to_all | solution.py:323
  143.7 1.1 shard_map.149
  (13 shorter events, 0.1 us)
Async XLA Ops:
  2.3 16.5 %all-to-all-start = ((bf16[8,32,256]{2,1,0:T(8,128)(2,1)}), bf16[8,32,256]{2,1,0:T(8,128)(2,1)S(1)}, u32[]{:S(2)}, u32[]{:S(2)}) async-start(bf16[8,32,256]{2,1,0:T(8,128)(2,1)} %shard_map.137), calls=%async_computation | async-start | bytes 262144 | tf_op jit(solution)/shard_map/all_to_all | solution.py:323
  18.8 0.7 copy-start.7
  22.0 5.0 %copy-start.1 = (bf16[128,256]{1,0:T(8,128)(2,1)S(1)}, bf16[128,256]{1,0:T(8,128)(2,1)}, u32[]{:S(2)}) copy-start(bf16[128,256]{1,0:T(8,128)(2,1)} %param.10) | copy-start | bytes 196612
  22.0 36.3 %copy-start.2 = (bf16[4,128,256]{2,1,0:T(8,128)(2,1)S(1)}, bf16[4,128,256]{2,1,0:T(8,128)(2,1)}, u32[]{:S(2)}) copy-start(bf16[4,128,256]{2,1,0:T(8,128)(2,1)} %get-tuple-element.17.diag_ref.diag_far_ref) | copy-start | bytes 786436
  22.0 36.3 %all-to-all-start.1 = ((bf16[8,41,16,256]{3,2,1,0:T(8,128)(2,1)}), bf16[8,41,16,256]{3,2,1,0:T(8,128)(2,1)S(1)}, u32[]{:S(2)}, u32[]{:S(2)}) async-start(bf16[8,41,16,256]{3,2,1,0:T(8,128)(2,1)} %get-tuple-element.16), calls=%async_computation.1 | async-start | bytes 5373952 | tf_op jit(solution)/shard_map/all_to_all | solution.py:323
  27.0 11.7 %collective-permute-start = (bf16[1,128,256]{2,1,0:T(8,128)(2,1)S(1)}, bf16[1,128,256]{2,1,0:T(8,128)(2,1)S(1)}, u32[]{:S(2)}, u32[]{:S(2)}) collective-permute-start(bf16[1,128,256]{2,1,0:T(8,128)(2,1)S(1)} %bitcast.11), channel_id=1, source_target_pairs={{0,32},{8,40},{16,48},{24,56},{32,0},{40,8},{48,16},{56,24},{1,33}... | collective-permute-start | bytes 196616 | tf_op jit(solution)/shard_map/ppermute | solution.py:318
  38.7 11.4 %collective-permute-start.1 = (bf16[2,128,256]{2,1,0:T(8,128)(2,1)S(1)}, bf16[2,128,256]{2,1,0:T(8,128)(2,1)S(1)}, u32[]{:S(2)}, u32[]{:S(2)}) collective-permute-start(bf16[2,128,256]{2,1,0:T(8,128)(2,1)S(1)} %shard_map.141.first_ref), channel_id=1, source_target_pairs={{0,16},{8,24},{16,0},{24,8},{32,48},{40,56},{48,32},{56,40},{1,17}... | collective-permute-start | bytes 393224 | tf_op jit(solution)/shard_map/ppermute | solution.py:318
  50.2 8.8 %collective-permute-start.2 = (bf16[4,128,256]{2,1,0:T(8,128)(2,1)S(1)}, bf16[4,128,256]{2,1,0:T(8,128)(2,1)S(1)}, u32[]{:S(2)}, u32[]{:S(2)}) collective-permute-start(bf16[4,128,256]{2,1,0:T(8,128)(2,1)S(1)} %shard_map.142.near_ref), channel_id=1, source_target_pairs={{0,8},{8,0},{16,24},{24,16},{32,40},{40,32},{48,56},{56,48},{1,9},... | collective-permute-start | bytes 786440 | tf_op jit(solution)/shard_map/ppermute | solution.py:318
  62.4 0.8 copy-start
  63.2 22.8 %all-to-all-start.2 = ((bf16[8,144,256]{2,1,0:T(8,128)(2,1)}), bf16[8,144,256]{2,1,0:T(8,128)(2,1)S(1)}, u32[]{:S(2)}, u32[]{:S(2)}) async-start(bf16[8,144,256]{2,1,0:T(8,128)(2,1)} %copy-done), calls=%async_computation.2 | async-start | bytes 1179648 | tf_op jit(solution)/shard_map/all_to_all | solution.py:323
  81.2 0.7 copy-start.3
  81.8 0.7 copy-start.5
  86.0 0.9 copy-start.4
  89.2 41.4 %copy-start.6 = (f32[128,256]{1,0:T(8,128)S(1)}, f32[128,256]{1,0:T(8,128)}, u32[]{:S(2)}) copy-start(f32[128,256]{1,0:T(8,128)} %copy-done.5) | copy-start | bytes 393220
  125.1 18.5 %all-to-all-start.5 = ((bf16[8,8,64,128]{3,2,1,0:T(8,128)(2,1)}), bf16[8,8,64,128]{3,2,1,0:T(8,128)(2,1)S(1)}, u32[]{:S(2)}, u32[]{:S(2)}) async-start(bf16[8,8,64,128]{3,2,1,0:T(8,128)(2,1)} %shard_map.148), calls=%async_computation.5 | async-start | bytes 2097152 | tf_op jit(solution)/shard_map/all_to_all | solution.py:323

commit v6 on v5

--- a/solution.py
+++ b/solution.py
@@ -229,7 +229,7 @@
         rows, lanes = slice(h * 64, h * 64 + 64), slice(h * 128, h * 128 + 128)
         sums_ref[0, rows, :] = key_terms[rows, lanes] * SCALE
         sums_ref[1, rows, :] = value_terms[rows, lanes]
-    own_ref[...] = out_ref[7 - lax.axis_index(ROWS)]
+    own_ref[...] = out_ref[lax.axis_index(ROWS)]
 
 
 def back_terms(
@@ -381,7 +381,7 @@
     )
     near = video_query.reshape(1, 128, 256)
     packed, near = lax.optimization_barrier((packed, near))
-    packed = backwards(packed, ROWS).reshape(8, PACK, 256)
+    packed = lax.all_to_all(packed, ROWS, 0, 0, tiled=True).reshape(8, PACK, 256)
     for distance in (4, 2):
         far = swap(near, "z", distance)
         (near,) = call(

time: 146 us -> 144 us (0.986)
  starting transfers between devices: 51.2 us -> 48.6 us
    all_to_all x0 -> x1, waiting for transfers between devices: none -> 7.86 us  [local(): lax.all_to_all(packed, ROWS, 0, 0, tiled=True).reshape(8, PACK, 256)]
    all_to_all x4 -> x3, waiting for transfers between devices: 22.9 us -> 15.7 us  [backwards(): lax.all_to_all(value, axes, 0, 0, axis_index_groups=[order], tiled=True)]
    all_to_all x4 -> x3, starting transfers between devices: 33.6 us -> 27.7 us  [backwards(): lax.all_to_all(value, axes, 0, 0, axis_index_groups=[order], tiled=True)]
    all_to_all x0 -> x1, starting transfers between devices: none -> 3.77 us  [local(): lax.all_to_all(packed, ROWS, 0, 0, tiled=True).reshape(8, PACK, 256)]
where the time goes in v6:
time: 144 us
  starting transfers between devices  48.6 us (34%)
  blocking collectives  35.8 us (25%)
  waiting for transfers between devices  30.8 us (21%)
  Pallas kernels  23.3 us (16%)
  local copies, waits for them, and re-layouts  3.71 us (3%)
    all_to_all x2, blocking collectives, backwards(): lax.all_to_all(value, axes, 0, 0, axis_index_groups=[order], tiled=True)  35.8 us
    all_to_all x3, starting transfers between devices, backwards(): lax.all_to_all(value, axes, 0, 0, axis_index_groups=[order], tiled=True)  27.7 us
    pallas_call x13, Pallas kernels, call(): pl.pallas_call(kernel, out_shape=[jax.ShapeDtypeStruct(s, d) for s, d in...  23.3 us
    ppermute x3, starting transfers between devices, swap(): return lax.ppermute(value, axis, [(i, i ^ distance) for i in range(count)])  17.1 us
    all_to_all x3, waiting for transfers between devices, backwards(): lax.all_to_all(value, axes, 0, 0, axis_index_groups=[order], tiled=True)  15.7 us
    all_to_all x1, waiting for transfers between devices, local(): lax.all_to_all(packed, ROWS, 0, 0, tiled=True).reshape(8, PACK, 256)  7.86 us
    ppermute x3, waiting for transfers between devices, swap(): return lax.ppermute(value, axis, [(i, i ^ distance) for i in range(count)])  7.26 us
    all_to_all x1, starting transfers between devices, local(): lax.all_to_all(packed, ROWS, 0, 0, tiled=True).reshape(8, PACK, 256)  3.77 us
  transfers between devices with their start and end apart: 7, of which 6 were waited for; matrix products, arithmetic and copies ran while one was open for 0% of the time, Pallas kernels for 8%

profile of v6, /device:TPU:1, one launch (start us, length us, event | category | flops | bytes accessed | tf_op | source)
XLA Modules:
  0.0 143.7 jit_solution(11496105589863373016)
XLA Ops:
  0.6 1.7 %shard_map.137 = bf16[8,32,256]{2,1,0:T(8,128)(2,1)} custom-call(bf16[64,2048]{1,0:T(8,128)(2,1)} %rest_0_.1, bf16[64,2048]{1,0:T(8,128)(2,1)} %rest_1_.1, bf16[64,2048]{1,0:T(8,128)(2,1)} %rest_2_.1, bf16[64,2048]{1,0:T(8,128)(2,1)} %rest_3_.1), custom_call_target="tpu_custom_call" | custom-call | flops 1000000 | bytes 4000000 | tf_op jit(solution)/shard_map/pallas_call | solution.py:42
  2.3 11.6 %all-to-all-start = ((bf16[8,32,256]{2,1,0:T(8,128)(2,1)}), bf16[8,32,256]{2,1,0:T(8,128)(2,1)S(1)}, u32[]{:S(2)}, u32[]{:S(2)}) async-start(bf16[8,32,256]{2,1,0:T(8,128)(2,1)} %shard_map.137), calls=%async_computation | async-start | bytes 262144 | tf_op jit(solution)/shard_map/all_to_all | solution.py:323
  14.6 3.1 %shard_map.138.given_ref = bf16[8,41,16,256]{3,2,1,0:T(8,128)(2,1)} custom-call(s32[1,3]{1,0:T(1,128)} %list_ref.1, s32[1]{0:T(128)S(6)} %copy.17.count_ref, bf16[8,16,256]{2,1,0:T(8,128)(2,1)} %bitcast.10, bf16[8,16,256]{2,1,0:T(8,128)(2,1)} %bitcast.13, bf16[8,16,256]{2,1,0:T(8,128)(2,1)} %bitcast.14, bf16[8,16,256]{2,1,0:T(8,128)(2,1)} %bitcast.15), custom_call_target="tpu_custom_call" | custom-call | flops 1000000 | bytes 4000000 | tf_op jit(solution)/shard_map/pallas_call | solution.py:42
  17.6 1.1 all-to-all-done.audio_ref
  18.8 0.7 copy-done.7
  19.4 2.5 %shard_map.139 = (bf16[4,128,256]{2,1,0:T(8,128)(2,1)}, bf16[8,41,16,256]{3,2,1,0:T(8,128)(2,1)}) custom-call(bf16[8,32,256]{2,1,0:T(8,128)(2,1)} %copy-done.7, bf16[8,41,16,256]{3,2,1,0:T(8,128)(2,1)} %shard_map.138.given_ref), custom_call_target="tpu_custom_call", output_to_operand_aliasing={{1}: (1, {})} | custom-call | flops 1000000 | bytes 4000000 | tf_op jit(solution)/shard_map/pallas_call | solution.py:42
  22.0 0.0 copy-start.1
  22.0 0.0 copy-start.2
  22.0 3.8 %all-to-all-start.1 = ((bf16[8,41,16,256]{3,2,1,0:T(8,128)(2,1)}), bf16[8,41,16,256]{3,2,1,0:T(8,128)(2,1)S(1)}, u32[]{:S(2)}, u32[]{:S(2)}) async-start(bf16[8,41,16,256]{3,2,1,0:T(8,128)(2,1)} %get-tuple-element.16), calls=%async_computation.1 | async-start | bytes 5373952 | tf_op jit(solution)/shard_map/all_to_all | solution.py:384
  25.8 9.3 %collective-permute-start = (bf16[1,128,256]{2,1,0:T(8,128)(2,1)S(1)}, bf16[1,128,256]{2,1,0:T(8,128)(2,1)S(1)}, u32[]{:S(2)}, u32[]{:S(2)}) collective-permute-start(bf16[1,128,256]{2,1,0:T(8,128)(2,1)S(1)} %bitcast.11), channel_id=1, source_target_pairs={{0,32},{8,40},{16,48},{24,56},{32,0},{40,8},{48,16},{56,24},{1,33}... | collective-permute-start | bytes 196616 | tf_op jit(solution)/shard_map/ppermute | solution.py:318
  35.1 1.7 %collective-permute-done.second_ref = bf16[1,128,256]{2,1,0:T(8,128)(2,1)S(1)} collective-permute-done((bf16[1,128,256]{2,1,0:T(8,128)(2,1)S(1)}, bf16[1,128,256]{2,1,0:T(8,128)(2,1)S(1)}, u32[]{:S(2)}, u32[]{:S(2)}) %collective-permute-start) | collective-permute-done | bytes 65568 | tf_op jit(solution)/shard_map/ppermute | solution.py:318
  36.8 5.9 %collective-permute-start.1 = (bf16[2,128,256]{2,1,0:T(8,128)(2,1)S(1)}, bf16[2,128,256]{2,1,0:T(8,128)(2,1)S(1)}, u32[]{:S(2)}, u32[]{:S(2)}) collective-permute-start(bf16[2,128,256]{2,1,0:T(8,128)(2,1)S(1)} %shard_map.141.first_ref), channel_id=1, source_target_pairs={{0,16},{8,24},{16,0},{24,8},{32,48},{40,56},{48,32},{56,40},{1,17}... | collective-permute-start | bytes 393224 | tf_op jit(solution)/shard_map/ppermute | solution.py:318
  42.7 5.5 %collective-permute-done.1.second_ref = bf16[2,128,256]{2,1,0:T(8,128)(2,1)S(1)} collective-permute-done((bf16[2,128,256]{2,1,0:T(8,128)(2,1)S(1)}, bf16[2,128,256]{2,1,0:T(8,128)(2,1)S(1)}, u32[]{:S(2)}, u32[]{:S(2)}) %collective-permute-start.1) | collective-permute-done | bytes 131104 | tf_op jit(solution)/shard_map/ppermute | solution.py:318
  48.3 1.9 %collective-permute-start.2 = (bf16[4,128,256]{2,1,0:T(8,128)(2,1)S(1)}, bf16[4,128,256]{2,1,0:T(8,128)(2,1)S(1)}, u32[]{:S(2)}, u32[]{:S(2)}) collective-permute-start(bf16[4,128,256]{2,1,0:T(8,128)(2,1)S(1)} %shard_map.142.near_ref), channel_id=1, source_target_pairs={{0,8},{8,0},{16,24},{24,16},{32,40},{40,32},{48,56},{56,48},{1,9},... | collective-permute-start | bytes 786440 | tf_op jit(solution)/shard_map/ppermute | solution.py:318
  50.2 7.9 %all-to-all-done.1 = bf16[8,41,16,256]{3,2,1,0:T(8,128)(2,1)S(1)} async-done(((bf16[8,41,16,256]{3,2,1,0:T(8,128)(2,1)}), bf16[8,41,16,256]{3,2,1,0:T(8,128)(2,1)S(1)}, u32[]{:S(2)}, u32[]{:S(2)}) %all-to-all-start.1) | async-done | bytes 2687008 | tf_op jit(solution)/shard_map/all_to_all | solution.py:384
  58.1 0.6 shard_map.143.stats_ref
  58.7 3.4 %shard_map.144 = bf16[8,144,256]{2,1,0:T(8,128)(2,1)S(1)} custom-call(bf16[4,128,256]{2,1,0:T(8,128)(2,1)S(1)} %shard_map.142.near_ref, bf16[4,128,256]{2,1,0:T(8,128)(2,1)S(1)} %collective-permute-done.2.far_ref, bf16[8,656,256]{2,1,0:T(8,128)(2,1)S(1)} %bitcast.7, f32[13,256]{1,0:T(8,128)S(1)} %shard_map.143.stats_ref), custom_call_target="tpu_custom_call" | custom-call | flops 4000000000 | bytes 4000000 | tf_op jit(solution)/shard_map/pallas_call | solution.py:42
  62.2 0.8 copy-done
  63.0 11.0 %all-to-all-start.2 = ((bf16[8,144,256]{2,1,0:T(8,128)(2,1)}), bf16[8,144,256]{2,1,0:T(8,128)(2,1)S(1)}, u32[]{:S(2)}, u32[]{:S(2)}) async-start(bf16[8,144,256]{2,1,0:T(8,128)(2,1)} %copy-done), calls=%async_computation.2 | async-start | bytes 1179648 | tf_op jit(solution)/shard_map/all_to_all | solution.py:323
  74.0 6.4 %shard_map.140 = (f32[128,256]{1,0:T(8,128)S(1)}, f32[2,128,128]{2,1,0:T(8,128)S(1)}) custom-call(bf16[8,656,256]{2,1,0:T(8,128)(2,1)S(1)} %bitcast.8, bf16[4,128,256]{2,1,0:T(8,128)(2,1)S(1)} %copy-done.2), custom_call_target="tpu_custom_call" | custom-call | flops 4000000000 | bytes 4000000 | tf_op jit(solution)/shard_map/pallas_call | solution.py:42
  80.4 0.6 copy-done.3
  81.1 0.7 copy-done.5
  81.7 2.9 %all-to-all-done.2.sent_ref = bf16[8,144,256]{2,1,0:T(8,128)(2,1)S(1)} async-done(((bf16[8,144,256]{2,1,0:T(8,128)(2,1)}), bf16[8,144,256]{2,1,0:T(8,128)(2,1)S(1)}, u32[]{:S(2)}, u32[]{:S(2)}) %all-to-all-start.2) | async-done | bytes 589856 | tf_op jit(solution)/shard_map/all_to_all | solution.py:323
  84.6 0.9 copy-done.4
  85.5 2.3 %shard_map.146 = f32[64,8,128]{2,1,0:T(8,128)S(1)} custom-call(bf16[8,144,256]{2,1,0:T(8,128)(2,1)S(1)} %all-to-all-done.2.sent_ref, bf16[8,656,256]{2,1,0:T(8,128)(2,1)S(1)} %bitcast.9, bf16[4,128,256]{2,1,0:T(8,128)(2,1)S(1)} %copy-done.2, f32[2,128,128]{2,1,0:T(8,128)S(1)} %copy-done.4), custom_call_target="tpu_custom_call" | custom-call | flops 1000000000 | bytes 4000000 | tf_op jit(solution)/shard_map/pallas_call | solution.py:42
  87.9 25.6 %all_to_all.30.terms_ref = f32[64,8,128]{2,1,0:T(8,128)S(1)} all-to-all(f32[64,8,128]{2,1,0:T(8,128)S(1)} %shard_map.146), channel_id=1, replica_groups={{63,55,47,39,31,23,15,7,62,54,46,38,30,22,14,6,61,53,45,37,29,21,13,5,6..., dimensions={0} | all-to-all | bytes 524288 | tf_op jit(solution)/shard_map/all_to_all | solution.py:323
  113.5 10.2 %all_to_all.31.ref = bf16[8,64,128]{2,1,0:T(8,128)(2,1)S(1)} all-to-all(bf16[8,64,128]{2,1,0:T(8,128)(2,1)S(1)} %shard_map.147), channel_id=1, replica_groups={{56,48,40,32,24,16,8,0},{57,49,41,33,25,17,9,1},{58,50,42,34,26,18,10,2..., dimensions={0} | all-to-all | bytes 262144 | tf_op jit(solution)/shard_map/all_to_all | solution.py:323
  123.7 1.1 shard_map.148
  124.8 5.0 %all-to-all-start.5 = ((bf16[8,8,64,128]{3,2,1,0:T(8,128)(2,1)}), bf16[8,8,64,128]{3,2,1,0:T(8,128)(2,1)S(1)}, u32[]{:S(2)}, u32[]{:S(2)}) async-start(bf16[8,8,64,128]{3,2,1,0:T(8,128)(2,1)} %shard_map.148), calls=%async_computation.5 | async-start | bytes 2097152 | tf_op jit(solution)/shard_map/all_to_all | solution.py:323
  129.9 1.0 shard_map.145
  130.9 11.7 %all-to-all-done.5.final_ref = bf16[8,8,64,128]{3,2,1,0:T(8,128)(2,1)S(1)} async-done(((bf16[8,8,64,128]{3,2,1,0:T(8,128)(2,1)}), bf16[8,8,64,128]{3,2,1,0:T(8,128)(2,1)S(1)}, u32[]{:S(2)}, u32[]{:S(2)}) %all-to-all-start.5) | async-done | bytes 1048608 | tf_op jit(solution)/shard_map/all_to_all | solution.py:323
  142.5 1.1 shard_map.149
  (13 shorter events, 0.1 us)
Async XLA Ops:
  2.3 16.5 %all-to-all-start = ((bf16[8,32,256]{2,1,0:T(8,128)(2,1)}), bf16[8,32,256]{2,1,0:T(8,128)(2,1)S(1)}, u32[]{:S(2)}, u32[]{:S(2)}) async-start(bf16[8,32,256]{2,1,0:T(8,128)(2,1)} %shard_map.137), calls=%async_computation | async-start | bytes 262144 | tf_op jit(solution)/shard_map/all_to_all | solution.py:323
  18.8 0.7 copy-start.7
  22.0 3.8 %copy-start.1 = (bf16[128,256]{1,0:T(8,128)(2,1)S(1)}, bf16[128,256]{1,0:T(8,128)(2,1)}, u32[]{:S(2)}) copy-start(bf16[128,256]{1,0:T(8,128)(2,1)} %param.10) | copy-start | bytes 196612
  22.0 36.1 %copy-start.2 = (bf16[4,128,256]{2,1,0:T(8,128)(2,1)S(1)}, bf16[4,128,256]{2,1,0:T(8,128)(2,1)}, u32[]{:S(2)}) copy-start(bf16[4,128,256]{2,1,0:T(8,128)(2,1)} %get-tuple-element.17.diag_ref.diag_far_ref) | copy-start | bytes 786436
  22.0 36.1 %all-to-all-start.1 = ((bf16[8,41,16,256]{3,2,1,0:T(8,128)(2,1)}), bf16[8,41,16,256]{3,2,1,0:T(8,128)(2,1)S(1)}, u32[]{:S(2)}, u32[]{:S(2)}) async-start(bf16[8,41,16,256]{3,2,1,0:T(8,128)(2,1)} %get-tuple-element.16), calls=%async_computation.1 | async-start | bytes 5373952 | tf_op jit(solution)/shard_map/all_to_all | solution.py:384
  25.8 11.1 %collective-permute-start = (bf16[1,128,256]{2,1,0:T(8,128)(2,1)S(1)}, bf16[1,128,256]{2,1,0:T(8,128)(2,1)S(1)}, u32[]{:S(2)}, u32[]{:S(2)}) collective-permute-start(bf16[1,128,256]{2,1,0:T(8,128)(2,1)S(1)} %bitcast.11), channel_id=1, source_target_pairs={{0,32},{8,40},{16,48},{24,56},{32,0},{40,8},{48,16},{56,24},{1,33}... | collective-permute-start | bytes 196616 | tf_op jit(solution)/shard_map/ppermute | solution.py:318
  36.8 11.4 %collective-permute-start.1 = (bf16[2,128,256]{2,1,0:T(8,128)(2,1)S(1)}, bf16[2,128,256]{2,1,0:T(8,128)(2,1)S(1)}, u32[]{:S(2)}, u32[]{:S(2)}) collective-permute-start(bf16[2,128,256]{2,1,0:T(8,128)(2,1)S(1)} %shard_map.141.first_ref), channel_id=1, source_target_pairs={{0,16},{8,24},{16,0},{24,8},{32,48},{40,56},{48,32},{56,40},{1,17}... | collective-permute-start | bytes 393224 | tf_op jit(solution)/shard_map/ppermute | solution.py:318
  48.3 10.4 %collective-permute-start.2 = (bf16[4,128,256]{2,1,0:T(8,128)(2,1)S(1)}, bf16[4,128,256]{2,1,0:T(8,128)(2,1)S(1)}, u32[]{:S(2)}, u32[]{:S(2)}) collective-permute-start(bf16[4,128,256]{2,1,0:T(8,128)(2,1)S(1)} %shard_map.142.near_ref), channel_id=1, source_target_pairs={{0,8},{8,0},{16,24},{24,16},{32,40},{40,32},{48,56},{56,48},{1,9},... | collective-permute-start | bytes 786440 | tf_op jit(solution)/shard_map/ppermute | solution.py:318
  62.2 0.8 copy-start
  63.0 21.6 %all-to-all-start.2 = ((bf16[8,144,256]{2,1,0:T(8,128)(2,1)}), bf16[8,144,256]{2,1,0:T(8,128)(2,1)S(1)}, u32[]{:S(2)}, u32[]{:S(2)}) async-start(bf16[8,144,256]{2,1,0:T(8,128)(2,1)} %copy-done), calls=%async_computation.2 | async-start | bytes 1179648 | tf_op jit(solution)/shard_map/all_to_all | solution.py:323
  80.4 0.7 copy-start.3
  81.0 0.7 copy-start.5
  84.6 0.9 copy-start.4
  87.8 42.0 %copy-start.6 = (f32[128,256]{1,0:T(8,128)S(1)}, f32[128,256]{1,0:T(8,128)}, u32[]{:S(2)}) copy-start(f32[128,256]{1,0:T(8,128)} %copy-done.5) | copy-start | bytes 393220
  124.8 17.7 %all-to-all-start.5 = ((bf16[8,8,64,128]{3,2,1,0:T(8,128)(2,1)}), bf16[8,8,64,128]{3,2,1,0:T(8,128)(2,1)S(1)}, u32[]{:S(2)}, u32[]{:S(2)}) async-start(bf16[8,8,64,128]{3,2,1,0:T(8,128)(2,1)} %shard_map.148), calls=%async_computation.5 | async-start | bytes 2097152 | tf_op jit(solution)/shard_map/all_to_all | solution.py:323
